TPU v7x, 256 devices: a whole 4x4x8 slice. The times are simulated.
256 devices in a mesh: slab: 64 (over z, x, core), ang: 4 (over y).
Axes of the slice: x: 4, y: 4, z: 8, core: 2. Of those that a mesh axis runs over, the one named last changes fastest.
Arguments:
- projections: float32 [8, 64, 16, 4096], P('ang', 'slab'), may hold values from -6 to 6
- weights: bfloat16 [8, 32, 3, 128, 128], P('ang'), may hold values from -0.3125 to 0.3125
- columns: int32 [8, 32, 3], P('ang'), may hold values from 0 to 31, as said below
- row_weights: float32 [8, 64, 3, 1, 4], P('ang', 'slab'), may hold values from -3 to 3
- reach: int32 [8, 64, 2], P('ang', 'slab'), may hold values from -1 to 1, as said below
Outputs:
- volume: float32 [256, 16, 4096], P('slab')
- residual: float32 [8, 64, 16, 4096], P('ang', 'slab')
- gradient: float32 [256, 16, 4096], P('slab')
Inputs may be any that keep to these rules, and one draw needn't show every extreme that they name: `columns`: each footprint names 3 consecutive blocks; the first detector column block starts at block 0 and the last ends at block 31 at every angle. `reach`: the first entry is -1 or 0 and the second 0 or 1; the first slab never reaches below, the last never above; at every angle slab 1 reaches the band below, slab 64 - 2 reaches the band above, and the two middle slabs reach both neighbours' bands; other slabs far from the centre reach their neighbours' bands more often.
All inputs are finite; a program needn't handle non-finite values.
Results may differ from a plain program's by a relative error of at most 0.0095.
Values may be sent and summed in bfloat16 or wider, within the bound.
No kernel may reach another device: no remote copies, remote signals or barrier semaphores. Data moves between devices by JAX's collectives and lax.ppermute only.
A program may use at most 128 MiB of HBM per device.

v0:
```python
import functools

import jax
import jax.numpy as jnp
from jax import lax
from jax.experimental import pallas as pl
from jax.experimental.pallas import tpu as pltpu
from jax.sharding import PartitionSpec as P

F32 = jnp.float32
BF16 = jnp.bfloat16
ANG = 4
PAIR = 2
L = 16
X = 4096
Q = X // ANG
UB = 32
ZD = 4
CH = 128
COEF = 3 * 128
GROUP = 8
VMEM = pl.BlockSpec(memory_space=pltpu.VMEM)
SMEM = pl.BlockSpec(memory_space=pltpu.SMEM)
HBM = pl.BlockSpec(memory_space=pltpu.HBM)
MID = BF16
LIMIT = 48 * 1024 * 1024


def call(kernel, outs, specs, scratch=(), flops=0, nbytes=2_000_000):
    return pl.pallas_call(
        kernel,
        out_shape=outs,
        in_specs=specs,
        out_specs=[VMEM] * len(outs),
        scratch_shapes=list(scratch),
        compiler_params=pltpu.CompilerParams(vmem_limit_bytes=LIMIT),
        cost_estimate=pl.CostEstimate(flops=flops, bytes_accessed=nbytes, transcendentals=0),
    )


def sds(shape, dtype):
    return jax.ShapeDtypeStruct(shape, dtype)


def halves(value):
    high = value.astype(BF16)
    low = (value - high.astype(F32)).astype(BF16)
    return jnp.concatenate([high, low], axis=0)


def fold(value):
    total = value[:8] + value[8:]
    out = total[:, :128]
    for at in range(1, total.shape[1] // 128):
        out = out + total[:, 128 * at:128 * (at + 1)]
    return out


def weight_copies(w_hbm, w_buf, sem):
    return [
        pltpu.make_async_copy(
            w_hbm.at[a, pl.ds(GROUP * g, GROUP)], w_buf.at[a, pl.ds(GROUP * g, GROUP)],
            sem.at[a, g],
        )
        for a in range(PAIR)
        for g in range(UB // GROUP)
    ]


def window(cols, a, block):
    return pl.ds(pl.multiple_of(cols[a, block, 0] * 128, 128), 384)


def back_block(a, block, value, cols, w_buf, acc):
    both = halves(value)
    spread = lax.dot_general(
        both, w_buf[a, block], (((1,), (1,)), ((), ())), preferred_element_type=F32
    )
    at = window(cols, a, block)
    acc[a, :, at] += spread[:L] + spread[L:]


def send_shares(me, acc, outs):
    for r in range(ANG):
        quarter = lax.rem(me + r, ANG)
        share = acc[:, :, pl.ds(pl.multiple_of(quarter * Q, Q), Q)]
        outs[r][:, :, :Q] = share.astype(outs[r].dtype)


def back_kernel(me_ref, cols, stencil, p_ref, w_hbm, o0, o1, o2, o3, w_buf, acc, sem):
    copies = weight_copies(w_hbm, w_buf, sem)
    for copy in copies:
        copy.start()
    acc[...] = jnp.zeros_like(acc)
    for a in range(PAIR):
        for g in range(UB // GROUP):
            copies[a * (UB // GROUP) + g].wait()
            for i in range(GROUP):
                block = g * GROUP + i
                back_block(a, block, p_ref[a, :, 128 * block:128 * (block + 1)], cols, w_buf, acc)
    outs = (o0, o1, o2, o3)
    send_shares(me_ref[0], acc, outs)
    at_row = lax.broadcasted_iota(jnp.int32, (L, 128), 0)
    for i in range(PAIR):
        rest = jnp.zeros((L, 128), F32)
        for e in range(12):
            rest = jnp.where(at_row == e, stencil[12 * i + e], rest)
        for part in range(3):
            piece = rest.astype(BF16)
            rest = rest - piece.astype(F32)
            for out in outs:
                out[i, :, Q + 128 * part:Q + 128 * (part + 1)] = piece


def both_body(cols, copies, w_buf, acc, lhs, store):
    acc[...] = jnp.zeros_like(acc)
    for a in range(PAIR):
        for g in range(UB // GROUP):
            copies[a * (UB // GROUP) + g].wait()
            images = []
            for i in range(GROUP):
                block = g * GROUP + i
                image = jnp.dot(lhs(a, window(cols, a, block)), w_buf[a, block], preferred_element_type=F32)
                if image.shape[0] > L:
                    image = image[:L] + image[L:]
                store(a, block, image)
                images.append(image)
            for i in range(GROUP):
                back_block(a, g * GROUP + i, images[i], cols, w_buf, acc)


def gather_shares(me, shares, place):
    for r in range(ANG):
        quarter = lax.rem(me + ANG - r, ANG)
        place(pl.ds(pl.multiple_of(quarter * Q, Q), Q), shares[r])


def first_kernel(me_ref, cols, h0, h1, h2, h3, w_hbm, o0, o1, o2, o3, q_out, dots, hb, w_buf, acc, sem):
    copies = weight_copies(w_hbm, w_buf, sem)
    for copy in copies:
        copy.start()

    def place(at, share):
        hb[:, :, at] = share[...]

    def store(a, block, image):
        q_out[a, :, 128 * block:128 * (block + 1)] = image

    gather_shares(me_ref[0], (h0, h1, h2, h3), place)
    both_body(cols, copies, w_buf, acc, lambda a, at: hb[a, :, at], store)
    send_shares(me_ref[0], acc, (o0, o1, o2, o3))
    dots[...] = fold(q_out[0] * q_out[0]) + fold(q_out[1] * q_out[1])


def second_kernel(me_ref, cols, h0, h1, h2, h3, q0_ref, gamma_ref, curve_ref, inner_ref, w_hbm,
                  o0, o1, o2, o3, w_out, sums, both, w_buf, acc, sem):
    copies = weight_copies(w_hbm, w_buf, sem)
    for copy in copies:
        copy.start()

    def place(at, share):
        for a in range(PAIR):
            both[a, :, at] = halves(share[a].astype(F32))

    def store(a, block, image):
        w_out[a, :, 128 * block:128 * (block + 1)] = image

    gather_shares(me_ref[0], (h0, h1, h2, h3), place)
    both_body(cols, copies, w_buf, acc, lambda a, at: both[a, :, at], store)
    send_shares(me_ref[0], acc, (o0, o1, o2, o3))
    cross = fold(w_out[0] * q0_ref[0]) + fold(w_out[1] * q0_ref[1])
    own = fold(w_out[0] * w_out[0]) + fold(w_out[1] * w_out[1])
    lane = lax.broadcasted_iota(jnp.int32, (1, 128), 1)
    row = jnp.zeros((1, 128), F32)
    for at, value in enumerate((gamma_ref[...], curve_ref[...], inner_ref[:8], inner_ref[8:], cross, own)):
        row = jnp.where(lane == at, jnp.sum(value), row)
    sums[...] = row


def spread_slices(coefs, parts, cut):
    totals = [None] * 12
    for r in range(ANG):
        for i in range(PAIR):
            value = parts[r][i, :, cut].astype(F32)
            for e in range(12):
                term = coefs[r, i, e:e + 1, :] * value
                totals[e] = term if totals[e] is None else totals[e] + term
    return totals


def cuts():
    return [pl.ds(at * CH, CH) for at in range(Q // CH)]


def combine_parts(coefs, parts, t1, up, down, up_far, down_far):
    for cut in cuts():
        totals = spread_slices(coefs, parts, cut)
        for z in range(ZD):
            below, own, above = totals[z], totals[4 + z], totals[8 + z]
            t1[z, :, cut] = own
            up[z, :, cut] = own.astype(BF16)
            down[z, :, cut] = own.astype(BF16)
            up[4 + z, :, cut] = above.astype(BF16)
            down[4 + z, :, cut] = below.astype(BF16)
            up_far[z, :, cut] = above.astype(BF16)
            down_far[z, :, cut] = below.astype(BF16)


def open_kernel(c0, c1, c2, c3, t1, up, down, up_far, down_far, coefs):
    parts = (c0, c1, c2, c3)
    for r in range(ANG):
        for i in range(PAIR):
            value = parts[r][i, :, Q:Q + 128].astype(F32)
            value = value + parts[r][i, :, Q + 128:Q + 256].astype(F32)
            coefs[r, i] = value + parts[r][i, :, Q + 256:].astype(F32)
    combine_parts(coefs, parts, t1, up, down, up_far, down_far)


def combine_kernel(coefs, c0, c1, c2, c3, t1, up, down, up_far, down_far):
    combine_parts(coefs, (c0, c1, c2, c3), t1, up, down, up_far, down_far)


def pieces_body(coefs, t1, up, down, from_low, from_high, far_low, far_high, g_out, outs, note):
    for cut in cuts():
        def get(ref, z):
            return ref[z, :, cut].astype(F32)

        cells = []
        for z in range(ZD):
            cells.append(get(from_low, z) + get(far_low, z) + get(down, 4 + z))
        for z in range(ZD):
            value = t1[z, :, cut] + get(from_low, 4 + z) + get(from_high, 4 + z)
            g_out[z, :, cut] = value
            note(z, cut, value)
            cells.append(value)
        for z in range(ZD):
            cells.append(get(from_high, z) + get(far_high, z) + get(up, 4 + z))
        for r in range(ANG):
            for i in range(PAIR):
                total = None
                for e in range(12):
                    term = coefs[(ANG - r) % ANG, i, e:e + 1, :] * cells[e]
                    total = term if total is None else total + term
                outs[r][i, :, cut] = total.astype(outs[r].dtype)


def pieces_first(coefs, t1, up, down, from_low, from_high, far_low, far_high,
                 g_out, h0, h1, h2, h3, dots):
    kept = [jnp.zeros((8, 128), F32)]

    def note(z, cut, value):
        kept[0] = kept[0] + fold(value * value)

    pieces_body(coefs, t1, up, down, from_low, from_high, far_low, far_high, g_out, (h0, h1, h2, h3), note)
    dots[...] = kept[0]


def pieces_second(coefs, g0, t1, up, down, from_low, from_high, far_low, far_high,
                  g_out, h0, h1, h2, h3, dots):
    kept = [jnp.zeros((8, 128), F32)] * 2

    def note(z, cut, value):
        kept[0] = kept[0] + fold(value * g0[z, :, cut])
        kept[1] = kept[1] + fold(value * value)

    pieces_body(coefs, t1, up, down, from_low, from_high, far_low, far_high, g_out, (h0, h1, h2, h3), note)
    dots[:8] = kept[0]
    dots[8:] = kept[1]


def last_kernel(coefs, c0, c1, c2, c3, t1, up, down):
    for cut in cuts():
        totals = spread_slices(coefs, (c0, c1, c2, c3), cut)
        for z in range(ZD):
            down[z, :, cut] = totals[z].astype(down.dtype)
            t1[z, :, cut] = totals[4 + z]
            up[z, :, cut] = totals[8 + z].astype(up.dtype)


def steps(sums_ref):
    total = sums_ref[0]
    for at in range(1, sums_ref.shape[0]):
        total = total + sums_ref[at]
    lane = lax.broadcasted_iota(jnp.int32, (1, 128), 1)
    gamma0, curve0, inner, norm, cross, own = [
        jnp.sum(jnp.where(lane == at, total, 0.0)) for at in range(6)
    ]
    step0 = gamma0 / curve0
    gamma1 = gamma0 - 2.0 * step0 * inner + step0 * step0 * norm
    ratio = gamma1 / gamma0
    curve1 = (1.0 + ratio) * (1.0 + ratio) * curve0 - 2.0 * (1.0 + ratio) * step0 * cross + step0 * step0 * own
    step1 = gamma1 / curve1
    return step0 + step1 * (1.0 + ratio), step0 * step1


def volume_kernel(sums, g0, z0, out):
    one, two = steps(sums)
    for z in range(ZD):
        out[z] = (one * g0[z] - two * z0[z]).astype(BF16)


def gradient_kernel(sums, t1, from_low, from_high, g0, z0, out):
    one, two = steps(sums)
    for z in range(ZD):
        last = t1[z] + from_low[z].astype(F32) + from_high[z].astype(F32)
        out[z] = (g0[z] - one * z0[z] + two * last).astype(BF16)


def residual_kernel(sums, p, q0, w0, out):
    one, two = steps(sums)
    for a in range(PAIR):
        out[a] = p[a] - one * q0[a] + two * w0[a]


def place_kernel(me_ref, s0, s1, s2, s3, out):
    def place(at, share):
        out[:, :, at] = share[...].astype(F32)

    gather_shares(me_ref[0], (s0, s1, s2, s3), place)


def along_ang(value, steps):
    return lax.ppermute(value, "ang", [(i, (i + steps) % ANG) for i in range(ANG)])


def along_slab(value, steps):
    count = lax.axis_size("slab")
    pairs = [(i, i + steps) for i in range(count) if 0 <= i + steps < count]
    return lax.ppermute(value, "slab", pairs)


def exchange(shares):
    far = along_ang(shares[2], 2)
    near = along_ang(shares[1], 1)
    back = along_ang(shares[3], 3)
    return (shares[0], near, far, back)


def per_device(projections, weights, columns, row_weights, reach):
    rows = row_weights[:, 0, :, 0, :]
    below = rows[:, 0] * (reach[:, 0, :1] == -1).astype(F32)
    above = rows[:, 2] * (reach[:, 0, 1:] == 1).astype(F32)
    stencil = jnp.stack([along_slab(above, 1), rows[:, 1], along_slab(below, -1)], axis=1).reshape(PAIR * 12)

    me = lax.axis_index("ang").astype(jnp.int32).reshape(1)
    w = weights.reshape(PAIR, UB, 384, 128)
    p = projections.reshape(PAIR, L, X)

    def share(dtype, more=0):
        return sds((PAIR, L, Q + more), dtype)

    full = sds((PAIR, L, X), F32)
    part = sds((ZD, L, Q), F32)
    part_b = sds((ZD, L, Q), BF16)
    two_b = sds((2 * ZD, L, Q), BF16)
    w_scratch = [
        pltpu.VMEM((PAIR, UB, 384, 128), BF16),
        pltpu.VMEM((PAIR, L, X), F32),
        pltpu.SemaphoreType.DMA((PAIR, UB // GROUP)),
    ]
    macs = 2 * PAIR * L * UB * 384 * 128
    sent = [part, two_b, two_b, part_b, part_b]

    def halo(t1, up, down, up_far, down_far):
        return (t1, up, down, along_slab(up, 1), along_slab(down, -1),
                along_slab(up_far, 2), along_slab(down_far, -2))

    shares = call(
        back_kernel, [share(BF16, COEF)] * 4, [SMEM] * 3 + [VMEM, HBM], w_scratch, flops=2 * macs, nbytes=7_000_000
    )(me, columns, stencil, p, w)
    *spread, coefs = call(
        open_kernel, sent + [sds((ANG, PAIR, L, 128), F32)], [VMEM] * 4, flops=10_000_000
    )(*exchange(shares))
    g0, *shares, gamma = call(
        pieces_first, [part] + [share(BF16)] * 4 + [sds((8, 128), F32)], [VMEM] * 8, flops=10_000_000
    )(coefs, *halo(*spread))

    *shares, q0, curve = call(
        first_kernel, [share(MID)] * 4 + [full, sds((8, 128), F32)],
        [SMEM] * 2 + [VMEM] * 4 + [HBM], [pltpu.VMEM((PAIR, L, X), BF16)] + w_scratch,
        flops=3 * macs, nbytes=7_000_000,
    )(me, columns, *exchange(shares), w)
    spread = call(combine_kernel, sent, [VMEM] * 5, flops=10_000_000)(coefs, *exchange(shares))
    z0, *shares, inner = call(
        pieces_second, [part] + [share(F32)] * 4 + [sds((16, 128), F32)], [VMEM] * 9, flops=10_000_000
    )(coefs, g0, *halo(*spread))

    *shares, w0, sums = call(
        second_kernel, [share(F32)] * 4 + [full, sds((1, 128), F32)],
        [SMEM] * 2 + [VMEM] * 8 + [HBM], [pltpu.VMEM((PAIR, 2 * L, X), BF16)] + w_scratch,
        flops=4 * macs, nbytes=9_000_000,
    )(me, columns, *exchange(shares), q0, gamma, curve, inner, w)
    shares = exchange(shares)
    count = lax.axis_size("slab") * ANG
    sums = lax.all_to_all(jnp.broadcast_to(sums[None], (count, 1, 128)), ("slab", "ang"), 0, 0, tiled=True)
    (volume,) = call(volume_kernel, [part_b], [VMEM] * 3)(sums, g0, z0)
    (residual,) = call(residual_kernel, [full], [VMEM] * 4)(sums, p, q0, w0)
    volume = exchange((volume,) * 4)
    t1, up, down = call(last_kernel, [part] * 3, [VMEM] * 5, flops=10_000_000)(coefs, *shares)
    (gradient,) = call(gradient_kernel, [part_b], [VMEM] * 6)(
        sums, t1, along_slab(up, 1), along_slab(down, -1), g0, z0
    )
    whole = [sds((ZD, L, X), F32)]
    (volume,) = call(place_kernel, whole, [SMEM] + [VMEM] * 4)(me, *volume)
    (gradient,) = call(place_kernel, whole, [SMEM] + [VMEM] * 4)(me, *exchange((gradient,) * 4))
    return volume, residual.reshape(projections.shape), gradient


def solution(mesh):
    in_specs = (
        P("ang", "slab", None, None),
        P("ang", None, None, None, None),
        P("ang", None, None),
        P("ang", "slab", None, None, None),
        P("ang", "slab", None),
    )
    out_specs = (P("slab", None, None), P("ang", "slab", None, None), P("slab", None, None))
    return jax.shard_map(
        per_device, mesh=mesh, in_specs=in_specs, out_specs=out_specs, check_vma=False
    )
```

profile of v0, /device:TPU:1, one launch (start us, length us, event | category | flops | bytes accessed | tf_op | source)
XLA Modules:
  0.0 160.5 jit_solution(3087157577168999159)
XLA Ops:
  2.3 4.5 %collective-permute-start = (f32[2,4]{1,0:T(2,128)S(1)}, f32[2,4]{1,0:T(2,128)S(1)}, u32[]{:S(2)}, u32[]{:S(2)}) collective-permute-start(f32[2,4]{1,0:T(2,128)S(1)} %get-tuple-element.95), channel_id=1, source_target_pairs={{0,4},{4,8},{8,12},{12,16},{16,20},{20,24},{24,28},{28,32},{32,36}... | collective-permute-start | bytes 104 | tf_op jit(solution)/shard_map/ppermute | solution.py:329
  9.6 2.2 %collective-permute-done.1 = f32[2,4]{1,0:T(2,128)S(1)} collective-permute-done((f32[2,4]{1,0:T(2,128)S(1)}, f32[2,4]{1,0:T(2,128)S(1)}, u32[]{:S(2)}, u32[]{:S(2)}) %collective-permute-start.1) | collective-permute-done | bytes 64 | tf_op jit(solution)/shard_map/ppermute | solution.py:329
  12.9 5.5 %shard_map.76 = (bf16[2,16,1408]{2,1,0:T(8,128)(2,1)S(1)}, bf16[2,16,1408]{2,1,0:T(8,128)(2,1)S(1)}, bf16[2,16,1408]{2,1,0:T(8,128)(2,1)S(1)}, bf16[2,16,1408]{2,1,0:T(8,128)(2,1)S(1)}) custom-call(s32[1]{0:T(128)} %bitcast.me_ref, s32[2,32,3]{2,1,0:T(8,128)S(1)} %copy.18.cols, f32[24]{0:T(128)S(1)} %reshape.51.stencil, f32[2,16,4096]{2,1,0:T(8,128)S(1)} %bitcast.20, ...), custom_call_target="tpu_custom_call" | custom-call | flops 201326592 | bytes 7000000 | tf_op jit(solution)/shard_map/pallas_call | solution.py:368
  19.8 2.6 %collective-permute-start.3 = (bf16[2,16,1408]{2,1,0:T(8,128)(2,1)S(1)}, bf16[2,16,1408]{2,1,0:T(8,128)(2,1)S(1)}, u32[]{:S(2)}, u32[]{:S(2)}) collective-permute-start(bf16[2,16,1408]{2,1,0:T(8,128)(2,1)S(1)} %get-tuple-element.47), channel_id=1, source_target_pairs={{0,2},{1,3},{2,0},{3,1},{4,6},{5,7},{6,4},{7,5},{8,10},{9,11},{10,... | collective-permute-start | bytes 270344 | tf_op jit(solution)/shard_map/ppermute | solution.py:323
  26.5 4.5 %collective-permute-start.5 = (bf16[8,16,1024]{2,1,0:T(8,128)(2,1)S(1)}, bf16[8,16,1024]{2,1,0:T(8,128)(2,1)S(1)}, u32[]{:S(2)}, u32[]{:S(2)}) collective-permute-start(bf16[8,16,1024]{2,1,0:T(8,128)(2,1)S(1)} %get-tuple-element.51.up), channel_id=1, source_target_pairs={{0,4},{4,8},{8,12},{12,16},{16,20},{20,24},{24,28},{28,32},{32,36}... | collective-permute-start | bytes 786440 | tf_op jit(solution)/shard_map/ppermute | solution.py:329
  32.9 2.9 %collective-permute-start.7 = (bf16[4,16,1024]{2,1,0:T(8,128)(2,1)S(1)}, bf16[4,16,1024]{2,1,0:T(8,128)(2,1)S(1)}, u32[]{:S(2)}, u32[]{:S(2)}) collective-permute-start(bf16[4,16,1024]{2,1,0:T(8,128)(2,1)S(1)} %get-tuple-element.53), channel_id=1, source_target_pairs={{0,8},{4,12},{8,16},{12,20},{16,24},{20,28},{24,32},{28,36},{32,40... | collective-permute-start | bytes 393224 | tf_op jit(solution)/shard_map/ppermute | solution.py:329
  37.7 3.8 %collective-permute-done.8.far_high = bf16[4,16,1024]{2,1,0:T(8,128)(2,1)S(1)} collective-permute-done((bf16[4,16,1024]{2,1,0:T(8,128)(2,1)S(1)}, bf16[4,16,1024]{2,1,0:T(8,128)(2,1)S(1)}, u32[]{:S(2)}, u32[]{:S(2)}) %collective-permute-start.8) | collective-permute-done | bytes 131104 | tf_op jit(solution)/shard_map/ppermute | solution.py:329
  45.7 1.9 %collective-permute-start.11 = (bf16[2,16,1024]{2,1,0:T(8,128)(2,1)S(1)}, bf16[2,16,1024]{2,1,0:T(8,128)(2,1)S(1)}, u32[]{:S(2)}, u32[]{:S(2)}) collective-permute-start(bf16[2,16,1024]{2,1,0:T(8,128)(2,1)S(1)} %get-tuple-element.59), channel_id=1, source_target_pairs={{0,3},{1,0},{2,1},{3,2},{4,7},{5,4},{6,5},{7,6},{8,11},{9,8},{10,9... | collective-permute-start | bytes 196616 | tf_op jit(solution)/shard_map/ppermute | solution.py:323
  49.1 6.7 %shard_map.79 = (bf16[2,16,1024]{2,1,0:T(8,128)(2,1)S(1)}, bf16[2,16,1024]{2,1,0:T(8,128)(2,1)S(1)}, bf16[2,16,1024]{2,1,0:T(8,128)(2,1)S(1)}, bf16[2,16,1024]{2...) custom-call(s32[1]{0:T(128)} %bitcast.me_ref, s32[2,32,3]{2,1,0:T(8,128)S(1)} %copy.18.cols, ...), custom_call_target="tpu_custom_call" | custom-call | flops 301989888 | bytes 7000000 | tf_op jit(solution)/shard_map/pallas_call | solution.py:378
  56.7 3.6 %collective-permute-start.13 = (bf16[2,16,1024]{2,1,0:T(8,128)(2,1)S(1)}, bf16[2,16,1024]{2,1,0:T(8,128)(2,1)S(1)}, u32[]{:S(2)}, u32[]{:S(2)}) collective-permute-start(bf16[2,16,1024]{2,1,0:T(8,128)(2,1)S(1)} %get-tuple-element.62), channel_id=1, source_target_pairs={{0,2},{1,3},{2,0},{3,1},{4,6},{5,7},{6,4},{7,5},{8,10},{9,11},{10,... | collective-permute-start | bytes 196616 | tf_op jit(solution)/shard_map/ppermute | solution.py:323
  63.8 7.8 %collective-permute-start.15 = (bf16[8,16,1024]{2,1,0:T(8,128)(2,1)S(1)}, bf16[8,16,1024]{2,1,0:T(8,128)(2,1)S(1)}, u32[]{:S(2)}, u32[]{:S(2)}) collective-permute-start(bf16[8,16,1024]{2,1,0:T(8,128)(2,1)S(1)} %get-tuple-element.65.up), channel_id=1, source_target_pairs={{0,4},{4,8},{8,12},{12,16},{16,20},{20,24},{24,28},{28,32},{32,36}... | collective-permute-start | bytes 786440 | tf_op jit(solution)/shard_map/ppermute | solution.py:329
  73.5 4.9 %collective-permute-start.17 = (bf16[4,16,1024]{2,1,0:T(8,128)(2,1)S(1)}, bf16[4,16,1024]{2,1,0:T(8,128)(2,1)S(1)}, u32[]{:S(2)}, u32[]{:S(2)}) collective-permute-start(bf16[4,16,1024]{2,1,0:T(8,128)(2,1)S(1)} %get-tuple-element.67), channel_id=1, source_target_pairs={{0,8},{4,12},{8,16},{12,20},{16,24},{20,28},{24,32},{28,36},{32,40... | collective-permute-start | bytes 393224 | tf_op jit(solution)/shard_map/ppermute | solution.py:329
  81.1 5.4 %collective-permute-done.18.far_high = bf16[4,16,1024]{2,1,0:T(8,128)(2,1)S(1)} collective-permute-done((bf16[4,16,1024]{2,1,0:T(8,128)(2,1)S(1)}, bf16[4,16,1024]{2,1,0:T(8,128)(2,1)S(1)}, u32[]{:S(2)}, u32[]{:S(2)}) %collective-permute-start.18) | collective-permute-done | bytes 131104 | tf_op jit(solution)/shard_map/ppermute | solution.py:329
  87.9 2.5 %collective-permute-start.20 = (f32[2,16,1024]{2,1,0:T(8,128)S(1)}, f32[2,16,1024]{2,1,0:T(8,128)S(1)}, u32[]{:S(2)}, u32[]{:S(2)}) collective-permute-start(f32[2,16,1024]{2,1,0:T(8,128)S(1)} %get-tuple-element.71), channel_id=1, source_target_pairs={{0,2},{1,3},{2,0},{3,1},{4,6},{5,7},{6,4},{7,5},{8,10},{9,11},{10,... | collective-permute-start | bytes 393224 | tf_op jit(solution)/shard_map/ppermute | solution.py:323
  90.6 2.7 %collective-permute-done.19.h1 = f32[2,16,1024]{2,1,0:T(8,128)S(1)} collective-permute-done((f32[2,16,1024]{2,1,0:T(8,128)S(1)}, f32[2,16,1024]{2,1,0:T(8,128)S(1)}, u32[]{:S(2)}, u32[]{:S(2)}) %collective-permute-start.19) | collective-permute-done | bytes 131104 | tf_op jit(solution)/shard_map/ppermute | solution.py:323
  93.3 3.3 %collective-permute-done.20.h2 = f32[2,16,1024]{2,1,0:T(8,128)S(1)} collective-permute-done((f32[2,16,1024]{2,1,0:T(8,128)S(1)}, f32[2,16,1024]{2,1,0:T(8,128)S(1)}, u32[]{:S(2)}, u32[]{:S(2)}) %collective-permute-start.20) | collective-permute-done | bytes 131104 | tf_op jit(solution)/shard_map/ppermute | solution.py:323
  97.2 6.7 %shard_map.82 = (f32[2,16,1024]{2,1,0:T(8,128)S(1)}, f32[2,16,1024]{2,1,0:T(8,128)S(1)}, f32[2,16,1024]{2,1,0:T(8,128)S(1)}, f32[2,16,1024]{2,1,0:T(8,128)S(1)},...) custom-call(s32[1]{0:T(128)} %bitcast.me_ref, s32[2,32,3]{2,1,0:T(8,128)S(1)} %copy.18.cols, ...), custom_call_target="tpu_custom_call" | custom-call | flops 402653184 | bytes 9000000 | tf_op jit(solution)/shard_map/pallas_call | solution.py:388
  104.7 3.0 %collective-permute-start.26 = (f32[2,16,1024]{2,1,0:T(8,128)S(1)}, f32[2,16,1024]{2,1,0:T(8,128)S(1)}, u32[]{:S(2)}, u32[]{:S(2)}) collective-permute-start(f32[2,16,1024]{2,1,0:T(8,128)S(1)} %get-tuple-element.82), channel_id=1, source_target_pairs={{0,2},{1,3},{2,0},{3,1},{4,6},{5,7},{6,4},{7,5},{8,10},{9,11},{10,... | collective-permute-start | bytes 393224 | tf_op jit(solution)/shard_map/ppermute | solution.py:323
  108.4 21.6 %all-to-all-start = ((f32[256,1,128]{2,1,0:T(1,128)}), f32[256,1,128]{2,1,0:T(1,128)S(1)}, u32[]{:S(2)}, u32[]{:S(2)}) async-start(f32[256,1,128]{2,1,0:T(1,128)} %broadcast_in_dim.9), calls=%async_computation | async-start | bytes 262144 | tf_op jit(solution)/shard_map/all_to_all | solution.py:395
  130.9 3.5 %collective-permute-start.28 = (f32[4,16,1024]{2,1,0:T(8,128)}, f32[4,16,1024]{2,1,0:T(8,128)S(1)}, u32[]{:S(2)}, u32[]{:S(2)}) collective-permute-start(f32[4,16,1024]{2,1,0:T(8,128)} %get-tuple-element.85), channel_id=1, source_target_pairs={{0,4},{4,8},{8,12},{12,16},{16,20},{20,24},{24,28},{28,32},{32,36}... | collective-permute-start | bytes 786440 | tf_op jit(solution)/shard_map/ppermute | solution.py:329
  136.3 6.3 %all-to-all-done.sums = f32[256,1,128]{2,1,0:T(1,128)S(1)} async-done(((f32[256,1,128]{2,1,0:T(1,128)}), f32[256,1,128]{2,1,0:T(1,128)S(1)}, u32[]{:S(2)}, u32[]{:S(2)}) %all-to-all-start) | async-done | bytes 131104 | tf_op jit(solution)/shard_map/all_to_all | solution.py:395
  145.9 2.7 %collective-permute-start.32 = (bf16[4,16,1024]{2,1,0:T(8,128)(2,1)S(1)}, bf16[4,16,1024]{2,1,0:T(8,128)(2,1)S(1)}, u32[]{:S(2)}, u32[]{:S(2)}) collective-permute-start(bf16[4,16,1024]{2,1,0:T(8,128)(2,1)S(1)} %shard_map.87.s0), channel_id=1, source_target_pairs={{0,3},{1,0},{2,1},{3,2},{4,7},{5,4},{6,5},{7,6},{8,11},{9,8},{10,9... | collective-permute-start | bytes 393224 | tf_op jit(solution)/shard_map/ppermute | solution.py:323
  151.2 3.6 %collective-permute-done.22.s1 = bf16[4,16,1024]{2,1,0:T(8,128)(2,1)S(1)} collective-permute-done((bf16[4,16,1024]{2,1,0:T(8,128)(2,1)S(1)}, bf16[4,16,1024]{2,1,0:T(8,128)(2,1)S(1)}, u32[]{:S(2)}, u32[]{:S(2)}) %collective-permute-start.22) | collective-permute-done | bytes 131104 | tf_op jit(solution)/shard_map/ppermute | solution.py:323
  155.8 3.7 %collective-permute-done.30.s1 = bf16[4,16,1024]{2,1,0:T(8,128)(2,1)S(1)} collective-permute-done((bf16[4,16,1024]{2,1,0:T(8,128)(2,1)S(1)}, bf16[4,16,1024]{2,1,0:T(8,128)(2,1)S(1)}, u32[]{:S(2)}, u32[]{:S(2)}) %collective-permute-start.30) | collective-permute-done | bytes 131104 | tf_op jit(solution)/shard_map/ppermute | solution.py:323
  (70 shorter events, 43.7 us)
Async XLA Ops:
  2.3 7.2 %collective-permute-start = (f32[2,4]{1,0:T(2,128)S(1)}, f32[2,4]{1,0:T(2,128)S(1)}, u32[]{:S(2)}, u32[]{:S(2)}) collective-permute-start(f32[2,4]{1,0:T(2,128)S(1)} %get-tuple-element.95), channel_id=1, source_target_pairs={{0,4},{4,8},{8,12},{12,16},{16,20},{20,24},{24,28},{28,32},{32,36}... | collective-permute-start | bytes 104 | tf_op jit(solution)/shard_map/ppermute | solution.py:329
  19.8 6.0 %collective-permute-start.3 = (bf16[2,16,1408]{2,1,0:T(8,128)(2,1)S(1)}, bf16[2,16,1408]{2,1,0:T(8,128)(2,1)S(1)}, u32[]{:S(2)}, u32[]{:S(2)}) collective-permute-start(bf16[2,16,1408]{2,1,0:T(8,128)(2,1)S(1)} %get-tuple-element.47), channel_id=1, source_target_pairs={{0,2},{1,3},{2,0},{3,1},{4,6},{5,7},{6,4},{7,5},{8,10},{9,11},{10,... | collective-permute-start | bytes 270344 | tf_op jit(solution)/shard_map/ppermute | solution.py:323
  26.5 15.0 %collective-permute-start.5 = (bf16[8,16,1024]{2,1,0:T(8,128)(2,1)S(1)}, bf16[8,16,1024]{2,1,0:T(8,128)(2,1)S(1)}, u32[]{:S(2)}, u32[]{:S(2)}) collective-permute-start(bf16[8,16,1024]{2,1,0:T(8,128)(2,1)S(1)} %get-tuple-element.51.up), channel_id=1, source_target_pairs={{0,4},{4,8},{8,12},{12,16},{16,20},{20,24},{24,28},{28,32},{32,36}... | collective-permute-start | bytes 786440 | tf_op jit(solution)/shard_map/ppermute | solution.py:329
  30.9 10.5 %collective-permute-start.6 = (bf16[8,16,1024]{2,1,0:T(8,128)(2,1)S(1)}, bf16[8,16,1024]{2,1,0:T(8,128)(2,1)S(1)}, u32[]{:S(2)}, u32[]{:S(2)}) collective-permute-start(bf16[8,16,1024]{2,1,0:T(8,128)(2,1)S(1)} %get-tuple-element.52.down), channel_id=1, source_target_pairs={{4,0},{8,4},{12,8},{16,12},{20,16},{24,20},{28,24},{32,28},{36,32}... | collective-permute-start | bytes 786440 | tf_op jit(solution)/shard_map/ppermute | solution.py:329
  56.7 5.9 %collective-permute-start.13 = (bf16[2,16,1024]{2,1,0:T(8,128)(2,1)S(1)}, bf16[2,16,1024]{2,1,0:T(8,128)(2,1)S(1)}, u32[]{:S(2)}, u32[]{:S(2)}) collective-permute-start(bf16[2,16,1024]{2,1,0:T(8,128)(2,1)S(1)} %get-tuple-element.62), channel_id=1, source_target_pairs={{0,2},{1,3},{2,0},{3,1},{4,6},{5,7},{6,4},{7,5},{8,10},{9,11},{10,... | collective-permute-start | bytes 196616 | tf_op jit(solution)/shard_map/ppermute | solution.py:323
  63.8 22.7 %collective-permute-start.15 = (bf16[8,16,1024]{2,1,0:T(8,128)(2,1)S(1)}, bf16[8,16,1024]{2,1,0:T(8,128)(2,1)S(1)}, u32[]{:S(2)}, u32[]{:S(2)}) collective-permute-start(bf16[8,16,1024]{2,1,0:T(8,128)(2,1)S(1)} %get-tuple-element.65.up), channel_id=1, source_target_pairs={{0,4},{4,8},{8,12},{12,16},{16,20},{20,24},{24,28},{28,32},{32,36}... | collective-permute-start | bytes 786440 | tf_op jit(solution)/shard_map/ppermute | solution.py:329
  71.6 14.9 %collective-permute-start.16 = (bf16[8,16,1024]{2,1,0:T(8,128)(2,1)S(1)}, bf16[8,16,1024]{2,1,0:T(8,128)(2,1)S(1)}, u32[]{:S(2)}, u32[]{:S(2)}) collective-permute-start(bf16[8,16,1024]{2,1,0:T(8,128)(2,1)S(1)} %get-tuple-element.66.down), channel_id=1, source_target_pairs={{4,0},{8,4},{12,8},{16,12},{20,16},{24,20},{28,24},{32,28},{36,32}... | collective-permute-start | bytes 786440 | tf_op jit(solution)/shard_map/ppermute | solution.py:329
  73.5 7.5 %collective-permute-start.17 = (bf16[4,16,1024]{2,1,0:T(8,128)(2,1)S(1)}, bf16[4,16,1024]{2,1,0:T(8,128)(2,1)S(1)}, u32[]{:S(2)}, u32[]{:S(2)}) collective-permute-start(bf16[4,16,1024]{2,1,0:T(8,128)(2,1)S(1)} %get-tuple-element.67), channel_id=1, source_target_pairs={{0,8},{4,12},{8,16},{12,20},{16,24},{20,28},{24,32},{28,36},{32,40... | collective-permute-start | bytes 393224 | tf_op jit(solution)/shard_map/ppermute | solution.py:329
  78.4 8.1 %collective-permute-start.18 = (bf16[4,16,1024]{2,1,0:T(8,128)(2,1)S(1)}, bf16[4,16,1024]{2,1,0:T(8,128)(2,1)S(1)}, u32[]{:S(2)}, u32[]{:S(2)}) collective-permute-start(bf16[4,16,1024]{2,1,0:T(8,128)(2,1)S(1)} %get-tuple-element.68), channel_id=1, source_target_pairs={{8,0},{12,4},{16,8},{20,12},{24,16},{28,20},{32,24},{36,28},{40,32... | collective-permute-start | bytes 393224 | tf_op jit(solution)/shard_map/ppermute | solution.py:329
  87.2 6.1 %collective-permute-start.19 = (f32[2,16,1024]{2,1,0:T(8,128)S(1)}, f32[2,16,1024]{2,1,0:T(8,128)S(1)}, u32[]{:S(2)}, u32[]{:S(2)}) collective-permute-start(f32[2,16,1024]{2,1,0:T(8,128)S(1)} %get-tuple-element.70), channel_id=1, source_target_pairs={{0,1},{1,2},{2,3},{3,0},{4,5},{5,6},{6,7},{7,4},{8,9},{9,10},{10,1... | collective-permute-start | bytes 393224 | tf_op jit(solution)/shard_map/ppermute | solution.py:323
  87.9 8.7 %collective-permute-start.20 = (f32[2,16,1024]{2,1,0:T(8,128)S(1)}, f32[2,16,1024]{2,1,0:T(8,128)S(1)}, u32[]{:S(2)}, u32[]{:S(2)}) collective-permute-start(f32[2,16,1024]{2,1,0:T(8,128)S(1)} %get-tuple-element.71), channel_id=1, source_target_pairs={{0,2},{1,3},{2,0},{3,1},{4,6},{5,7},{6,4},{7,5},{8,10},{9,11},{10,... | collective-permute-start | bytes 393224 | tf_op jit(solution)/shard_map/ppermute | solution.py:323
  90.4 6.8 %collective-permute-start.21 = (f32[2,16,1024]{2,1,0:T(8,128)S(1)}, f32[2,16,1024]{2,1,0:T(8,128)S(1)}, u32[]{:S(2)}, u32[]{:S(2)}) collective-permute-start(f32[2,16,1024]{2,1,0:T(8,128)S(1)} %get-tuple-element.72), channel_id=1, source_target_pairs={{0,3},{1,0},{2,1},{3,2},{4,7},{5,4},{6,5},{7,6},{8,11},{9,8},{10,9... | collective-permute-start | bytes 393224 | tf_op jit(solution)/shard_map/ppermute | solution.py:323
  103.9 26.0 %collective-permute-start.25 = (f32[2,16,1024]{2,1,0:T(8,128)S(1)}, f32[2,16,1024]{2,1,0:T(8,128)S(1)}, u32[]{:S(2)}, u32[]{:S(2)}) collective-permute-start(f32[2,16,1024]{2,1,0:T(8,128)S(1)} %get-tuple-element.81), channel_id=1, source_target_pairs={{0,1},{1,2},{2,3},{3,0},{4,5},{5,6},{6,7},{7,4},{8,9},{9,10},{10,1... | collective-permute-start | bytes 393224 | tf_op jit(solution)/shard_map/ppermute | solution.py:323
  104.7 25.3 %collective-permute-start.26 = (f32[2,16,1024]{2,1,0:T(8,128)S(1)}, f32[2,16,1024]{2,1,0:T(8,128)S(1)}, u32[]{:S(2)}, u32[]{:S(2)}) collective-permute-start(f32[2,16,1024]{2,1,0:T(8,128)S(1)} %get-tuple-element.82), channel_id=1, source_target_pairs={{0,2},{1,3},{2,0},{3,1},{4,6},{5,7},{6,4},{7,5},{8,10},{9,11},{10,... | collective-permute-start | bytes 393224 | tf_op jit(solution)/shard_map/ppermute | solution.py:323
  107.7 22.4 %collective-permute-start.27 = (f32[2,16,1024]{2,1,0:T(8,128)S(1)}, f32[2,16,1024]{2,1,0:T(8,128)S(1)}, u32[]{:S(2)}, u32[]{:S(2)}) collective-permute-start(f32[2,16,1024]{2,1,0:T(8,128)S(1)} %get-tuple-element.83), channel_id=1, source_target_pairs={{0,3},{1,0},{2,1},{3,2},{4,7},{5,4},{6,5},{7,6},{8,11},{9,8},{10,9... | collective-permute-start | bytes 393224 | tf_op jit(solution)/shard_map/ppermute | solution.py:323
  108.4 34.3 %all-to-all-start = ((f32[256,1,128]{2,1,0:T(1,128)}), f32[256,1,128]{2,1,0:T(1,128)S(1)}, u32[]{:S(2)}, u32[]{:S(2)}) async-start(f32[256,1,128]{2,1,0:T(1,128)} %broadcast_in_dim.9), calls=%async_computation | async-start | bytes 262144 | tf_op jit(solution)/shard_map/all_to_all | solution.py:395
  130.9 14.5 %collective-permute-start.28 = (f32[4,16,1024]{2,1,0:T(8,128)}, f32[4,16,1024]{2,1,0:T(8,128)S(1)}, u32[]{:S(2)}, u32[]{:S(2)}) collective-permute-start(f32[4,16,1024]{2,1,0:T(8,128)} %get-tuple-element.85), channel_id=1, source_target_pairs={{0,4},{4,8},{8,12},{12,16},{16,20},{20,24},{24,28},{28,32},{32,36}... | collective-permute-start | bytes 786440 | tf_op jit(solution)/shard_map/ppermute | solution.py:329
  134.4 11.0 %collective-permute-start.29 = (f32[4,16,1024]{2,1,0:T(8,128)S(1)}, f32[4,16,1024]{2,1,0:T(8,128)S(1)}, u32[]{:S(2)}, u32[]{:S(2)}) collective-permute-start(f32[4,16,1024]{2,1,0:T(8,128)S(1)} %get-tuple-element.86), channel_id=1, source_target_pairs={{4,0},{8,4},{12,8},{16,12},{20,16},{24,20},{28,24},{32,28},{36,32}... | collective-permute-start | bytes 786440 | tf_op jit(solution)/shard_map/ppermute | solution.py:329
  143.2 6.1 %collective-permute-start.24 = (bf16[4,16,1024]{2,1,0:T(8,128)(2,1)S(1)}, bf16[4,16,1024]{2,1,0:T(8,128)(2,1)S(1)}, u32[]{:S(2)}, u32[]{:S(2)}) collective-permute-start(bf16[4,16,1024]{2,1,0:T(8,128)(2,1)S(1)} %shard_map.83.s0), channel_id=1, source_target_pairs={{0,3},{1,0},{2,1},{3,2},{4,7},{5,4},{6,5},{7,6},{8,11},{9,8},{10,9... | collective-permute-start | bytes 393224 | tf_op jit(solution)/shard_map/ppermute | solution.py:323
  144.2 7.0 %collective-permute-start.23 = (bf16[4,16,1024]{2,1,0:T(8,128)(2,1)S(1)}, bf16[4,16,1024]{2,1,0:T(8,128)(2,1)S(1)}, u32[]{:S(2)}, u32[]{:S(2)}) collective-permute-start(bf16[4,16,1024]{2,1,0:T(8,128)(2,1)S(1)} %shard_map.83.s0), channel_id=1, source_target_pairs={{0,2},{1,3},{2,0},{3,1},{4,6},{5,7},{6,4},{7,5},{8,10},{9,11},{10,... | collective-permute-start | bytes 393224 | tf_op jit(solution)/shard_map/ppermute | solution.py:323
  145.4 9.4 %collective-permute-start.22 = (bf16[4,16,1024]{2,1,0:T(8,128)(2,1)S(1)}, bf16[4,16,1024]{2,1,0:T(8,128)(2,1)S(1)}, u32[]{:S(2)}, u32[]{:S(2)}) collective-permute-start(bf16[4,16,1024]{2,1,0:T(8,128)(2,1)S(1)} %shard_map.83.s0), channel_id=1, source_target_pairs={{0,1},{1,2},{2,3},{3,0},{4,5},{5,6},{6,7},{7,4},{8,9},{9,10},{10,1... | collective-permute-start | bytes 393224 | tf_op jit(solution)/shard_map/ppermute | solution.py:323
  145.9 9.9 %collective-permute-start.32 = (bf16[4,16,1024]{2,1,0:T(8,128)(2,1)S(1)}, bf16[4,16,1024]{2,1,0:T(8,128)(2,1)S(1)}, u32[]{:S(2)}, u32[]{:S(2)}) collective-permute-start(bf16[4,16,1024]{2,1,0:T(8,128)(2,1)S(1)} %shard_map.87.s0), channel_id=1, source_target_pairs={{0,3},{1,0},{2,1},{3,2},{4,7},{5,4},{6,5},{7,6},{8,11},{9,8},{10,9... | collective-permute-start | bytes 393224 | tf_op jit(solution)/shard_map/ppermute | solution.py:323
  148.7 7.1 %collective-permute-start.31 = (bf16[4,16,1024]{2,1,0:T(8,128)(2,1)S(1)}, bf16[4,16,1024]{2,1,0:T(8,128)(2,1)S(1)}, u32[]{:S(2)}, u32[]{:S(2)}) collective-permute-start(bf16[4,16,1024]{2,1,0:T(8,128)(2,1)S(1)} %shard_map.87.s0), channel_id=1, source_target_pairs={{0,2},{1,3},{2,0},{3,1},{4,6},{5,7},{6,4},{7,5},{8,10},{9,11},{10,... | collective-permute-start | bytes 393224 | tf_op jit(solution)/shard_map/ppermute | solution.py:323
  149.3 10.2 %collective-permute-start.30 = (bf16[4,16,1024]{2,1,0:T(8,128)(2,1)S(1)}, bf16[4,16,1024]{2,1,0:T(8,128)(2,1)S(1)}, u32[]{:S(2)}, u32[]{:S(2)}) collective-permute-start(bf16[4,16,1024]{2,1,0:T(8,128)(2,1)S(1)} %shard_map.87.s0), channel_id=1, source_target_pairs={{0,1},{1,2},{2,3},{3,0},{4,5},{5,6},{6,7},{7,4},{8,9},{9,10},{10,1... | collective-permute-start | bytes 393224 | tf_op jit(solution)/shard_map/ppermute | solution.py:323
  (12 other events, 110.5 us)
where the time goes:
time: 161 us
  starting transfers between devices  88 us (55%)
  waiting for transfers between devices  40.6 us (25%)
  Pallas kernels  26.7 us (17%)
  local copies, waits for them, and re-layouts  3.33 us (2%)
    ppermute x12, starting transfers between devices, along_slab(): return lax.ppermute(value, 'slab', pairs)  38.3 us
    ppermute x21, starting transfers between devices, along_ang(): lax.ppermute(value, 'ang', [(i, (i + steps) % ANG) for i in range(ANG)])  28.1 us
    all_to_all x1, starting transfers between devices, per_device(): lax.all_to_all(jnp.broadcast_to(sums[None], (count, 1, 128)), ('slab', 'a...  21.6 us
    ppermute x21, waiting for transfers between devices, along_ang(): lax.ppermute(value, 'ang', [(i, (i + steps) % ANG) for i in range(ANG)])  20.9 us
    ppermute x12, waiting for transfers between devices, along_slab(): return lax.ppermute(value, 'slab', pairs)  13.4 us
    pallas_call x1, Pallas kernels, per_device(): call(second_kernel, [share(F32)] * 4 + [full, sds((1, 128), F32)], [SMEM]...  6.74 us
    pallas_call x1, Pallas kernels, per_device(): call(first_kernel, [share(MID)] * 4 + [full, sds((8, 128), F32)], [SMEM]...  6.74 us
    all_to_all x1, waiting for transfers between devices, per_device(): lax.all_to_all(jnp.broadcast_to(sums[None], (count, 1, 128)), ('slab', 'a...  6.32 us
  transfers between devices with their start and end apart: 34, of which 19 were waited for; matrix products, arithmetic and copies ran while one was open for 1% of the time, Pallas kernels for 3%

commit v1 on v0

--- a/solution.py
+++ b/solution.py
@@ -21,19 +21,18 @@
 GROUP = 8
 VMEM = pl.BlockSpec(memory_space=pltpu.VMEM)
 SMEM = pl.BlockSpec(memory_space=pltpu.SMEM)
+MID = BF16
 HBM = pl.BlockSpec(memory_space=pltpu.HBM)
-MID = BF16
-LIMIT = 48 * 1024 * 1024
-
-
-def call(kernel, outs, specs, scratch=(), flops=0, nbytes=2_000_000):
+
+
+def call(kernel, outs, specs, scratch=(), flops=0, nbytes=2_000_000, limit=24):
     return pl.pallas_call(
         kernel,
         out_shape=outs,
         in_specs=specs,
         out_specs=[VMEM] * len(outs),
         scratch_shapes=list(scratch),
-        compiler_params=pltpu.CompilerParams(vmem_limit_bytes=LIMIT),
+        compiler_params=pltpu.CompilerParams(vmem_limit_bytes=limit * 1024 * 1024),
         cost_estimate=pl.CostEstimate(flops=flops, bytes_accessed=nbytes, transcendentals=0),
     )
 
@@ -56,25 +55,14 @@
     return out
 
 
-def weight_copies(w_hbm, w_buf, sem):
-    return [
-        pltpu.make_async_copy(
-            w_hbm.at[a, pl.ds(GROUP * g, GROUP)], w_buf.at[a, pl.ds(GROUP * g, GROUP)],
-            sem.at[a, g],
-        )
-        for a in range(PAIR)
-        for g in range(UB // GROUP)
-    ]
-
-
 def window(cols, a, block):
-    return pl.ds(pl.multiple_of(cols[a, block, 0] * 128, 128), 384)
-
-
-def back_block(a, block, value, cols, w_buf, acc):
+    return pl.ds(pl.multiple_of(cols[0, a, block] * 128, 128), 384)
+
+
+def back_block(a, block, value, cols, w, acc):
     both = halves(value)
     spread = lax.dot_general(
-        both, w_buf[a, block], (((1,), (1,)), ((), ())), preferred_element_type=F32
+        both, w[a, block], (((1,), (1,)), ((), ())), preferred_element_type=F32
     )
     at = window(cols, a, block)
     acc[a, :, at] += spread[:L] + spread[L:]
@@ -87,24 +75,35 @@
         outs[r][:, :, :Q] = share.astype(outs[r].dtype)
 
 
-def back_kernel(me_ref, cols, stencil, p_ref, w_hbm, o0, o1, o2, o3, w_buf, acc, sem):
-    copies = weight_copies(w_hbm, w_buf, sem)
-    for copy in copies:
-        copy.start()
+def mask_kernel(rows, reach, above, below):
+    for i in range(PAIR):
+        for z in range(ZD):
+            top = jnp.where(reach[i, 0, 1] == 1, rows[i, 0, 2, 0, z], 0.0)
+            low = jnp.where(reach[i, 0, 0] == -1, rows[i, 0, 0, 0, z], 0.0)
+            above[ZD * i + z:ZD * i + z + 1] = jnp.full((1, 128), top, F32)
+            below[ZD * i + z:ZD * i + z + 1] = jnp.full((1, 128), low, F32)
+
+
+def back_kernel(me_ref, cols, rows, from_low, from_high, p_ref, w_hbm, o0, o1, o2, o3, w, acc, sem):
+    copies = {}
+    for a in range(PAIR):
+        for g in range(UB // GROUP):
+            span = pl.ds(GROUP * g, GROUP)
+            copies[a, g] = pltpu.make_async_copy(w_hbm.at[a, span], w.at[a, span], sem.at[a, g])
+            copies[a, g].start()
     acc[...] = jnp.zeros_like(acc)
     for a in range(PAIR):
-        for g in range(UB // GROUP):
-            copies[a * (UB // GROUP) + g].wait()
-            for i in range(GROUP):
-                block = g * GROUP + i
-                back_block(a, block, p_ref[a, :, 128 * block:128 * (block + 1)], cols, w_buf, acc)
+        for block in range(UB):
+            if block % GROUP == 0:
+                copies[a, block // GROUP].wait()
+            back_block(a, block, p_ref[a, 0, :, 128 * block:128 * (block + 1)], cols, w, acc)
     outs = (o0, o1, o2, o3)
     send_shares(me_ref[0], acc, outs)
-    at_row = lax.broadcasted_iota(jnp.int32, (L, 128), 0)
     for i in range(PAIR):
-        rest = jnp.zeros((L, 128), F32)
-        for e in range(12):
-            rest = jnp.where(at_row == e, stencil[12 * i + e], rest)
+        own = [jnp.full((1, 128), rows[i, 0, 1, 0, z], F32) for z in range(ZD)]
+        rest = jnp.concatenate(
+            [from_low[ZD * i:ZD * (i + 1)]] + own + [from_high[ZD * i:ZD * (i + 1)], jnp.zeros((4, 128), F32)], axis=0
+        )
         for part in range(3):
             piece = rest.astype(BF16)
             rest = rest - piece.astype(F32)
@@ -112,21 +111,20 @@
                 out[i, :, Q + 128 * part:Q + 128 * (part + 1)] = piece
 
 
-def both_body(cols, copies, w_buf, acc, lhs, store):
+def both_body(cols, w, acc, lhs, store):
     acc[...] = jnp.zeros_like(acc)
     for a in range(PAIR):
         for g in range(UB // GROUP):
-            copies[a * (UB // GROUP) + g].wait()
             images = []
             for i in range(GROUP):
                 block = g * GROUP + i
-                image = jnp.dot(lhs(a, window(cols, a, block)), w_buf[a, block], preferred_element_type=F32)
+                image = jnp.dot(lhs(a, window(cols, a, block)), w[a, block], preferred_element_type=F32)
                 if image.shape[0] > L:
                     image = image[:L] + image[L:]
                 store(a, block, image)
                 images.append(image)
             for i in range(GROUP):
-                back_block(a, g * GROUP + i, images[i], cols, w_buf, acc)
+                back_block(a, g * GROUP + i, images[i], cols, w, acc)
 
 
 def gather_shares(me, shares, place):
@@ -135,10 +133,7 @@
         place(pl.ds(pl.multiple_of(quarter * Q, Q), Q), shares[r])
 
 
-def first_kernel(me_ref, cols, h0, h1, h2, h3, w_hbm, o0, o1, o2, o3, q_out, dots, hb, w_buf, acc, sem):
-    copies = weight_copies(w_hbm, w_buf, sem)
-    for copy in copies:
-        copy.start()
+def first_kernel(me_ref, cols, h0, h1, h2, h3, w, o0, o1, o2, o3, q_out, dots, hb, acc):
 
     def place(at, share):
         hb[:, :, at] = share[...]
@@ -147,16 +142,13 @@
         q_out[a, :, 128 * block:128 * (block + 1)] = image
 
     gather_shares(me_ref[0], (h0, h1, h2, h3), place)
-    both_body(cols, copies, w_buf, acc, lambda a, at: hb[a, :, at], store)
+    both_body(cols, w, acc, lambda a, at: hb[a, :, at], store)
     send_shares(me_ref[0], acc, (o0, o1, o2, o3))
     dots[...] = fold(q_out[0] * q_out[0]) + fold(q_out[1] * q_out[1])
 
 
-def second_kernel(me_ref, cols, h0, h1, h2, h3, q0_ref, gamma_ref, curve_ref, inner_ref, w_hbm,
-                  o0, o1, o2, o3, w_out, sums, both, w_buf, acc, sem):
-    copies = weight_copies(w_hbm, w_buf, sem)
-    for copy in copies:
-        copy.start()
+def second_kernel(me_ref, cols, h0, h1, h2, h3, q0_ref, gamma_ref, curve_ref, inner_ref, w,
+                  o0, o1, o2, o3, w_out, sums, both, acc):
 
     def place(at, share):
         for a in range(PAIR):
@@ -166,7 +158,7 @@
         w_out[a, :, 128 * block:128 * (block + 1)] = image
 
     gather_shares(me_ref[0], (h0, h1, h2, h3), place)
-    both_body(cols, copies, w_buf, acc, lambda a, at: both[a, :, at], store)
+    both_body(cols, w, acc, lambda a, at: both[a, :, at], store)
     send_shares(me_ref[0], acc, (o0, o1, o2, o3))
     cross = fold(w_out[0] * q0_ref[0]) + fold(w_out[1] * q0_ref[1])
     own = fold(w_out[0] * w_out[0]) + fold(w_out[1] * w_out[1])
@@ -174,7 +166,7 @@
     row = jnp.zeros((1, 128), F32)
     for at, value in enumerate((gamma_ref[...], curve_ref[...], inner_ref[:8], inner_ref[8:], cross, own)):
         row = jnp.where(lane == at, jnp.sum(value), row)
-    sums[...] = row
+    sums[...] = jnp.broadcast_to(row[None], sums.shape)
 
 
 def spread_slices(coefs, parts, cut):
@@ -309,7 +301,7 @@
 def residual_kernel(sums, p, q0, w0, out):
     one, two = steps(sums)
     for a in range(PAIR):
-        out[a] = p[a] - one * q0[a] + two * w0[a]
+        out[a, 0] = p[a, 0] - one * q0[a] + two * w0[a]
 
 
 def place_kernel(me_ref, s0, s1, s2, s3, out):
@@ -337,14 +329,12 @@
 
 
 def per_device(projections, weights, columns, row_weights, reach):
-    rows = row_weights[:, 0, :, 0, :]
-    below = rows[:, 0] * (reach[:, 0, :1] == -1).astype(F32)
-    above = rows[:, 2] * (reach[:, 0, 1:] == 1).astype(F32)
-    stencil = jnp.stack([along_slab(above, 1), rows[:, 1], along_slab(below, -1)], axis=1).reshape(PAIR * 12)
+    row = sds((PAIR * ZD, 128), F32)
+    above, below = call(mask_kernel, [row] * 2, [SMEM] * 2)(row_weights, reach)
+    edges = (along_slab(above, 1), along_slab(below, -1))
 
     me = lax.axis_index("ang").astype(jnp.int32).reshape(1)
-    w = weights.reshape(PAIR, UB, 384, 128)
-    p = projections.reshape(PAIR, L, X)
+    cols = columns.transpose(2, 0, 1)
 
     def share(dtype, more=0):
         return sds((PAIR, L, Q + more), dtype)
@@ -353,11 +343,7 @@
     part = sds((ZD, L, Q), F32)
     part_b = sds((ZD, L, Q), BF16)
     two_b = sds((2 * ZD, L, Q), BF16)
-    w_scratch = [
-        pltpu.VMEM((PAIR, UB, 384, 128), BF16),
-        pltpu.VMEM((PAIR, L, X), F32),
-        pltpu.SemaphoreType.DMA((PAIR, UB // GROUP)),
-    ]
+    acc = pltpu.VMEM((PAIR, L, X), F32)
     macs = 2 * PAIR * L * UB * 384 * 128
     sent = [part, two_b, two_b, part_b, part_b]
 
@@ -365,9 +351,11 @@
         return (t1, up, down, along_slab(up, 1), along_slab(down, -1),
                 along_slab(up_far, 2), along_slab(down_far, -2))
 
-    shares = call(
-        back_kernel, [share(BF16, COEF)] * 4, [SMEM] * 3 + [VMEM, HBM], w_scratch, flops=2 * macs, nbytes=7_000_000
-    )(me, columns, stencil, p, w)
+    *shares, w = call(
+        back_kernel, [share(BF16, COEF)] * 4 + [sds((PAIR, UB, 384, 128), BF16)],
+        [SMEM] * 3 + [VMEM] * 3 + [HBM], [acc, pltpu.SemaphoreType.DMA((PAIR, UB // GROUP))],
+        flops=2 * macs, nbytes=7_000_000, limit=46,
+    )(me, cols, row_weights, *edges, projections, weights.reshape(PAIR, UB, 384, 128))
     *spread, coefs = call(
         open_kernel, sent + [sds((ANG, PAIR, L, 128), F32)], [VMEM] * 4, flops=10_000_000
     )(*exchange(shares))
@@ -377,24 +365,23 @@
 
     *shares, q0, curve = call(
         first_kernel, [share(MID)] * 4 + [full, sds((8, 128), F32)],
-        [SMEM] * 2 + [VMEM] * 4 + [HBM], [pltpu.VMEM((PAIR, L, X), BF16)] + w_scratch,
+        [SMEM] * 2 + [VMEM] * 5, [pltpu.VMEM((PAIR, L, X), BF16), acc],
         flops=3 * macs, nbytes=7_000_000,
-    )(me, columns, *exchange(shares), w)
+    )(me, cols, *exchange(shares), w)
     spread = call(combine_kernel, sent, [VMEM] * 5, flops=10_000_000)(coefs, *exchange(shares))
     z0, *shares, inner = call(
         pieces_second, [part] + [share(F32)] * 4 + [sds((16, 128), F32)], [VMEM] * 9, flops=10_000_000
     )(coefs, g0, *halo(*spread))
 
     *shares, w0, sums = call(
-        second_kernel, [share(F32)] * 4 + [full, sds((1, 128), F32)],
-        [SMEM] * 2 + [VMEM] * 8 + [HBM], [pltpu.VMEM((PAIR, 2 * L, X), BF16)] + w_scratch,
+        second_kernel, [share(F32)] * 4 + [full, sds((lax.axis_size("slab") * ANG, 1, 128), F32)],
+        [SMEM] * 2 + [VMEM] * 9, [pltpu.VMEM((PAIR, 2 * L, X), BF16), acc],
         flops=4 * macs, nbytes=9_000_000,
-    )(me, columns, *exchange(shares), q0, gamma, curve, inner, w)
+    )(me, cols, *exchange(shares), q0, gamma, curve, inner, w)
     shares = exchange(shares)
-    count = lax.axis_size("slab") * ANG
-    sums = lax.all_to_all(jnp.broadcast_to(sums[None], (count, 1, 128)), ("slab", "ang"), 0, 0, tiled=True)
+    sums = lax.all_to_all(sums, ("slab", "ang"), 0, 0, tiled=True)
     (volume,) = call(volume_kernel, [part_b], [VMEM] * 3)(sums, g0, z0)
-    (residual,) = call(residual_kernel, [full], [VMEM] * 4)(sums, p, q0, w0)
+    (residual,) = call(residual_kernel, [sds(projections.shape, F32)], [VMEM] * 4)(sums, projections, q0, w0)
     volume = exchange((volume,) * 4)
     t1, up, down = call(last_kernel, [part] * 3, [VMEM] * 5, flops=10_000_000)(coefs, *shares)
     (gradient,) = call(gradient_kernel, [part_b], [VMEM] * 6)(
@@ -403,7 +390,7 @@
     whole = [sds((ZD, L, X), F32)]
     (volume,) = call(place_kernel, whole, [SMEM] + [VMEM] * 4)(me, *volume)
     (gradient,) = call(place_kernel, whole, [SMEM] + [VMEM] * 4)(me, *exchange((gradient,) * 4))
-    return volume, residual.reshape(projections.shape), gradient
+    return volume, residual, gradient
 
 
 def solution(mesh):

time: 161 us -> 157 us (0.975)
  Pallas kernels: 26.7 us -> 22.2 us
    pallas_call x1, Pallas kernels: 6.74 us -> 4.11 us  [per_device(): call(first_kernel, [share(MID)] * 4 + [full, sds((8, 128), F32)], [SMEM]...]
    pallas_call x3 -> x4, Pallas kernels: 13.7 us -> 11.9 us  [the longest x1 5.08 us: per_device(): call(back_kernel, [share(BF16, COEF)] * 4 + [sds((PAIR, UB, 384, 128), BF...]
    unnamed x6 -> x12, local copies, waits for them, and re-layouts: 2.51 us -> 3.77 us
  transfers between devices with their start and end apart: 34 -> 34, of which waited for: 19 -> 19; matrix products, arithmetic and copies ran while one was open for 1% -> 0% of each run, Pallas kernels for 3% -> 3%
where the time goes in v1:
time: 157 us
  starting transfers between devices  88.3 us (56%)
  waiting for transfers between devices  41.5 us (26%)
  Pallas kernels  22.2 us (14%)
  local copies, waits for them, and re-layouts  3.77 us (2%)
    ppermute x12, starting transfers between devices, along_slab(): return lax.ppermute(value, 'slab', pairs)  38.4 us
    ppermute x21, starting transfers between devices, along_ang(): lax.ppermute(value, 'ang', [(i, (i + steps) % ANG) for i in range(ANG)])  28 us
    all_to_all x1, starting transfers between devices, per_device(): sums = lax.all_to_all(sums, ('slab', 'ang'), 0, 0, tiled=True)  21.9 us
    ppermute x21, waiting for transfers between devices, along_ang(): lax.ppermute(value, 'ang', [(i, (i + steps) % ANG) for i in range(ANG)])  20.9 us
    ppermute x12, waiting for transfers between devices, along_slab(): return lax.ppermute(value, 'slab', pairs)  14.2 us
    all_to_all x1, waiting for transfers between devices, per_device(): sums = lax.all_to_all(sums, ('slab', 'ang'), 0, 0, tiled=True)  6.32 us
    pallas_call x1, Pallas kernels, per_device(): call(back_kernel, [share(BF16, COEF)] * 4 + [sds((PAIR, UB, 384, 128), BF...  5.08 us
    pallas_call x1, Pallas kernels, per_device(): call(second_kernel, [share(F32)] * 4 + [full, sds((lax.axis_size('slab')...  4.76 us
  transfers between devices with their start and end apart: 34, of which 19 were waited for; matrix products, arithmetic and copies ran while one was open for 0% of the time, Pallas kernels for 3%

profile of v1, /device:TPU:1, one launch (start us, length us, event | category | flops | bytes accessed | tf_op | source)
XLA Modules:
  0.0 156.7 jit_solution(4403677415915666166)
XLA Ops:
  2.6 4.5 %collective-permute-start = (f32[8,128]{1,0:T(8,128)S(1)}, f32[8,128]{1,0:T(8,128)S(1)}, u32[]{:S(2)}, u32[]{:S(2)}) collective-permute-start(f32[8,128]{1,0:T(8,128)S(1)} %get-tuple-element.48), channel_id=1, source_target_pairs={{0,4},{4,8},{8,12},{12,16},{16,20},{20,24},{24,28},{28,32},{32,36}... | collective-permute-start | bytes 12296 | tf_op jit(solution)/shard_map/ppermute | solution.py:321
  7.1 1.9 %collective-permute-start.1 = (f32[8,128]{1,0:T(8,128)S(1)}, f32[8,128]{1,0:T(8,128)S(1)}, u32[]{:S(2)}, u32[]{:S(2)}) collective-permute-start(f32[8,128]{1,0:T(8,128)S(1)} %get-tuple-element.49), channel_id=1, source_target_pairs={{4,0},{8,4},{12,8},{16,12},{20,16},{24,20},{28,24},{32,28},{36,32}... | collective-permute-start | bytes 12296 | tf_op jit(solution)/shard_map/ppermute | solution.py:321
  9.1 3.0 %collective-permute-done.1.from_high = f32[8,128]{1,0:T(8,128)S(1)} collective-permute-done((f32[8,128]{1,0:T(8,128)S(1)}, f32[8,128]{1,0:T(8,128)S(1)}, u32[]{:S(2)}, u32[]{:S(2)}) %collective-permute-start.1) | collective-permute-done | bytes 4128 | tf_op jit(solution)/shard_map/ppermute | solution.py:321
  14.5 5.1 %shard_map.77 = (bf16[2,16,1408]{2,1,0:T(8,128)(2,1)S(1)}, bf16[2,16,1408]{2,1,0:T(8,128)(2,1)S(1)}, bf16[2,16,1408]{2,1,0:T(8,128)(2,1)S(1)}, bf16[2,16,1408]{2...) custom-call(s32[1]{0:T(128)} %bitcast.me_ref, s32[3,2,32]{2,1,0:T(2,128)S(1)} %bitcast.3, f32[2,1,3,1,4]{4,3,2,1,0:T(1,128)S(1)} %copy-done.4, ...), custom_call_target="tpu_custom_call" | custom-call | flops 201326592 | bytes 7000000 | tf_op jit(solution)/shard_map/pallas_call | solution.py:354
  20.9 2.6 %collective-permute-start.3 = (bf16[2,16,1408]{2,1,0:T(8,128)(2,1)S(1)}, bf16[2,16,1408]{2,1,0:T(8,128)(2,1)S(1)}, u32[]{:S(2)}, u32[]{:S(2)}) collective-permute-start(bf16[2,16,1408]{2,1,0:T(8,128)(2,1)S(1)} %get-tuple-element.52), channel_id=1, source_target_pairs={{0,2},{1,3},{2,0},{3,1},{4,6},{5,7},{6,4},{7,5},{8,10},{9,11},{10,... | collective-permute-start | bytes 270344 | tf_op jit(solution)/shard_map/ppermute | solution.py:315
  27.6 4.5 %collective-permute-start.5 = (bf16[8,16,1024]{2,1,0:T(8,128)(2,1)S(1)}, bf16[8,16,1024]{2,1,0:T(8,128)(2,1)S(1)}, u32[]{:S(2)}, u32[]{:S(2)}) collective-permute-start(bf16[8,16,1024]{2,1,0:T(8,128)(2,1)S(1)} %get-tuple-element.56.up), channel_id=1, source_target_pairs={{0,4},{4,8},{8,12},{12,16},{16,20},{20,24},{24,28},{28,32},{32,36}... | collective-permute-start | bytes 786440 | tf_op jit(solution)/shard_map/ppermute | solution.py:321
  34.0 2.9 %collective-permute-start.7 = (bf16[4,16,1024]{2,1,0:T(8,128)(2,1)S(1)}, bf16[4,16,1024]{2,1,0:T(8,128)(2,1)S(1)}, u32[]{:S(2)}, u32[]{:S(2)}) collective-permute-start(bf16[4,16,1024]{2,1,0:T(8,128)(2,1)S(1)} %get-tuple-element.58), channel_id=1, source_target_pairs={{0,8},{4,12},{8,16},{12,20},{16,24},{20,28},{24,32},{28,36},{32,40... | collective-permute-start | bytes 393224 | tf_op jit(solution)/shard_map/ppermute | solution.py:321
  38.8 3.8 %collective-permute-done.8.far_high = bf16[4,16,1024]{2,1,0:T(8,128)(2,1)S(1)} collective-permute-done((bf16[4,16,1024]{2,1,0:T(8,128)(2,1)S(1)}, bf16[4,16,1024]{2,1,0:T(8,128)(2,1)S(1)}, u32[]{:S(2)}, u32[]{:S(2)}) %collective-permute-start.8) | collective-permute-done | bytes 131104 | tf_op jit(solution)/shard_map/ppermute | solution.py:321
  50.2 4.1 %shard_map.80 = (bf16[2,16,1024]{2,1,0:T(8,128)(2,1)S(1)}, bf16[2,16,1024]{2,1,0:T(8,128)(2,1)S(1)}, bf16[2,16,1024]{2,1,0:T(8,128)(2,1)S(1)}, bf16[2,16,1024]{2...) custom-call(s32[1]{0:T(128)} %bitcast.me_ref, s32[3,2,32]{2,1,0:T(2,128)S(1)} %bitcast.4, ...), custom_call_target="tpu_custom_call" | custom-call | flops 301989888 | bytes 7000000 | tf_op jit(solution)/shard_map/pallas_call | solution.py:366
  55.2 3.6 %collective-permute-start.13 = (bf16[2,16,1024]{2,1,0:T(8,128)(2,1)S(1)}, bf16[2,16,1024]{2,1,0:T(8,128)(2,1)S(1)}, u32[]{:S(2)}, u32[]{:S(2)}) collective-permute-start(bf16[2,16,1024]{2,1,0:T(8,128)(2,1)S(1)} %get-tuple-element.68), channel_id=1, source_target_pairs={{0,2},{1,3},{2,0},{3,1},{4,6},{5,7},{6,4},{7,5},{8,10},{9,11},{10,... | collective-permute-start | bytes 196616 | tf_op jit(solution)/shard_map/ppermute | solution.py:315
  62.3 7.9 %collective-permute-start.15 = (bf16[8,16,1024]{2,1,0:T(8,128)(2,1)S(1)}, bf16[8,16,1024]{2,1,0:T(8,128)(2,1)S(1)}, u32[]{:S(2)}, u32[]{:S(2)}) collective-permute-start(bf16[8,16,1024]{2,1,0:T(8,128)(2,1)S(1)} %get-tuple-element.71.up), channel_id=1, source_target_pairs={{0,4},{4,8},{8,12},{12,16},{16,20},{20,24},{24,28},{28,32},{32,36}... | collective-permute-start | bytes 786440 | tf_op jit(solution)/shard_map/ppermute | solution.py:321
  72.2 4.9 %collective-permute-start.17 = (bf16[4,16,1024]{2,1,0:T(8,128)(2,1)S(1)}, bf16[4,16,1024]{2,1,0:T(8,128)(2,1)S(1)}, u32[]{:S(2)}, u32[]{:S(2)}) collective-permute-start(bf16[4,16,1024]{2,1,0:T(8,128)(2,1)S(1)} %get-tuple-element.73), channel_id=1, source_target_pairs={{0,8},{4,12},{8,16},{12,20},{16,24},{20,28},{24,32},{28,36},{32,40... | collective-permute-start | bytes 393224 | tf_op jit(solution)/shard_map/ppermute | solution.py:321
  79.7 5.4 %collective-permute-done.18.far_high = bf16[4,16,1024]{2,1,0:T(8,128)(2,1)S(1)} collective-permute-done((bf16[4,16,1024]{2,1,0:T(8,128)(2,1)S(1)}, bf16[4,16,1024]{2,1,0:T(8,128)(2,1)S(1)}, u32[]{:S(2)}, u32[]{:S(2)}) %collective-permute-start.18) | collective-permute-done | bytes 131104 | tf_op jit(solution)/shard_map/ppermute | solution.py:321
  86.5 2.5 %collective-permute-start.20 = (f32[2,16,1024]{2,1,0:T(8,128)S(1)}, f32[2,16,1024]{2,1,0:T(8,128)S(1)}, u32[]{:S(2)}, u32[]{:S(2)}) collective-permute-start(f32[2,16,1024]{2,1,0:T(8,128)S(1)} %get-tuple-element.77), channel_id=1, source_target_pairs={{0,2},{1,3},{2,0},{3,1},{4,6},{5,7},{6,4},{7,5},{8,10},{9,11},{10,... | collective-permute-start | bytes 393224 | tf_op jit(solution)/shard_map/ppermute | solution.py:315
  89.2 2.7 %collective-permute-done.19.h1 = f32[2,16,1024]{2,1,0:T(8,128)S(1)} collective-permute-done((f32[2,16,1024]{2,1,0:T(8,128)S(1)}, f32[2,16,1024]{2,1,0:T(8,128)S(1)}, u32[]{:S(2)}, u32[]{:S(2)}) %collective-permute-start.19) | collective-permute-done | bytes 131104 | tf_op jit(solution)/shard_map/ppermute | solution.py:315
  91.9 3.3 %collective-permute-done.20.h2 = f32[2,16,1024]{2,1,0:T(8,128)S(1)} collective-permute-done((f32[2,16,1024]{2,1,0:T(8,128)S(1)}, f32[2,16,1024]{2,1,0:T(8,128)S(1)}, u32[]{:S(2)}, u32[]{:S(2)}) %collective-permute-start.20) | collective-permute-done | bytes 131104 | tf_op jit(solution)/shard_map/ppermute | solution.py:315
  95.8 4.8 %shard_map.83 = (f32[2,16,1024]{2,1,0:T(8,128)S(1)}, f32[2,16,1024]{2,1,0:T(8,128)S(1)}, f32[2,16,1024]{2,1,0:T(8,128)S(1)}, f32[2,16,1024]{2,1,0:T(8,128)S(1)},...) custom-call(s32[1]{0:T(128)} %bitcast.me_ref, s32[3,2,32]{2,1,0:T(2,128)S(1)} %bitcast.5, ...), custom_call_target="tpu_custom_call" | custom-call | flops 402653184 | bytes 9000000 | tf_op jit(solution)/shard_map/pallas_call | solution.py:376
  101.2 3.0 %collective-permute-start.26 = (f32[2,16,1024]{2,1,0:T(8,128)S(1)}, f32[2,16,1024]{2,1,0:T(8,128)S(1)}, u32[]{:S(2)}, u32[]{:S(2)}) collective-permute-start(f32[2,16,1024]{2,1,0:T(8,128)S(1)} %get-tuple-element.88), channel_id=1, source_target_pairs={{0,2},{1,3},{2,0},{3,1},{4,6},{5,7},{6,4},{7,5},{8,10},{9,11},{10,... | collective-permute-start | bytes 393224 | tf_op jit(solution)/shard_map/ppermute | solution.py:315
  104.2 21.9 %all-to-all-start = ((f32[256,1,128]{2,1,0:T(1,128)}), f32[256,1,128]{2,1,0:T(1,128)S(1)}, u32[]{:S(2)}, u32[]{:S(2)}) async-start(f32[256,1,128]{2,1,0:T(1,128)} %get-tuple-element.83), calls=%async_computation | async-start | bytes 262144 | tf_op jit(solution)/shard_map/all_to_all | solution.py:382
  127.0 3.5 %collective-permute-start.28 = (f32[4,16,1024]{2,1,0:T(8,128)}, f32[4,16,1024]{2,1,0:T(8,128)S(1)}, u32[]{:S(2)}, u32[]{:S(2)}) collective-permute-start(f32[4,16,1024]{2,1,0:T(8,128)} %get-tuple-element.91), channel_id=1, source_target_pairs={{0,4},{4,8},{8,12},{12,16},{16,20},{20,24},{24,28},{28,32},{32,36}... | collective-permute-start | bytes 786440 | tf_op jit(solution)/shard_map/ppermute | solution.py:321
  132.4 6.3 %all-to-all-done.sums = f32[256,1,128]{2,1,0:T(1,128)S(1)} async-done(((f32[256,1,128]{2,1,0:T(1,128)}), f32[256,1,128]{2,1,0:T(1,128)S(1)}, u32[]{:S(2)}, u32[]{:S(2)}) %all-to-all-start) | async-done | bytes 131104 | tf_op jit(solution)/shard_map/all_to_all | solution.py:382
  142.1 2.7 %collective-permute-start.32 = (bf16[4,16,1024]{2,1,0:T(8,128)(2,1)S(1)}, bf16[4,16,1024]{2,1,0:T(8,128)(2,1)S(1)}, u32[]{:S(2)}, u32[]{:S(2)}) collective-permute-start(bf16[4,16,1024]{2,1,0:T(8,128)(2,1)S(1)} %shard_map.88.s0), channel_id=1, source_target_pairs={{0,3},{1,0},{2,1},{3,2},{4,7},{5,4},{6,5},{7,6},{8,11},{9,8},{10,9... | collective-permute-start | bytes 393224 | tf_op jit(solution)/shard_map/ppermute | solution.py:315
  147.3 3.6 %collective-permute-done.22.s1 = bf16[4,16,1024]{2,1,0:T(8,128)(2,1)S(1)} collective-permute-done((bf16[4,16,1024]{2,1,0:T(8,128)(2,1)S(1)}, bf16[4,16,1024]{2,1,0:T(8,128)(2,1)S(1)}, u32[]{:S(2)}, u32[]{:S(2)}) %collective-permute-start.22) | collective-permute-done | bytes 131104 | tf_op jit(solution)/shard_map/ppermute | solution.py:315
  151.9 3.7 %collective-permute-done.30.s1 = bf16[4,16,1024]{2,1,0:T(8,128)(2,1)S(1)} collective-permute-done((bf16[4,16,1024]{2,1,0:T(8,128)(2,1)S(1)}, bf16[4,16,1024]{2,1,0:T(8,128)(2,1)S(1)}, u32[]{:S(2)}, u32[]{:S(2)}) %collective-permute-start.30) | collective-permute-done | bytes 131104 | tf_op jit(solution)/shard_map/ppermute | solution.py:315
  (70 shorter events, 43.6 us)
Async XLA Ops:
  2.6 6.5 %collective-permute-start = (f32[8,128]{1,0:T(8,128)S(1)}, f32[8,128]{1,0:T(8,128)S(1)}, u32[]{:S(2)}, u32[]{:S(2)}) collective-permute-start(f32[8,128]{1,0:T(8,128)S(1)} %get-tuple-element.48), channel_id=1, source_target_pairs={{0,4},{4,8},{8,12},{12,16},{16,20},{20,24},{24,28},{28,32},{32,36}... | collective-permute-start | bytes 12296 | tf_op jit(solution)/shard_map/ppermute | solution.py:321
  20.9 6.0 %collective-permute-start.3 = (bf16[2,16,1408]{2,1,0:T(8,128)(2,1)S(1)}, bf16[2,16,1408]{2,1,0:T(8,128)(2,1)S(1)}, u32[]{:S(2)}, u32[]{:S(2)}) collective-permute-start(bf16[2,16,1408]{2,1,0:T(8,128)(2,1)S(1)} %get-tuple-element.52), channel_id=1, source_target_pairs={{0,2},{1,3},{2,0},{3,1},{4,6},{5,7},{6,4},{7,5},{8,10},{9,11},{10,... | collective-permute-start | bytes 270344 | tf_op jit(solution)/shard_map/ppermute | solution.py:315
  27.6 15.0 %collective-permute-start.5 = (bf16[8,16,1024]{2,1,0:T(8,128)(2,1)S(1)}, bf16[8,16,1024]{2,1,0:T(8,128)(2,1)S(1)}, u32[]{:S(2)}, u32[]{:S(2)}) collective-permute-start(bf16[8,16,1024]{2,1,0:T(8,128)(2,1)S(1)} %get-tuple-element.56.up), channel_id=1, source_target_pairs={{0,4},{4,8},{8,12},{12,16},{16,20},{20,24},{24,28},{28,32},{32,36}... | collective-permute-start | bytes 786440 | tf_op jit(solution)/shard_map/ppermute | solution.py:321
  32.0 10.6 %collective-permute-start.6 = (bf16[8,16,1024]{2,1,0:T(8,128)(2,1)S(1)}, bf16[8,16,1024]{2,1,0:T(8,128)(2,1)S(1)}, u32[]{:S(2)}, u32[]{:S(2)}) collective-permute-start(bf16[8,16,1024]{2,1,0:T(8,128)(2,1)S(1)} %get-tuple-element.57.down), channel_id=1, source_target_pairs={{4,0},{8,4},{12,8},{16,12},{20,16},{24,20},{28,24},{32,28},{36,32}... | collective-permute-start | bytes 786440 | tf_op jit(solution)/shard_map/ppermute | solution.py:321
  55.2 5.9 %collective-permute-start.13 = (bf16[2,16,1024]{2,1,0:T(8,128)(2,1)S(1)}, bf16[2,16,1024]{2,1,0:T(8,128)(2,1)S(1)}, u32[]{:S(2)}, u32[]{:S(2)}) collective-permute-start(bf16[2,16,1024]{2,1,0:T(8,128)(2,1)S(1)} %get-tuple-element.68), channel_id=1, source_target_pairs={{0,2},{1,3},{2,0},{3,1},{4,6},{5,7},{6,4},{7,5},{8,10},{9,11},{10,... | collective-permute-start | bytes 196616 | tf_op jit(solution)/shard_map/ppermute | solution.py:315
  62.3 22.8 %collective-permute-start.15 = (bf16[8,16,1024]{2,1,0:T(8,128)(2,1)S(1)}, bf16[8,16,1024]{2,1,0:T(8,128)(2,1)S(1)}, u32[]{:S(2)}, u32[]{:S(2)}) collective-permute-start(bf16[8,16,1024]{2,1,0:T(8,128)(2,1)S(1)} %get-tuple-element.71.up), channel_id=1, source_target_pairs={{0,4},{4,8},{8,12},{12,16},{16,20},{20,24},{24,28},{28,32},{32,36}... | collective-permute-start | bytes 786440 | tf_op jit(solution)/shard_map/ppermute | solution.py:321
  70.2 14.9 %collective-permute-start.16 = (bf16[8,16,1024]{2,1,0:T(8,128)(2,1)S(1)}, bf16[8,16,1024]{2,1,0:T(8,128)(2,1)S(1)}, u32[]{:S(2)}, u32[]{:S(2)}) collective-permute-start(bf16[8,16,1024]{2,1,0:T(8,128)(2,1)S(1)} %get-tuple-element.72.down), channel_id=1, source_target_pairs={{4,0},{8,4},{12,8},{16,12},{20,16},{24,20},{28,24},{32,28},{36,32}... | collective-permute-start | bytes 786440 | tf_op jit(solution)/shard_map/ppermute | solution.py:321
  72.2 7.5 %collective-permute-start.17 = (bf16[4,16,1024]{2,1,0:T(8,128)(2,1)S(1)}, bf16[4,16,1024]{2,1,0:T(8,128)(2,1)S(1)}, u32[]{:S(2)}, u32[]{:S(2)}) collective-permute-start(bf16[4,16,1024]{2,1,0:T(8,128)(2,1)S(1)} %get-tuple-element.73), channel_id=1, source_target_pairs={{0,8},{4,12},{8,16},{12,20},{16,24},{20,28},{24,32},{28,36},{32,40... | collective-permute-start | bytes 393224 | tf_op jit(solution)/shard_map/ppermute | solution.py:321
  77.0 8.1 %collective-permute-start.18 = (bf16[4,16,1024]{2,1,0:T(8,128)(2,1)S(1)}, bf16[4,16,1024]{2,1,0:T(8,128)(2,1)S(1)}, u32[]{:S(2)}, u32[]{:S(2)}) collective-permute-start(bf16[4,16,1024]{2,1,0:T(8,128)(2,1)S(1)} %get-tuple-element.74), channel_id=1, source_target_pairs={{8,0},{12,4},{16,8},{20,12},{24,16},{28,20},{32,24},{36,28},{40,32... | collective-permute-start | bytes 393224 | tf_op jit(solution)/shard_map/ppermute | solution.py:321
  85.8 6.1 %collective-permute-start.19 = (f32[2,16,1024]{2,1,0:T(8,128)S(1)}, f32[2,16,1024]{2,1,0:T(8,128)S(1)}, u32[]{:S(2)}, u32[]{:S(2)}) collective-permute-start(f32[2,16,1024]{2,1,0:T(8,128)S(1)} %get-tuple-element.76), channel_id=1, source_target_pairs={{0,1},{1,2},{2,3},{3,0},{4,5},{5,6},{6,7},{7,4},{8,9},{9,10},{10,1... | collective-permute-start | bytes 393224 | tf_op jit(solution)/shard_map/ppermute | solution.py:315
  86.5 8.7 %collective-permute-start.20 = (f32[2,16,1024]{2,1,0:T(8,128)S(1)}, f32[2,16,1024]{2,1,0:T(8,128)S(1)}, u32[]{:S(2)}, u32[]{:S(2)}) collective-permute-start(f32[2,16,1024]{2,1,0:T(8,128)S(1)} %get-tuple-element.77), channel_id=1, source_target_pairs={{0,2},{1,3},{2,0},{3,1},{4,6},{5,7},{6,4},{7,5},{8,10},{9,11},{10,... | collective-permute-start | bytes 393224 | tf_op jit(solution)/shard_map/ppermute | solution.py:315
  89.0 6.8 %collective-permute-start.21 = (f32[2,16,1024]{2,1,0:T(8,128)S(1)}, f32[2,16,1024]{2,1,0:T(8,128)S(1)}, u32[]{:S(2)}, u32[]{:S(2)}) collective-permute-start(f32[2,16,1024]{2,1,0:T(8,128)S(1)} %get-tuple-element.78), channel_id=1, source_target_pairs={{0,3},{1,0},{2,1},{3,2},{4,7},{5,4},{6,5},{7,6},{8,11},{9,8},{10,9... | collective-permute-start | bytes 393224 | tf_op jit(solution)/shard_map/ppermute | solution.py:315
  100.6 25.5 %collective-permute-start.25 = (f32[2,16,1024]{2,1,0:T(8,128)S(1)}, f32[2,16,1024]{2,1,0:T(8,128)S(1)}, u32[]{:S(2)}, u32[]{:S(2)}) collective-permute-start(f32[2,16,1024]{2,1,0:T(8,128)S(1)} %get-tuple-element.87), channel_id=1, source_target_pairs={{0,1},{1,2},{2,3},{3,0},{4,5},{5,6},{6,7},{7,4},{8,9},{9,10},{10,1... | collective-permute-start | bytes 393224 | tf_op jit(solution)/shard_map/ppermute | solution.py:315
  101.2 24.9 %collective-permute-start.26 = (f32[2,16,1024]{2,1,0:T(8,128)S(1)}, f32[2,16,1024]{2,1,0:T(8,128)S(1)}, u32[]{:S(2)}, u32[]{:S(2)}) collective-permute-start(f32[2,16,1024]{2,1,0:T(8,128)S(1)} %get-tuple-element.88), channel_id=1, source_target_pairs={{0,2},{1,3},{2,0},{3,1},{4,6},{5,7},{6,4},{7,5},{8,10},{9,11},{10,... | collective-permute-start | bytes 393224 | tf_op jit(solution)/shard_map/ppermute | solution.py:315
  104.2 21.9 %collective-permute-start.27 = (f32[2,16,1024]{2,1,0:T(8,128)S(1)}, f32[2,16,1024]{2,1,0:T(8,128)S(1)}, u32[]{:S(2)}, u32[]{:S(2)}) collective-permute-start(f32[2,16,1024]{2,1,0:T(8,128)S(1)} %get-tuple-element.89), channel_id=1, source_target_pairs={{0,3},{1,0},{2,1},{3,2},{4,7},{5,4},{6,5},{7,6},{8,11},{9,8},{10,9... | collective-permute-start | bytes 393224 | tf_op jit(solution)/shard_map/ppermute | solution.py:315
  104.2 34.6 %all-to-all-start = ((f32[256,1,128]{2,1,0:T(1,128)}), f32[256,1,128]{2,1,0:T(1,128)S(1)}, u32[]{:S(2)}, u32[]{:S(2)}) async-start(f32[256,1,128]{2,1,0:T(1,128)} %get-tuple-element.83), calls=%async_computation | async-start | bytes 262144 | tf_op jit(solution)/shard_map/all_to_all | solution.py:382
  127.0 14.5 %collective-permute-start.28 = (f32[4,16,1024]{2,1,0:T(8,128)}, f32[4,16,1024]{2,1,0:T(8,128)S(1)}, u32[]{:S(2)}, u32[]{:S(2)}) collective-permute-start(f32[4,16,1024]{2,1,0:T(8,128)} %get-tuple-element.91), channel_id=1, source_target_pairs={{0,4},{4,8},{8,12},{12,16},{16,20},{20,24},{24,28},{28,32},{32,36}... | collective-permute-start | bytes 786440 | tf_op jit(solution)/shard_map/ppermute | solution.py:321
  130.5 11.0 %collective-permute-start.29 = (f32[4,16,1024]{2,1,0:T(8,128)S(1)}, f32[4,16,1024]{2,1,0:T(8,128)S(1)}, u32[]{:S(2)}, u32[]{:S(2)}) collective-permute-start(f32[4,16,1024]{2,1,0:T(8,128)S(1)} %get-tuple-element.92), channel_id=1, source_target_pairs={{4,0},{8,4},{12,8},{16,12},{20,16},{24,20},{28,24},{32,28},{36,32}... | collective-permute-start | bytes 786440 | tf_op jit(solution)/shard_map/ppermute | solution.py:321
  139.3 6.1 %collective-permute-start.24 = (bf16[4,16,1024]{2,1,0:T(8,128)(2,1)S(1)}, bf16[4,16,1024]{2,1,0:T(8,128)(2,1)S(1)}, u32[]{:S(2)}, u32[]{:S(2)}) collective-permute-start(bf16[4,16,1024]{2,1,0:T(8,128)(2,1)S(1)} %shard_map.84.s0), channel_id=1, source_target_pairs={{0,3},{1,0},{2,1},{3,2},{4,7},{5,4},{6,5},{7,6},{8,11},{9,8},{10,9... | collective-permute-start | bytes 393224 | tf_op jit(solution)/shard_map/ppermute | solution.py:315
  140.4 7.0 %collective-permute-start.23 = (bf16[4,16,1024]{2,1,0:T(8,128)(2,1)S(1)}, bf16[4,16,1024]{2,1,0:T(8,128)(2,1)S(1)}, u32[]{:S(2)}, u32[]{:S(2)}) collective-permute-start(bf16[4,16,1024]{2,1,0:T(8,128)(2,1)S(1)} %shard_map.84.s0), channel_id=1, source_target_pairs={{0,2},{1,3},{2,0},{3,1},{4,6},{5,7},{6,4},{7,5},{8,10},{9,11},{10,... | collective-permute-start | bytes 393224 | tf_op jit(solution)/shard_map/ppermute | solution.py:315
  141.5 9.4 %collective-permute-start.22 = (bf16[4,16,1024]{2,1,0:T(8,128)(2,1)S(1)}, bf16[4,16,1024]{2,1,0:T(8,128)(2,1)S(1)}, u32[]{:S(2)}, u32[]{:S(2)}) collective-permute-start(bf16[4,16,1024]{2,1,0:T(8,128)(2,1)S(1)} %shard_map.84.s0), channel_id=1, source_target_pairs={{0,1},{1,2},{2,3},{3,0},{4,5},{5,6},{6,7},{7,4},{8,9},{9,10},{10,1... | collective-permute-start | bytes 393224 | tf_op jit(solution)/shard_map/ppermute | solution.py:315
  142.1 9.9 %collective-permute-start.32 = (bf16[4,16,1024]{2,1,0:T(8,128)(2,1)S(1)}, bf16[4,16,1024]{2,1,0:T(8,128)(2,1)S(1)}, u32[]{:S(2)}, u32[]{:S(2)}) collective-permute-start(bf16[4,16,1024]{2,1,0:T(8,128)(2,1)S(1)} %shard_map.88.s0), channel_id=1, source_target_pairs={{0,3},{1,0},{2,1},{3,2},{4,7},{5,4},{6,5},{7,6},{8,11},{9,8},{10,9... | collective-permute-start | bytes 393224 | tf_op jit(solution)/shard_map/ppermute | solution.py:315
  144.8 7.1 %collective-permute-start.31 = (bf16[4,16,1024]{2,1,0:T(8,128)(2,1)S(1)}, bf16[4,16,1024]{2,1,0:T(8,128)(2,1)S(1)}, u32[]{:S(2)}, u32[]{:S(2)}) collective-permute-start(bf16[4,16,1024]{2,1,0:T(8,128)(2,1)S(1)} %shard_map.88.s0), channel_id=1, source_target_pairs={{0,2},{1,3},{2,0},{3,1},{4,6},{5,7},{6,4},{7,5},{8,10},{9,11},{10,... | collective-permute-start | bytes 393224 | tf_op jit(solution)/shard_map/ppermute | solution.py:315
  145.4 10.2 %collective-permute-start.30 = (bf16[4,16,1024]{2,1,0:T(8,128)(2,1)S(1)}, bf16[4,16,1024]{2,1,0:T(8,128)(2,1)S(1)}, u32[]{:S(2)}, u32[]{:S(2)}) collective-permute-start(bf16[4,16,1024]{2,1,0:T(8,128)(2,1)S(1)} %shard_map.88.s0), channel_id=1, source_target_pairs={{0,1},{1,2},{2,3},{3,0},{4,5},{5,6},{6,7},{7,4},{8,9},{9,10},{10,1... | collective-permute-start | bytes 393224 | tf_op jit(solution)/shard_map/ppermute | solution.py:315
  (16 other events, 133.6 us)

commit v2 on v1

--- a/solution.py
+++ b/solution.py
@@ -70,21 +70,23 @@
 
 def send_shares(me, acc, outs):
     for r in range(ANG):
-        quarter = lax.rem(me + r, ANG)
+        quarter = me ^ r
         share = acc[:, :, pl.ds(pl.multiple_of(quarter * Q, Q), Q)]
         outs[r][:, :, :Q] = share.astype(outs[r].dtype)
 
 
-def mask_kernel(rows, reach, above, below):
+def mask_kernel(me, rows, reach, inner, outer):
+    even = me[1] == 0
     for i in range(PAIR):
         for z in range(ZD):
             top = jnp.where(reach[i, 0, 1] == 1, rows[i, 0, 2, 0, z], 0.0)
             low = jnp.where(reach[i, 0, 0] == -1, rows[i, 0, 0, 0, z], 0.0)
-            above[ZD * i + z:ZD * i + z + 1] = jnp.full((1, 128), top, F32)
-            below[ZD * i + z:ZD * i + z + 1] = jnp.full((1, 128), low, F32)
-
-
-def back_kernel(me_ref, cols, rows, from_low, from_high, p_ref, w_hbm, o0, o1, o2, o3, w, acc, sem):
+            at = slice(ZD * i + z, ZD * i + z + 1)
+            inner[at] = jnp.full((1, 128), jnp.where(even, top, low), F32)
+            outer[at] = jnp.full((1, 128), jnp.where(even, low, top), F32)
+
+
+def back_kernel(me_ref, cols, rows, inner, outer, p_ref, w_hbm, o0, o1, o2, o3, w, acc, sem):
     copies = {}
     for a in range(PAIR):
         for g in range(UB // GROUP):
@@ -99,6 +101,9 @@
             back_block(a, block, p_ref[a, 0, :, 128 * block:128 * (block + 1)], cols, w, acc)
     outs = (o0, o1, o2, o3)
     send_shares(me_ref[0], acc, outs)
+    even = me_ref[1] == 0
+    from_low = jnp.where(even, outer[...], inner[...])
+    from_high = jnp.where(even, inner[...], outer[...])
     for i in range(PAIR):
         own = [jnp.full((1, 128), rows[i, 0, 1, 0, z], F32) for z in range(ZD)]
         rest = jnp.concatenate(
@@ -129,7 +134,7 @@
 
 def gather_shares(me, shares, place):
     for r in range(ANG):
-        quarter = lax.rem(me + ANG - r, ANG)
+        quarter = me ^ r
         place(pl.ds(pl.multiple_of(quarter * Q, Q), Q), shares[r])
 
 
@@ -184,89 +189,105 @@
     return [pl.ds(at * CH, CH) for at in range(Q // CH)]
 
 
-def combine_parts(coefs, parts, t1, up, down, up_far, down_far):
+def combine_parts(coefs, parts, mine, sent):
     for cut in cuts():
-        totals = spread_slices(coefs, parts, cut)
-        for z in range(ZD):
-            below, own, above = totals[z], totals[4 + z], totals[8 + z]
-            t1[z, :, cut] = own
-            up[z, :, cut] = own.astype(BF16)
-            down[z, :, cut] = own.astype(BF16)
-            up[4 + z, :, cut] = above.astype(BF16)
-            down[4 + z, :, cut] = below.astype(BF16)
-            up_far[z, :, cut] = above.astype(BF16)
-            down_far[z, :, cut] = below.astype(BF16)
-
-
-def open_kernel(c0, c1, c2, c3, t1, up, down, up_far, down_far, coefs):
+        for e, total in enumerate(spread_slices(coefs, parts, cut)):
+            mine[e, :, cut] = total
+            sent[e, :, cut] = total.astype(BF16)
+
+
+def open_kernel(c0, c1, c2, c3, mine, sent, coefs):
     parts = (c0, c1, c2, c3)
     for r in range(ANG):
         for i in range(PAIR):
             value = parts[r][i, :, Q:Q + 128].astype(F32)
             value = value + parts[r][i, :, Q + 128:Q + 256].astype(F32)
             coefs[r, i] = value + parts[r][i, :, Q + 256:].astype(F32)
-    combine_parts(coefs, parts, t1, up, down, up_far, down_far)
-
-
-def combine_kernel(coefs, c0, c1, c2, c3, t1, up, down, up_far, down_far):
-    combine_parts(coefs, (c0, c1, c2, c3), t1, up, down, up_far, down_far)
-
-
-def pieces_body(coefs, t1, up, down, from_low, from_high, far_low, far_high, g_out, outs, note):
-    for cut in cuts():
-        def get(ref, z):
-            return ref[z, :, cut].astype(F32)
-
-        cells = []
-        for z in range(ZD):
-            cells.append(get(from_low, z) + get(far_low, z) + get(down, 4 + z))
-        for z in range(ZD):
-            value = t1[z, :, cut] + get(from_low, 4 + z) + get(from_high, 4 + z)
-            g_out[z, :, cut] = value
-            note(z, cut, value)
-            cells.append(value)
-        for z in range(ZD):
-            cells.append(get(from_high, z) + get(far_high, z) + get(up, 4 + z))
-        for r in range(ANG):
-            for i in range(PAIR):
-                total = None
-                for e in range(12):
-                    term = coefs[(ANG - r) % ANG, i, e:e + 1, :] * cells[e]
-                    total = term if total is None else total + term
-                outs[r][i, :, cut] = total.astype(outs[r].dtype)
-
-
-def pieces_first(coefs, t1, up, down, from_low, from_high, far_low, far_high,
-                 g_out, h0, h1, h2, h3, dots):
-    kept = [jnp.zeros((8, 128), F32)]
-
-    def note(z, cut, value):
-        kept[0] = kept[0] + fold(value * value)
-
-    pieces_body(coefs, t1, up, down, from_low, from_high, far_low, far_high, g_out, (h0, h1, h2, h3), note)
-    dots[...] = kept[0]
-
-
-def pieces_second(coefs, g0, t1, up, down, from_low, from_high, far_low, far_high,
-                  g_out, h0, h1, h2, h3, dots):
-    kept = [jnp.zeros((8, 128), F32)] * 2
-
-    def note(z, cut, value):
-        kept[0] = kept[0] + fold(value * g0[z, :, cut])
-        kept[1] = kept[1] + fold(value * value)
-
-    pieces_body(coefs, t1, up, down, from_low, from_high, far_low, far_high, g_out, (h0, h1, h2, h3), note)
-    dots[:8] = kept[0]
-    dots[8:] = kept[1]
-
-
-def last_kernel(coefs, c0, c1, c2, c3, t1, up, down):
-    for cut in cuts():
-        totals = spread_slices(coefs, (c0, c1, c2, c3), cut)
-        for z in range(ZD):
-            down[z, :, cut] = totals[z].astype(down.dtype)
-            t1[z, :, cut] = totals[4 + z]
-            up[z, :, cut] = totals[8 + z].astype(up.dtype)
+    combine_parts(coefs, parts, mine, sent)
+
+
+def combine_kernel(coefs, c0, c1, c2, c3, mine, sent):
+    combine_parts(coefs, (c0, c1, c2, c3), mine, sent)
+
+
+def edge_kernel(me, mine, other, sent):
+    for parity, outer, facing in ((0, 0, 0), (1, 8, 8)):
+        @pl.when(me[1] == parity)
+        def _(outer=outer, facing=facing):
+            for z in range(ZD):
+                sent[z] = (mine[4 + z] + other[facing + z].astype(F32)).astype(BF16)
+                sent[ZD + z] = mine[outer + z].astype(BF16)
+
+
+def pieces_body(me, coefs, mine, other, outer, inner, g_out, outs, begin, note, end):
+    def get(ref, z, cut):
+        return ref[z, :, cut].astype(F32)
+
+    def even_cells(cut):
+        below = [mine[z, :, cut] + get(outer, z, cut) for z in range(ZD)]
+        own = [mine[4 + z, :, cut] + get(other, z, cut) + get(outer, 4 + z, cut) for z in range(ZD)]
+        above = [mine[8 + z, :, cut] + get(other, 4 + z, cut) + get(inner, 4 + z, cut) for z in range(ZD)]
+        return below, own, above
+
+    def odd_cells(cut):
+        below = [mine[z, :, cut] + get(other, 4 + z, cut) + get(inner, 4 + z, cut) for z in range(ZD)]
+        own = [mine[4 + z, :, cut] + get(other, 8 + z, cut) + get(outer, 4 + z, cut) for z in range(ZD)]
+        above = [mine[8 + z, :, cut] + get(outer, z, cut) for z in range(ZD)]
+        return below, own, above
+
+    for parity, cells_of in ((0, even_cells), (1, odd_cells)):
+        @pl.when(me[1] == parity)
+        def _(cells_of=cells_of):
+            kept = begin()
+            for cut in cuts():
+                below, own, above = cells_of(cut)
+                for z in range(ZD):
+                    g_out[z, :, cut] = own[z]
+                    kept = note(kept, z, cut, own[z])
+                cells = below + own + above
+                for r in range(ANG):
+                    for i in range(PAIR):
+                        total = None
+                        for e in range(12):
+                            term = coefs[r, i, e:e + 1, :] * cells[e]
+                            total = term if total is None else total + term
+                        outs[r][i, :, cut] = total.astype(outs[r].dtype)
+            end(kept)
+
+
+def pieces_first(me, coefs, mine, other, outer, inner, g_out, h0, h1, h2, h3, dots):
+    def note(kept, z, cut, value):
+        return kept + fold(value * value)
+
+    def end(kept):
+        dots[...] = kept
+
+    pieces_body(me, coefs, mine, other, outer, inner, g_out, (h0, h1, h2, h3),
+                lambda: jnp.zeros((8, 128), F32), note, end)
+
+
+def pieces_second(me, coefs, g0, mine, other, outer, inner, g_out, h0, h1, h2, h3, dots):
+    def note(kept, z, cut, value):
+        return kept[0] + fold(value * g0[z, :, cut]), kept[1] + fold(value * value)
+
+    def end(kept):
+        dots[:8] = kept[0]
+        dots[8:] = kept[1]
+
+    pieces_body(me, coefs, mine, other, outer, inner, g_out, (h0, h1, h2, h3),
+                lambda: (jnp.zeros((8, 128), F32),) * 2, note, end)
+
+
+def last_kernel(me, coefs, c0, c1, c2, c3, own, inner, outer):
+    for parity, far, near in ((0, 0, 8), (1, 8, 0)):
+        @pl.when(me[1] == parity)
+        def _(far=far, near=near):
+            for cut in cuts():
+                totals = spread_slices(coefs, (c0, c1, c2, c3), cut)
+                for z in range(ZD):
+                    outer[z, :, cut] = totals[far + z]
+                    own[z, :, cut] = totals[4 + z]
+                    inner[z, :, cut] = totals[near + z]
 
 
 def steps(sums_ref):
@@ -291,10 +312,10 @@
         out[z] = (one * g0[z] - two * z0[z]).astype(BF16)
 
 
-def gradient_kernel(sums, t1, from_low, from_high, g0, z0, out):
+def gradient_kernel(sums, t1, inner, outer, g0, z0, out):
     one, two = steps(sums)
     for z in range(ZD):
-        last = t1[z] + from_low[z].astype(F32) + from_high[z].astype(F32)
+        last = t1[z] + inner[z] + outer[z]
         out[z] = (g0[z] - one * z0[z] + two * last).astype(BF16)
 
 
@@ -311,14 +332,19 @@
     gather_shares(me_ref[0], (s0, s1, s2, s3), place)
 
 
-def along_ang(value, steps):
-    return lax.ppermute(value, "ang", [(i, (i + steps) % ANG) for i in range(ANG)])
-
-
-def along_slab(value, steps):
+def along_ang(value, other):
+    return lax.ppermute(value, "ang", [(i, i ^ other) for i in range(ANG)])
+
+
+def on_chip(value):
+    return lax.ppermute(value, "slab", [(i, i ^ 1) for i in range(lax.axis_size("slab"))])
+
+
+def across(value):
     count = lax.axis_size("slab")
-    pairs = [(i, i + steps) for i in range(count) if 0 <= i + steps < count]
-    return lax.ppermute(value, "slab", pairs)
+    return lax.ppermute(
+        value, "slab", [pair for i in range(1, count - 1, 2) for pair in ((i, i + 1), (i + 1, i))]
+    )
 
 
 def exchange(shares):
@@ -329,11 +355,12 @@
 
 
 def per_device(projections, weights, columns, row_weights, reach):
+    me = jnp.stack([lax.axis_index("ang"), lax.axis_index("slab") % 2]).astype(jnp.int32)
     row = sds((PAIR * ZD, 128), F32)
-    above, below = call(mask_kernel, [row] * 2, [SMEM] * 2)(row_weights, reach)
-    edges = (along_slab(above, 1), along_slab(below, -1))
-
-    me = lax.axis_index("ang").astype(jnp.int32).reshape(1)
+    inner, outer = call(mask_kernel, [row] * 2, [SMEM] * 3)(me, row_weights, reach)
+    outer = across(outer)
+    edges = (on_chip(inner), outer)
+
     cols = columns.transpose(2, 0, 1)
 
     def share(dtype, more=0):
@@ -342,14 +369,15 @@
     full = sds((PAIR, L, X), F32)
     part = sds((ZD, L, Q), F32)
     part_b = sds((ZD, L, Q), BF16)
-    two_b = sds((2 * ZD, L, Q), BF16)
     acc = pltpu.VMEM((PAIR, L, X), F32)
     macs = 2 * PAIR * L * UB * 384 * 128
-    sent = [part, two_b, two_b, part_b, part_b]
-
-    def halo(t1, up, down, up_far, down_far):
-        return (t1, up, down, along_slab(up, 1), along_slab(down, -1),
-                along_slab(up_far, 2), along_slab(down_far, -2))
+    sent = [sds((3 * ZD, L, Q), F32), sds((3 * ZD, L, Q), BF16)]
+
+    def halo(mine, sent):
+        other = on_chip(sent)
+        (edge,) = call(edge_kernel, [sds((2 * ZD, L, Q), BF16)], [SMEM] + [VMEM] * 2)(me, mine, other)
+        outer = across(edge)
+        return mine, other, outer, on_chip(outer)
 
     *shares, w = call(
         back_kernel, [share(BF16, COEF)] * 4 + [sds((PAIR, UB, 384, 128), BF16)],
@@ -360,8 +388,8 @@
         open_kernel, sent + [sds((ANG, PAIR, L, 128), F32)], [VMEM] * 4, flops=10_000_000
     )(*exchange(shares))
     g0, *shares, gamma = call(
-        pieces_first, [part] + [share(BF16)] * 4 + [sds((8, 128), F32)], [VMEM] * 8, flops=10_000_000
-    )(coefs, *halo(*spread))
+        pieces_first, [part] + [share(BF16)] * 4 + [sds((8, 128), F32)], [SMEM] + [VMEM] * 5, flops=10_000_000
+    )(me, coefs, *halo(*spread))
 
     *shares, q0, curve = call(
         first_kernel, [share(MID)] * 4 + [full, sds((8, 128), F32)],
@@ -370,8 +398,8 @@
     )(me, cols, *exchange(shares), w)
     spread = call(combine_kernel, sent, [VMEM] * 5, flops=10_000_000)(coefs, *exchange(shares))
     z0, *shares, inner = call(
-        pieces_second, [part] + [share(F32)] * 4 + [sds((16, 128), F32)], [VMEM] * 9, flops=10_000_000
-    )(coefs, g0, *halo(*spread))
+        pieces_second, [part] + [share(F32)] * 4 + [sds((16, 128), F32)], [SMEM] + [VMEM] * 6, flops=10_000_000
+    )(me, coefs, g0, *halo(*spread))
 
     *shares, w0, sums = call(
         second_kernel, [share(F32)] * 4 + [full, sds((lax.axis_size("slab") * ANG, 1, 128), F32)],
@@ -383,10 +411,9 @@
     (volume,) = call(volume_kernel, [part_b], [VMEM] * 3)(sums, g0, z0)
     (residual,) = call(residual_kernel, [sds(projections.shape, F32)], [VMEM] * 4)(sums, projections, q0, w0)
     volume = exchange((volume,) * 4)
-    t1, up, down = call(last_kernel, [part] * 3, [VMEM] * 5, flops=10_000_000)(coefs, *shares)
-    (gradient,) = call(gradient_kernel, [part_b], [VMEM] * 6)(
-        sums, t1, along_slab(up, 1), along_slab(down, -1), g0, z0
-    )
+    t1, inner, outer = call(last_kernel, [part] * 3, [SMEM] + [VMEM] * 5, flops=10_000_000)(me, coefs, *shares)
+    outer = across(outer)
+    (gradient,) = call(gradient_kernel, [part_b], [VMEM] * 6)(sums, t1, on_chip(inner), outer, g0, z0)
     whole = [sds((ZD, L, X), F32)]
     (volume,) = call(place_kernel, whole, [SMEM] + [VMEM] * 4)(me, *volume)
     (gradient,) = call(place_kernel, whole, [SMEM] + [VMEM] * 4)(me, *exchange((gradient,) * 4))

time: 157 us -> 146 us (0.930)
  starting transfers between devices: 88.3 us -> 68.9 us
  Pallas kernels: 22.2 us -> 26.4 us
  waiting for transfers between devices: 41.5 us -> 45.6 us
    ppermute x33 -> x31, starting transfers between devices: 66.4 us -> 47.1 us  [the longest x21 25.2 us: along_ang(): return lax.ppermute(value, 'ang', [(i, i ^ other) for i in range(ANG)])]
    ppermute x33 -> x31, waiting for transfers between devices: 35.1 us -> 38.7 us  [the longest x21 21.5 us: along_ang(): return lax.ppermute(value, 'ang', [(i, i ^ other) for i in range(ANG)])]
    pallas_call x4 -> x6, Pallas kernels: 2.78 us -> 5.81 us  [the longest x1 1.64 us: per_device(): call(last_kernel, [part] * 3, [SMEM] + [VMEM] * 5, flops=10000000)]
  transfers between devices with their start and end apart: 34 -> 32, of which waited for: 19 -> 20; matrix products, arithmetic and copies ran while one was open for 0% -> 0% of each run, Pallas kernels for 3% -> 4%
where the time goes in v2:
time: 146 us
  starting transfers between devices  68.9 us (47%)
  waiting for transfers between devices  45.6 us (31%)
  Pallas kernels  26.4 us (18%)
  local copies, waits for them, and re-layouts  3.78 us (3%)
    ppermute x21, starting transfers between devices, along_ang(): return lax.ppermute(value, 'ang', [(i, i ^ other) for i in range(ANG)])  25.2 us
    all_to_all x1, starting transfers between devices, per_device(): sums = lax.all_to_all(sums, ('slab', 'ang'), 0, 0, tiled=True)  21.8 us
    ppermute x21, waiting for transfers between devices, along_ang(): return lax.ppermute(value, 'ang', [(i, i ^ other) for i in range(ANG)])  21.5 us
    ppermute x4, starting transfers between devices, across(): lax.ppermute(value, 'slab', [pair for i in range(1, count - 1, 2) for pai...  13.5 us
    ppermute x4, waiting for transfers between devices, across(): lax.ppermute(value, 'slab', [pair for i in range(1, count - 1, 2) for pai...  11.1 us
    ppermute x6, starting transfers between devices, on_chip(): lax.ppermute(value, 'slab', [(i, i ^ 1) for i in range(lax.axis_size('sla...  8.39 us
    all_to_all x1, waiting for transfers between devices, per_device(): sums = lax.all_to_all(sums, ('slab', 'ang'), 0, 0, tiled=True)  6.92 us
    ppermute x6, waiting for transfers between devices, on_chip(): lax.ppermute(value, 'slab', [(i, i ^ 1) for i in range(lax.axis_size('sla...  6.13 us
  transfers between devices with their start and end apart: 32, of which 20 were waited for; matrix products, arithmetic and copies ran while one was open for 0% of the time, Pallas kernels for 4%

profile of v2, /device:TPU:1, one launch (start us, length us, event | category | flops | bytes accessed | tf_op | source)
XLA Modules:
  0.0 145.6 jit_solution(17125442331238420483)
XLA Ops:
  2.7 3.3 %collective-permute-start = (f32[8,128]{1,0:T(8,128)S(1)}, f32[8,128]{1,0:T(8,128)S(1)}, u32[]{:S(2)}, u32[]{:S(2)}) collective-permute-start(f32[8,128]{1,0:T(8,128)S(1)} %get-tuple-element.42), channel_id=1, source_target_pairs={{0,4},{4,0},{8,12},{12,8},{16,20},{20,16},{24,28},{28,24},{32,36},... | collective-permute-start | bytes 12296 | tf_op jit(solution)/shard_map/ppermute | solution.py:340
  6.0 1.9 %collective-permute-start.1 = (f32[8,128]{1,0:T(8,128)S(1)}, f32[8,128]{1,0:T(8,128)S(1)}, u32[]{:S(2)}, u32[]{:S(2)}) collective-permute-start(f32[8,128]{1,0:T(8,128)S(1)} %get-tuple-element.43), channel_id=1, source_target_pairs={{4,8},{8,4},{12,16},{16,12},{20,24},{24,20},{28,32},{32,28},{36,40... | collective-permute-start | bytes 12296 | tf_op jit(solution)/shard_map/ppermute | solution.py:345
  8.0 3.0 %collective-permute-done.1.outer = f32[8,128]{1,0:T(8,128)S(1)} collective-permute-done((f32[8,128]{1,0:T(8,128)S(1)}, f32[8,128]{1,0:T(8,128)S(1)}, u32[]{:S(2)}, u32[]{:S(2)}) %collective-permute-start.1) | collective-permute-done | bytes 4128 | tf_op jit(solution)/shard_map/ppermute | solution.py:345
  13.4 5.1 %shard_map.77 = (bf16[2,16,1408]{2,1,0:T(8,128)(2,1)S(1)}, bf16[2,16,1408]{2,1,0:T(8,128)(2,1)S(1)}, bf16[2,16,1408]{2,1,0:T(8,128)(2,1)S(1)}, bf16[2,16,1408]{2...) custom-call(s32[2]{0:T(128)S(1)} %pad_add_fusion.me.me_ref, s32[3,2,32]{2,1,0:T(2,128)S(1)} %bitcast.4, ...), custom_call_target="tpu_custom_call" | custom-call | flops 201326592 | bytes 7000000 | tf_op jit(solution)/shard_map/pallas_call | solution.py:382
  18.6 2.2 %collective-permute-start.3 = (bf16[2,16,1408]{2,1,0:T(8,128)(2,1)S(1)}, bf16[2,16,1408]{2,1,0:T(8,128)(2,1)S(1)}, u32[]{:S(2)}, u32[]{:S(2)}) collective-permute-start(bf16[2,16,1408]{2,1,0:T(8,128)(2,1)S(1)} %get-tuple-element.46), channel_id=1, source_target_pairs={{0,2},{1,3},{2,0},{3,1},{4,6},{5,7},{6,4},{7,5},{8,10},{9,11},{10,... | collective-permute-start | bytes 270344 | tf_op jit(solution)/shard_map/ppermute | solution.py:336
  28.3 5.8 %collective-permute-start.6 = (bf16[8,16,1024]{2,1,0:T(8,128)(2,1)S(1)}, bf16[8,16,1024]{2,1,0:T(8,128)(2,1)S(1)}, u32[]{:S(2)}, u32[]{:S(2)}) collective-permute-start(bf16[8,16,1024]{2,1,0:T(8,128)(2,1)S(1)} %shard_map.79), channel_id=1, source_target_pairs={{4,8},{8,4},{12,16},{16,12},{20,24},{24,20},{28,32},{32,28},{36,40... | collective-permute-start | bytes 786440 | tf_op jit(solution)/shard_map/ppermute | solution.py:345
  34.1 4.0 %collective-permute-done.6.outer = bf16[8,16,1024]{2,1,0:T(8,128)(2,1)S(1)} collective-permute-done((bf16[8,16,1024]{2,1,0:T(8,128)(2,1)S(1)}, bf16[8,16,1024]{2,1,0:T(8,128)(2,1)S(1)}, u32[]{:S(2)}, u32[]{:S(2)}) %collective-permute-start.6) | collective-permute-done | bytes 262176 | tf_op jit(solution)/shard_map/ppermute | solution.py:345
  42.5 2.4 %collective-permute-start.10 = (bf16[2,16,1024]{2,1,0:T(8,128)(2,1)S(1)}, bf16[2,16,1024]{2,1,0:T(8,128)(2,1)S(1)}, u32[]{:S(2)}, u32[]{:S(2)}) collective-permute-start(bf16[2,16,1024]{2,1,0:T(8,128)(2,1)S(1)} %get-tuple-element.55), channel_id=1, source_target_pairs={{0,3},{1,2},{2,1},{3,0},{4,7},{5,6},{6,5},{7,4},{8,11},{9,10},{10,... | collective-permute-start | bytes 196616 | tf_op jit(solution)/shard_map/ppermute | solution.py:336
  47.1 4.1 %shard_map.81 = (bf16[2,16,1024]{2,1,0:T(8,128)(2,1)S(1)}, bf16[2,16,1024]{2,1,0:T(8,128)(2,1)S(1)}, bf16[2,16,1024]{2,1,0:T(8,128)(2,1)S(1)}, bf16[2,16,1024]{2...) custom-call(s32[2]{0:T(128)S(1)} %pad_add_fusion.me.me_ref, s32[3,2,32]{2,1,0:T(2,128)S(1)} %bitcast.5, ...), custom_call_target="tpu_custom_call" | custom-call | flops 301989888 | bytes 7000000 | tf_op jit(solution)/shard_map/pallas_call | solution.py:394
  51.3 3.3 %collective-permute-start.12 = (bf16[2,16,1024]{2,1,0:T(8,128)(2,1)S(1)}, bf16[2,16,1024]{2,1,0:T(8,128)(2,1)S(1)}, u32[]{:S(2)}, u32[]{:S(2)}) collective-permute-start(bf16[2,16,1024]{2,1,0:T(8,128)(2,1)S(1)} %get-tuple-element.59), channel_id=1, source_target_pairs={{0,2},{1,3},{2,0},{3,1},{4,6},{5,7},{6,4},{7,5},{8,10},{9,11},{10,... | collective-permute-start | bytes 196616 | tf_op jit(solution)/shard_map/ppermute | solution.py:336
  57.0 2.7 %collective-permute-done.13.c3 = bf16[2,16,1024]{2,1,0:T(8,128)(2,1)S(1)} collective-permute-done((bf16[2,16,1024]{2,1,0:T(8,128)(2,1)S(1)}, bf16[2,16,1024]{2,1,0:T(8,128)(2,1)S(1)}, u32[]{:S(2)}, u32[]{:S(2)}) %collective-permute-start.13) | collective-permute-done | bytes 65568 | tf_op jit(solution)/shard_map/ppermute | solution.py:336
  60.1 2.8 %collective-permute-start.14 = (bf16[12,16,1024]{2,1,0:T(8,128)(2,1)S(1)}, bf16[12,16,1024]{2,1,0:T(8,128)(2,1)S(1)}, u32[]{:S(2)}, u32[]{:S(2)}) collective-permute-start(bf16[12,16,1024]{2,1,0:T(8,128)(2,1)S(1)} %get-tuple-element.62), channel_id=1, source_target_pairs={{0,4},{4,0},{8,12},{12,8},{16,20},{20,16},{24,28},{28,24},{32,36},... | collective-permute-start | bytes 1179656 | tf_op jit(solution)/shard_map/ppermute | solution.py:340
  64.9 3.9 %collective-permute-start.15 = (bf16[8,16,1024]{2,1,0:T(8,128)(2,1)S(1)}, bf16[8,16,1024]{2,1,0:T(8,128)(2,1)S(1)}, u32[]{:S(2)}, u32[]{:S(2)}) collective-permute-start(bf16[8,16,1024]{2,1,0:T(8,128)(2,1)S(1)} %shard_map.83), channel_id=1, source_target_pairs={{4,8},{8,4},{12,16},{16,12},{20,24},{24,20},{28,32},{32,28},{36,40... | collective-permute-start | bytes 786440 | tf_op jit(solution)/shard_map/ppermute | solution.py:345
  68.8 4.0 %collective-permute-done.15.outer = bf16[8,16,1024]{2,1,0:T(8,128)(2,1)S(1)} collective-permute-done((bf16[8,16,1024]{2,1,0:T(8,128)(2,1)S(1)}, bf16[8,16,1024]{2,1,0:T(8,128)(2,1)S(1)}, u32[]{:S(2)}, u32[]{:S(2)}) %collective-permute-start.15) | collective-permute-done | bytes 262176 | tf_op jit(solution)/shard_map/ppermute | solution.py:345
  77.1 2.4 %collective-permute-start.19 = (f32[2,16,1024]{2,1,0:T(8,128)S(1)}, f32[2,16,1024]{2,1,0:T(8,128)S(1)}, u32[]{:S(2)}, u32[]{:S(2)}) collective-permute-start(f32[2,16,1024]{2,1,0:T(8,128)S(1)} %get-tuple-element.66), channel_id=1, source_target_pairs={{0,3},{1,2},{2,1},{3,0},{4,7},{5,6},{6,5},{7,4},{8,11},{9,10},{10,... | collective-permute-start | bytes 393224 | tf_op jit(solution)/shard_map/ppermute | solution.py:336
  80.6 2.9 %collective-permute-done.18.h2 = f32[2,16,1024]{2,1,0:T(8,128)S(1)} collective-permute-done((f32[2,16,1024]{2,1,0:T(8,128)S(1)}, f32[2,16,1024]{2,1,0:T(8,128)S(1)}, u32[]{:S(2)}, u32[]{:S(2)}) %collective-permute-start.18) | collective-permute-done | bytes 131104 | tf_op jit(solution)/shard_map/ppermute | solution.py:336
  83.5 2.5 %collective-permute-done.19.h3 = f32[2,16,1024]{2,1,0:T(8,128)S(1)} collective-permute-done((f32[2,16,1024]{2,1,0:T(8,128)S(1)}, f32[2,16,1024]{2,1,0:T(8,128)S(1)}, u32[]{:S(2)}, u32[]{:S(2)}) %collective-permute-start.19) | collective-permute-done | bytes 131104 | tf_op jit(solution)/shard_map/ppermute | solution.py:336
  86.0 4.8 %shard_map.85 = (f32[2,16,1024]{2,1,0:T(8,128)S(1)}, f32[2,16,1024]{2,1,0:T(8,128)S(1)}, f32[2,16,1024]{2,1,0:T(8,128)S(1)}, f32[2,16,1024]{2,1,0:T(8,128)S(1)},...) custom-call(s32[2]{0:T(128)S(1)} %pad_add_fusion.me.me_ref, s32[3,2,32]{2,1,0:T(2,128)S(1)} %bitcast.6, ...), custom_call_target="tpu_custom_call" | custom-call | flops 402653184 | bytes 9000000 | tf_op jit(solution)/shard_map/pallas_call | solution.py:404
  90.8 3.5 %collective-permute-start.24 = (f32[2,16,1024]{2,1,0:T(8,128)S(1)}, f32[2,16,1024]{2,1,0:T(8,128)S(1)}, u32[]{:S(2)}, u32[]{:S(2)}) collective-permute-start(f32[2,16,1024]{2,1,0:T(8,128)S(1)} %get-tuple-element.76), channel_id=1, source_target_pairs={{0,2},{1,3},{2,0},{3,1},{4,6},{5,7},{6,4},{7,5},{8,10},{9,11},{10,... | collective-permute-start | bytes 393224 | tf_op jit(solution)/shard_map/ppermute | solution.py:336
  94.6 21.8 %all-to-all-start = ((f32[256,1,128]{2,1,0:T(1,128)}), f32[256,1,128]{2,1,0:T(1,128)S(1)}, u32[]{:S(2)}, u32[]{:S(2)}) async-start(f32[256,1,128]{2,1,0:T(1,128)} %get-tuple-element.71), calls=%async_computation | async-start | bytes 262144 | tf_op jit(solution)/shard_map/all_to_all | solution.py:410
  118.1 2.1 %collective-permute-start.26 = (f32[4,16,1024]{2,1,0:T(8,128)}, f32[4,16,1024]{2,1,0:T(8,128)S(1)}, u32[]{:S(2)}, u32[]{:S(2)}) collective-permute-start(f32[4,16,1024]{2,1,0:T(8,128)} %get-tuple-element.79), channel_id=1, source_target_pairs={{0,4},{4,0},{8,12},{12,8},{16,20},{20,16},{24,28},{28,24},{32,36},... | collective-permute-start | bytes 786440 | tf_op jit(solution)/shard_map/ppermute | solution.py:340
  120.3 1.9 %collective-permute-start.27 = (f32[4,16,1024]{2,1,0:T(8,128)S(1)}, f32[4,16,1024]{2,1,0:T(8,128)S(1)}, u32[]{:S(2)}, u32[]{:S(2)}) collective-permute-start(f32[4,16,1024]{2,1,0:T(8,128)S(1)} %get-tuple-element.80), channel_id=1, source_target_pairs={{4,8},{8,4},{12,16},{16,12},{20,24},{24,20},{28,32},{32,28},{36,40... | collective-permute-start | bytes 786440 | tf_op jit(solution)/shard_map/ppermute | solution.py:345
  122.2 6.9 %all-to-all-done.sums = f32[256,1,128]{2,1,0:T(1,128)S(1)} async-done(((f32[256,1,128]{2,1,0:T(1,128)}), f32[256,1,128]{2,1,0:T(1,128)S(1)}, u32[]{:S(2)}, u32[]{:S(2)}) %all-to-all-start) | async-done | bytes 131104 | tf_op jit(solution)/shard_map/all_to_all | solution.py:410
  140.1 3.2 %collective-permute-done.30.s3 = bf16[4,16,1024]{2,1,0:T(8,128)(2,1)S(1)} collective-permute-done((bf16[4,16,1024]{2,1,0:T(8,128)(2,1)S(1)}, bf16[4,16,1024]{2,1,0:T(8,128)(2,1)S(1)}, u32[]{:S(2)}, u32[]{:S(2)}) %collective-permute-start.30) | collective-permute-done | bytes 131104 | tf_op jit(solution)/shard_map/ppermute | solution.py:336
  (69 shorter events, 44.2 us)
Async XLA Ops:
  2.7 5.2 %collective-permute-start = (f32[8,128]{1,0:T(8,128)S(1)}, f32[8,128]{1,0:T(8,128)S(1)}, u32[]{:S(2)}, u32[]{:S(2)}) collective-permute-start(f32[8,128]{1,0:T(8,128)S(1)} %get-tuple-element.42), channel_id=1, source_target_pairs={{0,4},{4,0},{8,12},{12,8},{16,20},{20,16},{24,28},{28,24},{32,36},... | collective-permute-start | bytes 12296 | tf_op jit(solution)/shard_map/ppermute | solution.py:340
  6.0 4.9 %collective-permute-start.1 = (f32[8,128]{1,0:T(8,128)S(1)}, f32[8,128]{1,0:T(8,128)S(1)}, u32[]{:S(2)}, u32[]{:S(2)}) collective-permute-start(f32[8,128]{1,0:T(8,128)S(1)} %get-tuple-element.43), channel_id=1, source_target_pairs={{4,8},{8,4},{12,16},{16,12},{20,24},{24,20},{28,32},{32,28},{36,40... | collective-permute-start | bytes 12296 | tf_op jit(solution)/shard_map/ppermute | solution.py:345
  18.6 5.0 %collective-permute-start.3 = (bf16[2,16,1408]{2,1,0:T(8,128)(2,1)S(1)}, bf16[2,16,1408]{2,1,0:T(8,128)(2,1)S(1)}, u32[]{:S(2)}, u32[]{:S(2)}) collective-permute-start(bf16[2,16,1408]{2,1,0:T(8,128)(2,1)S(1)} %get-tuple-element.46), channel_id=1, source_target_pairs={{0,2},{1,3},{2,0},{3,1},{4,6},{5,7},{6,4},{7,5},{8,10},{9,11},{10,... | collective-permute-start | bytes 270344 | tf_op jit(solution)/shard_map/ppermute | solution.py:336
  28.3 9.9 %collective-permute-start.6 = (bf16[8,16,1024]{2,1,0:T(8,128)(2,1)S(1)}, bf16[8,16,1024]{2,1,0:T(8,128)(2,1)S(1)}, u32[]{:S(2)}, u32[]{:S(2)}) collective-permute-start(bf16[8,16,1024]{2,1,0:T(8,128)(2,1)S(1)} %shard_map.79), channel_id=1, source_target_pairs={{4,8},{8,4},{12,16},{16,12},{20,24},{24,20},{28,32},{32,28},{36,40... | collective-permute-start | bytes 786440 | tf_op jit(solution)/shard_map/ppermute | solution.py:345
  41.0 5.2 %collective-permute-start.9 = (bf16[2,16,1024]{2,1,0:T(8,128)(2,1)S(1)}, bf16[2,16,1024]{2,1,0:T(8,128)(2,1)S(1)}, u32[]{:S(2)}, u32[]{:S(2)}) collective-permute-start(bf16[2,16,1024]{2,1,0:T(8,128)(2,1)S(1)} %get-tuple-element.54), channel_id=1, source_target_pairs={{0,2},{1,3},{2,0},{3,1},{4,6},{5,7},{6,4},{7,5},{8,10},{9,11},{10,... | collective-permute-start | bytes 196616 | tf_op jit(solution)/shard_map/ppermute | solution.py:336
  42.5 4.6 %collective-permute-start.10 = (bf16[2,16,1024]{2,1,0:T(8,128)(2,1)S(1)}, bf16[2,16,1024]{2,1,0:T(8,128)(2,1)S(1)}, u32[]{:S(2)}, u32[]{:S(2)}) collective-permute-start(bf16[2,16,1024]{2,1,0:T(8,128)(2,1)S(1)} %get-tuple-element.55), channel_id=1, source_target_pairs={{0,3},{1,2},{2,1},{3,0},{4,7},{5,6},{6,5},{7,4},{8,11},{9,10},{10,... | collective-permute-start | bytes 196616 | tf_op jit(solution)/shard_map/ppermute | solution.py:336
  51.3 5.7 %collective-permute-start.12 = (bf16[2,16,1024]{2,1,0:T(8,128)(2,1)S(1)}, bf16[2,16,1024]{2,1,0:T(8,128)(2,1)S(1)}, u32[]{:S(2)}, u32[]{:S(2)}) collective-permute-start(bf16[2,16,1024]{2,1,0:T(8,128)(2,1)S(1)} %get-tuple-element.59), channel_id=1, source_target_pairs={{0,2},{1,3},{2,0},{3,1},{4,6},{5,7},{6,4},{7,5},{8,10},{9,11},{10,... | collective-permute-start | bytes 196616 | tf_op jit(solution)/shard_map/ppermute | solution.py:336
  54.7 5.0 %collective-permute-start.13 = (bf16[2,16,1024]{2,1,0:T(8,128)(2,1)S(1)}, bf16[2,16,1024]{2,1,0:T(8,128)(2,1)S(1)}, u32[]{:S(2)}, u32[]{:S(2)}) collective-permute-start(bf16[2,16,1024]{2,1,0:T(8,128)(2,1)S(1)} %get-tuple-element.60), channel_id=1, source_target_pairs={{0,3},{1,2},{2,1},{3,0},{4,7},{5,6},{6,5},{7,4},{8,11},{9,10},{10,... | collective-permute-start | bytes 196616 | tf_op jit(solution)/shard_map/ppermute | solution.py:336
  64.9 7.9 %collective-permute-start.15 = (bf16[8,16,1024]{2,1,0:T(8,128)(2,1)S(1)}, bf16[8,16,1024]{2,1,0:T(8,128)(2,1)S(1)}, u32[]{:S(2)}, u32[]{:S(2)}) collective-permute-start(bf16[8,16,1024]{2,1,0:T(8,128)(2,1)S(1)} %shard_map.83), channel_id=1, source_target_pairs={{4,8},{8,4},{12,16},{16,12},{20,24},{24,20},{28,32},{32,28},{36,40... | collective-permute-start | bytes 786440 | tf_op jit(solution)/shard_map/ppermute | solution.py:345
  75.5 5.1 %collective-permute-start.17 = (f32[2,16,1024]{2,1,0:T(8,128)S(1)}, f32[2,16,1024]{2,1,0:T(8,128)S(1)}, u32[]{:S(2)}, u32[]{:S(2)}) collective-permute-start(f32[2,16,1024]{2,1,0:T(8,128)S(1)} %get-tuple-element.64), channel_id=1, source_target_pairs={{0,1},{1,0},{2,3},{3,2},{4,5},{5,4},{6,7},{7,6},{8,9},{9,8},{10,11... | collective-permute-start | bytes 393224 | tf_op jit(solution)/shard_map/ppermute | solution.py:336
  75.6 7.8 %collective-permute-start.18 = (f32[2,16,1024]{2,1,0:T(8,128)S(1)}, f32[2,16,1024]{2,1,0:T(8,128)S(1)}, u32[]{:S(2)}, u32[]{:S(2)}) collective-permute-start(f32[2,16,1024]{2,1,0:T(8,128)S(1)} %get-tuple-element.65), channel_id=1, source_target_pairs={{0,2},{1,3},{2,0},{3,1},{4,6},{5,7},{6,4},{7,5},{8,10},{9,11},{10,... | collective-permute-start | bytes 393224 | tf_op jit(solution)/shard_map/ppermute | solution.py:336
  77.1 8.9 %collective-permute-start.19 = (f32[2,16,1024]{2,1,0:T(8,128)S(1)}, f32[2,16,1024]{2,1,0:T(8,128)S(1)}, u32[]{:S(2)}, u32[]{:S(2)}) collective-permute-start(f32[2,16,1024]{2,1,0:T(8,128)S(1)} %get-tuple-element.66), channel_id=1, source_target_pairs={{0,3},{1,2},{2,1},{3,0},{4,7},{5,6},{6,5},{7,4},{8,11},{9,10},{10,... | collective-permute-start | bytes 393224 | tf_op jit(solution)/shard_map/ppermute | solution.py:336
  90.8 25.7 %collective-permute-start.23 = (f32[2,16,1024]{2,1,0:T(8,128)S(1)}, f32[2,16,1024]{2,1,0:T(8,128)S(1)}, u32[]{:S(2)}, u32[]{:S(2)}) collective-permute-start(f32[2,16,1024]{2,1,0:T(8,128)S(1)} %get-tuple-element.75), channel_id=1, source_target_pairs={{0,1},{1,0},{2,3},{3,2},{4,5},{5,4},{6,7},{7,6},{8,9},{9,8},{10,11... | collective-permute-start | bytes 393224 | tf_op jit(solution)/shard_map/ppermute | solution.py:336
  90.8 25.7 %collective-permute-start.24 = (f32[2,16,1024]{2,1,0:T(8,128)S(1)}, f32[2,16,1024]{2,1,0:T(8,128)S(1)}, u32[]{:S(2)}, u32[]{:S(2)}) collective-permute-start(f32[2,16,1024]{2,1,0:T(8,128)S(1)} %get-tuple-element.76), channel_id=1, source_target_pairs={{0,2},{1,3},{2,0},{3,1},{4,6},{5,7},{6,4},{7,5},{8,10},{9,11},{10,... | collective-permute-start | bytes 393224 | tf_op jit(solution)/shard_map/ppermute | solution.py:336
  94.3 22.2 %collective-permute-start.25 = (f32[2,16,1024]{2,1,0:T(8,128)S(1)}, f32[2,16,1024]{2,1,0:T(8,128)S(1)}, u32[]{:S(2)}, u32[]{:S(2)}) collective-permute-start(f32[2,16,1024]{2,1,0:T(8,128)S(1)} %get-tuple-element.77), channel_id=1, source_target_pairs={{0,3},{1,2},{2,1},{3,0},{4,7},{5,6},{6,5},{7,4},{8,11},{9,10},{10,... | collective-permute-start | bytes 393224 | tf_op jit(solution)/shard_map/ppermute | solution.py:336
  94.6 34.5 %all-to-all-start = ((f32[256,1,128]{2,1,0:T(1,128)}), f32[256,1,128]{2,1,0:T(1,128)S(1)}, u32[]{:S(2)}, u32[]{:S(2)}) async-start(f32[256,1,128]{2,1,0:T(1,128)} %get-tuple-element.71), calls=%async_computation | async-start | bytes 262144 | tf_op jit(solution)/shard_map/all_to_all | solution.py:410
  118.1 14.8 %collective-permute-start.26 = (f32[4,16,1024]{2,1,0:T(8,128)}, f32[4,16,1024]{2,1,0:T(8,128)S(1)}, u32[]{:S(2)}, u32[]{:S(2)}) collective-permute-start(f32[4,16,1024]{2,1,0:T(8,128)} %get-tuple-element.79), channel_id=1, source_target_pairs={{0,4},{4,0},{8,12},{12,8},{16,20},{20,16},{24,28},{28,24},{32,36},... | collective-permute-start | bytes 786440 | tf_op jit(solution)/shard_map/ppermute | solution.py:340
  120.3 12.7 %collective-permute-start.27 = (f32[4,16,1024]{2,1,0:T(8,128)S(1)}, f32[4,16,1024]{2,1,0:T(8,128)S(1)}, u32[]{:S(2)}, u32[]{:S(2)}) collective-permute-start(f32[4,16,1024]{2,1,0:T(8,128)S(1)} %get-tuple-element.80), channel_id=1, source_target_pairs={{4,8},{8,4},{12,16},{16,12},{20,24},{24,20},{28,32},{32,28},{36,40... | collective-permute-start | bytes 786440 | tf_op jit(solution)/shard_map/ppermute | solution.py:345
  129.6 7.4 %collective-permute-start.22 = (bf16[4,16,1024]{2,1,0:T(8,128)(2,1)S(1)}, bf16[4,16,1024]{2,1,0:T(8,128)(2,1)S(1)}, u32[]{:S(2)}, u32[]{:S(2)}) collective-permute-start(bf16[4,16,1024]{2,1,0:T(8,128)(2,1)S(1)} %shard_map.86.s0), channel_id=1, source_target_pairs={{0,3},{1,2},{2,1},{3,0},{4,7},{5,6},{6,5},{7,4},{8,11},{9,10},{10,... | collective-permute-start | bytes 393224 | tf_op jit(solution)/shard_map/ppermute | solution.py:336
  130.7 7.8 %collective-permute-start.21 = (bf16[4,16,1024]{2,1,0:T(8,128)(2,1)S(1)}, bf16[4,16,1024]{2,1,0:T(8,128)(2,1)S(1)}, u32[]{:S(2)}, u32[]{:S(2)}) collective-permute-start(bf16[4,16,1024]{2,1,0:T(8,128)(2,1)S(1)} %shard_map.86.s0), channel_id=1, source_target_pairs={{0,2},{1,3},{2,0},{3,1},{4,6},{5,7},{6,4},{7,5},{8,10},{9,11},{10,... | collective-permute-start | bytes 393224 | tf_op jit(solution)/shard_map/ppermute | solution.py:336
  131.9 6.7 %collective-permute-start.20 = (bf16[4,16,1024]{2,1,0:T(8,128)(2,1)S(1)}, bf16[4,16,1024]{2,1,0:T(8,128)(2,1)S(1)}, u32[]{:S(2)}, u32[]{:S(2)}) collective-permute-start(bf16[4,16,1024]{2,1,0:T(8,128)(2,1)S(1)} %shard_map.86.s0), channel_id=1, source_target_pairs={{0,1},{1,0},{2,3},{3,2},{4,5},{5,4},{6,7},{7,6},{8,9},{9,8},{10,11... | collective-permute-start | bytes 393224 | tf_op jit(solution)/shard_map/ppermute | solution.py:336
  133.5 9.7 %collective-permute-start.30 = (bf16[4,16,1024]{2,1,0:T(8,128)(2,1)S(1)}, bf16[4,16,1024]{2,1,0:T(8,128)(2,1)S(1)}, u32[]{:S(2)}, u32[]{:S(2)}) collective-permute-start(bf16[4,16,1024]{2,1,0:T(8,128)(2,1)S(1)} %shard_map.90.s0), channel_id=1, source_target_pairs={{0,3},{1,2},{2,1},{3,0},{4,7},{5,6},{6,5},{7,4},{8,11},{9,10},{10,... | collective-permute-start | bytes 393224 | tf_op jit(solution)/shard_map/ppermute | solution.py:336
  134.6 8.7 %collective-permute-start.29 = (bf16[4,16,1024]{2,1,0:T(8,128)(2,1)S(1)}, bf16[4,16,1024]{2,1,0:T(8,128)(2,1)S(1)}, u32[]{:S(2)}, u32[]{:S(2)}) collective-permute-start(bf16[4,16,1024]{2,1,0:T(8,128)(2,1)S(1)} %shard_map.90.s0), channel_id=1, source_target_pairs={{0,2},{1,3},{2,0},{3,1},{4,6},{5,7},{6,4},{7,5},{8,10},{9,11},{10,... | collective-permute-start | bytes 393224 | tf_op jit(solution)/shard_map/ppermute | solution.py:336
  137.1 6.9 %collective-permute-start.28 = (bf16[4,16,1024]{2,1,0:T(8,128)(2,1)S(1)}, bf16[4,16,1024]{2,1,0:T(8,128)(2,1)S(1)}, u32[]{:S(2)}, u32[]{:S(2)}) collective-permute-start(bf16[4,16,1024]{2,1,0:T(8,128)(2,1)S(1)} %shard_map.90.s0), channel_id=1, source_target_pairs={{0,1},{1,0},{2,3},{3,2},{4,5},{5,4},{6,7},{7,6},{8,9},{9,8},{10,11... | collective-permute-start | bytes 393224 | tf_op jit(solution)/shard_map/ppermute | solution.py:336
  (14 other events, 92.0 us)

commit v3 on v2

--- a/solution.py
+++ b/solution.py
@@ -16,6 +16,7 @@
 Q = X // ANG
 UB = 32
 ZD = 4
+AHEAD = 3
 CH = 128
 COEF = 3 * 128
 GROUP = 8
@@ -75,7 +76,15 @@
         outs[r][:, :, :Q] = share.astype(outs[r].dtype)
 
 
-def mask_kernel(me, rows, reach, inner, outer):
+def open_inputs(me, rows_hbm, reach_hbm, cols_hbm, p_hbm, inner, own, outer, cols, p, rows, reach, sem):
+    copies = [
+        pltpu.make_async_copy(src, dst, sem.at[at])
+        for at, (src, dst) in enumerate(((rows_hbm, rows), (reach_hbm, reach), (cols_hbm, cols), (p_hbm, p)))
+    ]
+    for copy in copies:
+        copy.start()
+    copies[0].wait()
+    copies[1].wait()
     even = me[1] == 0
     for i in range(PAIR):
         for z in range(ZD):
@@ -84,20 +93,27 @@
             at = slice(ZD * i + z, ZD * i + z + 1)
             inner[at] = jnp.full((1, 128), jnp.where(even, top, low), F32)
             outer[at] = jnp.full((1, 128), jnp.where(even, low, top), F32)
-
-
-def back_kernel(me_ref, cols, rows, inner, outer, p_ref, w_hbm, o0, o1, o2, o3, w, acc, sem):
-    copies = {}
+            own[at] = jnp.full((1, 128), rows[i, 0, 1, 0, z], F32)
+    copies[2].wait()
+    copies[3].wait()
+
+
+def back_kernel(me_ref, cols, own, inner, outer, p_ref, w_hbm, o0, o1, o2, o3, w, acc, sem):
+    copies = []
     for a in range(PAIR):
         for g in range(UB // GROUP):
             span = pl.ds(GROUP * g, GROUP)
-            copies[a, g] = pltpu.make_async_copy(w_hbm.at[a, span], w.at[a, span], sem.at[a, g])
-            copies[a, g].start()
+            copies.append(pltpu.make_async_copy(w_hbm.at[a, span], w.at[a, span], sem.at[a, g]))
+    for copy in copies[:AHEAD]:
+        copy.start()
     acc[...] = jnp.zeros_like(acc)
     for a in range(PAIR):
         for block in range(UB):
+            at = (a * UB + block) // GROUP
             if block % GROUP == 0:
-                copies[a, block // GROUP].wait()
+                copies[at].wait()
+                if at + AHEAD < len(copies):
+                    copies[at + AHEAD].start()
             back_block(a, block, p_ref[a, 0, :, 128 * block:128 * (block + 1)], cols, w, acc)
     outs = (o0, o1, o2, o3)
     send_shares(me_ref[0], acc, outs)
@@ -105,10 +121,8 @@
     from_low = jnp.where(even, outer[...], inner[...])
     from_high = jnp.where(even, inner[...], outer[...])
     for i in range(PAIR):
-        own = [jnp.full((1, 128), rows[i, 0, 1, 0, z], F32) for z in range(ZD)]
-        rest = jnp.concatenate(
-            [from_low[ZD * i:ZD * (i + 1)]] + own + [from_high[ZD * i:ZD * (i + 1)], jnp.zeros((4, 128), F32)], axis=0
-        )
+        at = slice(ZD * i, ZD * (i + 1))
+        rest = jnp.concatenate([from_low[at], own[at], from_high[at], jnp.zeros((4, 128), F32)], axis=0)
         for part in range(3):
             piece = rest.astype(BF16)
             rest = rest - piece.astype(F32)
@@ -153,17 +167,16 @@
 
 
 def second_kernel(me_ref, cols, h0, h1, h2, h3, q0_ref, gamma_ref, curve_ref, inner_ref, w,
-                  o0, o1, o2, o3, w_out, sums, both, acc):
+                  o0, o1, o2, o3, w_out, hb, acc):
 
     def place(at, share):
-        for a in range(PAIR):
-            both[a, :, at] = halves(share[a].astype(F32))
+        hb[:, :, at] = share[...]
 
     def store(a, block, image):
         w_out[a, :, 128 * block:128 * (block + 1)] = image
 
     gather_shares(me_ref[0], (h0, h1, h2, h3), place)
-    both_body(cols, w, acc, lambda a, at: both[a, :, at], store)
+    both_body(cols, w, acc, lambda a, at: hb[a, :, at], store)
     send_shares(me_ref[0], acc, (o0, o1, o2, o3))
     cross = fold(w_out[0] * q0_ref[0]) + fold(w_out[1] * q0_ref[1])
     own = fold(w_out[0] * w_out[0]) + fold(w_out[1] * w_out[1])
@@ -171,7 +184,8 @@
     row = jnp.zeros((1, 128), F32)
     for at, value in enumerate((gamma_ref[...], curve_ref[...], inner_ref[:8], inner_ref[8:], cross, own)):
         row = jnp.where(lane == at, jnp.sum(value), row)
-    sums[...] = jnp.broadcast_to(row[None], sums.shape)
+    for out in (o0, o1, o2, o3):
+        out[:, :, Q:] = jnp.broadcast_to(row[None], (PAIR, L, 128))
 
 
 def spread_slices(coefs, parts, cut):
@@ -278,7 +292,9 @@
                 lambda: (jnp.zeros((8, 128), F32),) * 2, note, end)
 
 
-def last_kernel(me, coefs, c0, c1, c2, c3, own, inner, outer):
+def last_kernel(me, coefs, c0, c1, c2, c3, own, inner, outer, sums):
+    row = (c0[0, :1, Q:] + c1[0, :1, Q:]) + (c2[0, :1, Q:] + c3[0, :1, Q:])
+    sums[...] = jnp.broadcast_to(row[None], sums.shape)
     for parity, far, near in ((0, 0, 8), (1, 8, 0)):
         @pl.when(me[1] == parity)
         def _(far=far, near=near):
@@ -357,11 +373,13 @@
 def per_device(projections, weights, columns, row_weights, reach):
     me = jnp.stack([lax.axis_index("ang"), lax.axis_index("slab") % 2]).astype(jnp.int32)
     row = sds((PAIR * ZD, 128), F32)
-    inner, outer = call(mask_kernel, [row] * 2, [SMEM] * 3)(me, row_weights, reach)
+    inner, own, outer, cols, p = call(
+        open_inputs, [row] * 3 + [sds((3, PAIR, UB), jnp.int32), sds(projections.shape, F32)], [SMEM] + [HBM] * 4,
+        [pltpu.SMEM(row_weights.shape, F32), pltpu.SMEM(reach.shape, jnp.int32), pltpu.SemaphoreType.DMA((4,))],
+        limit=53,
+    )(me, row_weights, reach, columns.transpose(2, 0, 1), projections)
     outer = across(outer)
-    edges = (on_chip(inner), outer)
-
-    cols = columns.transpose(2, 0, 1)
+    edges = (own, on_chip(inner), outer)
 
     def share(dtype, more=0):
         return sds((PAIR, L, Q + more), dtype)
@@ -381,9 +399,9 @@
 
     *shares, w = call(
         back_kernel, [share(BF16, COEF)] * 4 + [sds((PAIR, UB, 384, 128), BF16)],
-        [SMEM] * 3 + [VMEM] * 3 + [HBM], [acc, pltpu.SemaphoreType.DMA((PAIR, UB // GROUP))],
+        [SMEM] * 2 + [VMEM] * 4 + [HBM], [acc, pltpu.SemaphoreType.DMA((PAIR, UB // GROUP))],
         flops=2 * macs, nbytes=7_000_000, limit=46,
-    )(me, cols, row_weights, *edges, projections, weights.reshape(PAIR, UB, 384, 128))
+    )(me, cols, *edges, p, weights.reshape(PAIR, UB, 384, 128))
     *spread, coefs = call(
         open_kernel, sent + [sds((ANG, PAIR, L, 128), F32)], [VMEM] * 4, flops=10_000_000
     )(*exchange(shares))
@@ -398,22 +416,24 @@
     )(me, cols, *exchange(shares), w)
     spread = call(combine_kernel, sent, [VMEM] * 5, flops=10_000_000)(coefs, *exchange(shares))
     z0, *shares, inner = call(
-        pieces_second, [part] + [share(F32)] * 4 + [sds((16, 128), F32)], [SMEM] + [VMEM] * 6, flops=10_000_000
+        pieces_second, [part] + [share(BF16)] * 4 + [sds((16, 128), F32)], [SMEM] + [VMEM] * 6, flops=10_000_000
     )(me, coefs, g0, *halo(*spread))
 
-    *shares, w0, sums = call(
-        second_kernel, [share(F32)] * 4 + [full, sds((lax.axis_size("slab") * ANG, 1, 128), F32)],
-        [SMEM] * 2 + [VMEM] * 9, [pltpu.VMEM((PAIR, 2 * L, X), BF16), acc],
+    *shares, w0 = call(
+        second_kernel, [share(F32, 128)] * 4 + [full],
+        [SMEM] * 2 + [VMEM] * 9, [pltpu.VMEM((PAIR, L, X), BF16), acc],
         flops=4 * macs, nbytes=9_000_000,
     )(me, cols, *exchange(shares), q0, gamma, curve, inner, w)
-    shares = exchange(shares)
-    sums = lax.all_to_all(sums, ("slab", "ang"), 0, 0, tiled=True)
+    own, inner, outer, sums = call(
+        last_kernel, [part] * 3 + [sds((lax.axis_size("slab"), 1, 128), F32)], [SMEM] + [VMEM] * 5, flops=10_000_000
+    )(me, coefs, *exchange(shares))
+    outer = across(outer)
+    inner = on_chip(inner)
+    sums = lax.all_to_all(sums, "slab", 0, 0, tiled=True)
     (volume,) = call(volume_kernel, [part_b], [VMEM] * 3)(sums, g0, z0)
     (residual,) = call(residual_kernel, [sds(projections.shape, F32)], [VMEM] * 4)(sums, projections, q0, w0)
     volume = exchange((volume,) * 4)
-    t1, inner, outer = call(last_kernel, [part] * 3, [SMEM] + [VMEM] * 5, flops=10_000_000)(me, coefs, *shares)
-    outer = across(outer)
-    (gradient,) = call(gradient_kernel, [part_b], [VMEM] * 6)(sums, t1, on_chip(inner), outer, g0, z0)
+    (gradient,) = call(gradient_kernel, [part_b], [VMEM] * 6)(sums, own, inner, outer, g0, z0)
     whole = [sds((ZD, L, X), F32)]
     (volume,) = call(place_kernel, whole, [SMEM] + [VMEM] * 4)(me, *volume)
     (gradient,) = call(place_kernel, whole, [SMEM] + [VMEM] * 4)(me, *exchange((gradient,) * 4))

time: 146 us -> 149 us (1.021)
  blocking collectives: 0 us -> 28.4 us
  starting transfers between devices: 68.9 us -> 48.1 us
  waiting for transfers between devices: 45.6 us -> 42.6 us
  local copies, waits for them, and re-layouts: 3.78 us -> 2.05 us
    all_to_all x0 -> x1, blocking collectives: none -> 28.4 us  [per_device(): sums = lax.all_to_all(sums, 'slab', 0, 0, tiled=True)]
    all_to_all x1 -> x0, starting transfers between devices: 21.8 us -> none  [per_device(): sums = lax.all_to_all(sums, ('slab', 'ang'), 0, 0, tiled=True)]
    all_to_all x1 -> x0, waiting for transfers between devices: 6.92 us -> none  [per_device(): sums = lax.all_to_all(sums, ('slab', 'ang'), 0, 0, tiled=True)]
    ppermute x21, waiting for transfers between devices: 21.5 us -> 25.4 us  [along_ang(): return lax.ppermute(value, 'ang', [(i, i ^ other) for i in range(ANG)])]
    unnamed x12 -> x8, local copies, waits for them, and re-layouts: 3.78 us -> 2.05 us
  transfers between devices with their start and end apart: 32 -> 31, of which waited for: 20 -> 21; matrix products, arithmetic and copies ran while one was open for 0% -> 0% of each run, Pallas kernels for 4% -> 2%
where the time goes in v3:
time: 149 us; the launch traced here: 148 us
  starting transfers between devices  48.1 us (32%)
  waiting for transfers between devices  42.6 us (29%)
  blocking collectives  28.4 us (19%)
  Pallas kernels  25.6 us (17%)
  local copies, waits for them, and re-layouts  2.05 us (1%)
    all_to_all x1, blocking collectives, per_device(): sums = lax.all_to_all(sums, 'slab', 0, 0, tiled=True)  28.4 us
    ppermute x21, waiting for transfers between devices, along_ang(): return lax.ppermute(value, 'ang', [(i, i ^ other) for i in range(ANG)])  25.4 us
    ppermute x21, starting transfers between devices, along_ang(): return lax.ppermute(value, 'ang', [(i, i ^ other) for i in range(ANG)])  24.9 us
    ppermute x4, starting transfers between devices, across(): lax.ppermute(value, 'slab', [pair for i in range(1, count - 1, 2) for pai...  14.9 us
    ppermute x4, waiting for transfers between devices, across(): lax.ppermute(value, 'slab', [pair for i in range(1, count - 1, 2) for pai...  11.1 us
    ppermute x6, starting transfers between devices, on_chip(): lax.ppermute(value, 'slab', [(i, i ^ 1) for i in range(lax.axis_size('sla...  8.25 us
    ppermute x6, waiting for transfers between devices, on_chip(): lax.ppermute(value, 'slab', [(i, i ^ 1) for i in range(lax.axis_size('sla...  6.13 us
    pallas_call x1, Pallas kernels, per_device(): call(back_kernel, [share(BF16, COEF)] * 4 + [sds((PAIR, UB, 384, 128), BF...  5.13 us
  transfers between devices with their start and end apart: 31, of which 21 were waited for; matrix products, arithmetic and copies ran while one was open for 0% of the time, Pallas kernels for 2%

profile of v3, /device:TPU:1, one launch (start us, length us, event | category | flops | bytes accessed | tf_op | source)
XLA Modules:
  0.0 147.6 jit_solution(3528527330309373116)
XLA Ops:
  4.4 3.3 %collective-permute-start = (f32[8,128]{1,0:T(8,128)S(1)}, f32[8,128]{1,0:T(8,128)S(1)}, u32[]{:S(2)}, u32[]{:S(2)}) collective-permute-start(f32[8,128]{1,0:T(8,128)S(1)} %get-tuple-element.47), channel_id=1, source_target_pairs={{0,4},{4,0},{8,12},{12,8},{16,20},{20,16},{24,28},{28,24},{32,36},... | collective-permute-start | bytes 12296 | tf_op jit(solution)/shard_map/ppermute | solution.py:356
  9.6 3.0 %collective-permute-done.1.outer = f32[8,128]{1,0:T(8,128)S(1)} collective-permute-done((f32[8,128]{1,0:T(8,128)S(1)}, f32[8,128]{1,0:T(8,128)S(1)}, u32[]{:S(2)}, u32[]{:S(2)}) %collective-permute-start.1) | collective-permute-done | bytes 4128 | tf_op jit(solution)/shard_map/ppermute | solution.py:361
  12.6 5.1 %shard_map.77 = (bf16[2,16,1408]{2,1,0:T(8,128)(2,1)S(1)}, bf16[2,16,1408]{2,1,0:T(8,128)(2,1)S(1)}, bf16[2,16,1408]{2,1,0:T(8,128)(2,1)S(1)}, bf16[2,16,1408]{2...) custom-call(s32[2]{0:T(128)S(1)} %pad_add_fusion.me.me_ref, s32[3,2,32]{2,1,0:T(2,128)S(1)} %get-tuple-element.45.cols, ...), custom_call_target="tpu_custom_call" | custom-call | flops 201326592 | bytes 7000000 | tf_op jit(solution)/shard_map/pallas_call | solution.py:400
  17.9 2.2 %collective-permute-start.3 = (bf16[2,16,1408]{2,1,0:T(8,128)(2,1)S(1)}, bf16[2,16,1408]{2,1,0:T(8,128)(2,1)S(1)}, u32[]{:S(2)}, u32[]{:S(2)}) collective-permute-start(bf16[2,16,1408]{2,1,0:T(8,128)(2,1)S(1)} %get-tuple-element.52), channel_id=1, source_target_pairs={{0,2},{1,3},{2,0},{3,1},{4,6},{5,7},{6,4},{7,5},{8,10},{9,11},{10,... | collective-permute-start | bytes 270344 | tf_op jit(solution)/shard_map/ppermute | solution.py:352
  27.6 5.8 %collective-permute-start.6 = (bf16[8,16,1024]{2,1,0:T(8,128)(2,1)S(1)}, bf16[8,16,1024]{2,1,0:T(8,128)(2,1)S(1)}, u32[]{:S(2)}, u32[]{:S(2)}) collective-permute-start(bf16[8,16,1024]{2,1,0:T(8,128)(2,1)S(1)} %shard_map.79), channel_id=1, source_target_pairs={{4,8},{8,4},{12,16},{16,12},{20,24},{24,20},{28,32},{32,28},{36,40... | collective-permute-start | bytes 786440 | tf_op jit(solution)/shard_map/ppermute | solution.py:361
  33.4 4.0 %collective-permute-done.6.outer = bf16[8,16,1024]{2,1,0:T(8,128)(2,1)S(1)} collective-permute-done((bf16[8,16,1024]{2,1,0:T(8,128)(2,1)S(1)}, bf16[8,16,1024]{2,1,0:T(8,128)(2,1)S(1)}, u32[]{:S(2)}, u32[]{:S(2)}) %collective-permute-start.6) | collective-permute-done | bytes 262176 | tf_op jit(solution)/shard_map/ppermute | solution.py:361
  41.8 2.4 %collective-permute-start.10 = (bf16[2,16,1024]{2,1,0:T(8,128)(2,1)S(1)}, bf16[2,16,1024]{2,1,0:T(8,128)(2,1)S(1)}, u32[]{:S(2)}, u32[]{:S(2)}) collective-permute-start(bf16[2,16,1024]{2,1,0:T(8,128)(2,1)S(1)} %get-tuple-element.61), channel_id=1, source_target_pairs={{0,3},{1,2},{2,1},{3,0},{4,7},{5,6},{6,5},{7,4},{8,11},{9,10},{10,... | collective-permute-start | bytes 196616 | tf_op jit(solution)/shard_map/ppermute | solution.py:352
  46.4 4.1 %shard_map.81 = (bf16[2,16,1024]{2,1,0:T(8,128)(2,1)S(1)}, bf16[2,16,1024]{2,1,0:T(8,128)(2,1)S(1)}, bf16[2,16,1024]{2,1,0:T(8,128)(2,1)S(1)}, bf16[2,16,1024]{2...) custom-call(s32[2]{0:T(128)S(1)} %pad_add_fusion.me.me_ref, ...), custom_call_target="tpu_custom_call" | custom-call | flops 301989888 | bytes 7000000 | tf_op jit(solution)/shard_map/pallas_call | solution.py:412
  50.7 3.3 %collective-permute-start.12 = (bf16[2,16,1024]{2,1,0:T(8,128)(2,1)S(1)}, bf16[2,16,1024]{2,1,0:T(8,128)(2,1)S(1)}, u32[]{:S(2)}, u32[]{:S(2)}) collective-permute-start(bf16[2,16,1024]{2,1,0:T(8,128)(2,1)S(1)} %get-tuple-element.65), channel_id=1, source_target_pairs={{0,2},{1,3},{2,0},{3,1},{4,6},{5,7},{6,4},{7,5},{8,10},{9,11},{10,... | collective-permute-start | bytes 196616 | tf_op jit(solution)/shard_map/ppermute | solution.py:352
  56.3 2.7 %collective-permute-done.13.c3 = bf16[2,16,1024]{2,1,0:T(8,128)(2,1)S(1)} collective-permute-done((bf16[2,16,1024]{2,1,0:T(8,128)(2,1)S(1)}, bf16[2,16,1024]{2,1,0:T(8,128)(2,1)S(1)}, u32[]{:S(2)}, u32[]{:S(2)}) %collective-permute-start.13) | collective-permute-done | bytes 65568 | tf_op jit(solution)/shard_map/ppermute | solution.py:352
  59.5 2.8 %collective-permute-start.14 = (bf16[12,16,1024]{2,1,0:T(8,128)(2,1)S(1)}, bf16[12,16,1024]{2,1,0:T(8,128)(2,1)S(1)}, u32[]{:S(2)}, u32[]{:S(2)}) collective-permute-start(bf16[12,16,1024]{2,1,0:T(8,128)(2,1)S(1)} %get-tuple-element.68), channel_id=1, source_target_pairs={{0,4},{4,0},{8,12},{12,8},{16,20},{20,16},{24,28},{28,24},{32,36},... | collective-permute-start | bytes 1179656 | tf_op jit(solution)/shard_map/ppermute | solution.py:356
  64.2 4.0 %collective-permute-start.15 = (bf16[8,16,1024]{2,1,0:T(8,128)(2,1)S(1)}, bf16[8,16,1024]{2,1,0:T(8,128)(2,1)S(1)}, u32[]{:S(2)}, u32[]{:S(2)}) collective-permute-start(bf16[8,16,1024]{2,1,0:T(8,128)(2,1)S(1)} %shard_map.83), channel_id=1, source_target_pairs={{4,8},{8,4},{12,16},{16,12},{20,24},{24,20},{28,32},{32,28},{36,40... | collective-permute-start | bytes 786440 | tf_op jit(solution)/shard_map/ppermute | solution.py:361
  68.2 4.0 %collective-permute-done.15.outer = bf16[8,16,1024]{2,1,0:T(8,128)(2,1)S(1)} collective-permute-done((bf16[8,16,1024]{2,1,0:T(8,128)(2,1)S(1)}, bf16[8,16,1024]{2,1,0:T(8,128)(2,1)S(1)}, u32[]{:S(2)}, u32[]{:S(2)}) %collective-permute-start.15) | collective-permute-done | bytes 262176 | tf_op jit(solution)/shard_map/ppermute | solution.py:361
  76.6 2.4 %collective-permute-start.19 = (bf16[2,16,1024]{2,1,0:T(8,128)(2,1)S(1)}, bf16[2,16,1024]{2,1,0:T(8,128)(2,1)S(1)}, u32[]{:S(2)}, u32[]{:S(2)}) collective-permute-start(bf16[2,16,1024]{2,1,0:T(8,128)(2,1)S(1)} %get-tuple-element.72), channel_id=1, source_target_pairs={{0,3},{1,2},{2,1},{3,0},{4,7},{5,6},{6,5},{7,4},{8,11},{9,10},{10,... | collective-permute-start | bytes 196616 | tf_op jit(solution)/shard_map/ppermute | solution.py:352
  81.3 4.1 %shard_map.85 = (f32[2,16,1152]{2,1,0:T(8,128)S(1)}, f32[2,16,1152]{2,1,0:T(8,128)S(1)}, f32[2,16,1152]{2,1,0:T(8,128)S(1)}, f32[2,16,1152]{2,1,0:T(8,128)S(1)}, f32[2,16,4096]{2,1,0:T(8,128)S(1)}) custom-call(s32[2]{0:T(128)S(1)} %pad_add_fusion.me.me_ref, s32[3,2,32]{2,1,0:T(2,128)S(1)} %get-tuple-element.45.cols, ...), custom_call_target="tpu_custom_call" | custom-call | flops 402653184 | bytes 9000000 | tf_op jit(solution)/shard_map/pallas_call | solution.py:422
  85.6 3.3 %collective-permute-start.21 = (f32[2,16,1152]{2,1,0:T(8,128)S(1)}, f32[2,16,1152]{2,1,0:T(8,128)S(1)}, u32[]{:S(2)}, u32[]{:S(2)}) collective-permute-start(f32[2,16,1152]{2,1,0:T(8,128)S(1)} %get-tuple-element.79), channel_id=1, source_target_pairs={{0,2},{1,3},{2,0},{3,1},{4,6},{5,7},{6,4},{7,5},{8,10},{9,11},{10,... | collective-permute-start | bytes 442376 | tf_op jit(solution)/shard_map/ppermute | solution.py:352
  89.5 4.4 %collective-permute-done.21.c2 = f32[2,16,1152]{2,1,0:T(8,128)S(1)} collective-permute-done((f32[2,16,1152]{2,1,0:T(8,128)S(1)}, f32[2,16,1152]{2,1,0:T(8,128)S(1)}, u32[]{:S(2)}, u32[]{:S(2)}) %collective-permute-start.21) | collective-permute-done | bytes 147488 | tf_op jit(solution)/shard_map/ppermute | solution.py:352
  93.9 2.8 %collective-permute-done.22.c3 = f32[2,16,1152]{2,1,0:T(8,128)S(1)} collective-permute-done((f32[2,16,1152]{2,1,0:T(8,128)S(1)}, f32[2,16,1152]{2,1,0:T(8,128)S(1)}, u32[]{:S(2)}, u32[]{:S(2)}) %collective-permute-start.22) | collective-permute-done | bytes 147488 | tf_op jit(solution)/shard_map/ppermute | solution.py:352
  97.7 2.0 %collective-permute-start.26 = (f32[4,16,1024]{2,1,0:T(8,128)S(1)}, f32[4,16,1024]{2,1,0:T(8,128)S(1)}, u32[]{:S(2)}, u32[]{:S(2)}) collective-permute-start(f32[4,16,1024]{2,1,0:T(8,128)S(1)} %get-tuple-element.85), channel_id=1, source_target_pairs={{0,4},{4,0},{8,12},{12,8},{16,20},{20,16},{24,28},{28,24},{32,36},... | collective-permute-start | bytes 786440 | tf_op jit(solution)/shard_map/ppermute | solution.py:356
  99.7 3.2 %collective-permute-start.27 = (f32[4,16,1024]{2,1,0:T(8,128)S(1)}, f32[4,16,1024]{2,1,0:T(8,128)S(1)}, u32[]{:S(2)}, u32[]{:S(2)}) collective-permute-start(f32[4,16,1024]{2,1,0:T(8,128)S(1)} %get-tuple-element.86), channel_id=1, source_target_pairs={{4,8},{8,4},{12,16},{16,12},{20,24},{24,20},{28,32},{32,28},{36,40... | collective-permute-start | bytes 786440 | tf_op jit(solution)/shard_map/ppermute | solution.py:361
  102.9 28.4 %all_to_all.5.sums = f32[64,1,128]{2,1,0:T(1,128)S(1)} all-to-all(f32[64,1,128]{2,1,0:T(1,128)S(1)} %get-tuple-element.81), channel_id=1, replica_groups=mesh['slab'=64,'ang'=4] {'slab'}, dimensions={0} | all-to-all | bytes 65536 | tf_op jit(solution)/shard_map/all_to_all | solution.py:432
  132.7 2.2 %collective-permute-start.23 = (bf16[4,16,1024]{2,1,0:T(8,128)(2,1)S(1)}, bf16[4,16,1024]{2,1,0:T(8,128)(2,1)S(1)}, u32[]{:S(2)}, u32[]{:S(2)}) collective-permute-start(bf16[4,16,1024]{2,1,0:T(8,128)(2,1)S(1)} %shard_map.87.s0), channel_id=1, source_target_pairs={{0,1},{1,0},{2,3},{3,2},{4,5},{5,4},{6,7},{7,6},{8,9},{9,8},{10,11... | collective-permute-start | bytes 393224 | tf_op jit(solution)/shard_map/ppermute | solution.py:352
  137.1 2.0 %collective-permute-done.25.s3 = bf16[4,16,1024]{2,1,0:T(8,128)(2,1)S(1)} collective-permute-done((bf16[4,16,1024]{2,1,0:T(8,128)(2,1)S(1)}, bf16[4,16,1024]{2,1,0:T(8,128)(2,1)S(1)}, u32[]{:S(2)}, u32[]{:S(2)}) %collective-permute-start.25) | collective-permute-done | bytes 131104 | tf_op jit(solution)/shard_map/ppermute | solution.py:352
  141.9 2.9 %collective-permute-done.30.s3 = bf16[4,16,1024]{2,1,0:T(8,128)(2,1)S(1)} collective-permute-done((bf16[4,16,1024]{2,1,0:T(8,128)(2,1)S(1)}, bf16[4,16,1024]{2,1,0:T(8,128)(2,1)S(1)}, u32[]{:S(2)}, u32[]{:S(2)}) %collective-permute-start.30) | collective-permute-done | bytes 131104 | tf_op jit(solution)/shard_map/ppermute | solution.py:352
  (64 shorter events, 42.3 us)
Async XLA Ops:
  4.4 5.2 %collective-permute-start = (f32[8,128]{1,0:T(8,128)S(1)}, f32[8,128]{1,0:T(8,128)S(1)}, u32[]{:S(2)}, u32[]{:S(2)}) collective-permute-start(f32[8,128]{1,0:T(8,128)S(1)} %get-tuple-element.47), channel_id=1, source_target_pairs={{0,4},{4,0},{8,12},{12,8},{16,20},{20,16},{24,28},{28,24},{32,36},... | collective-permute-start | bytes 12296 | tf_op jit(solution)/shard_map/ppermute | solution.py:356
  7.7 4.9 %collective-permute-start.1 = (f32[8,128]{1,0:T(8,128)S(1)}, f32[8,128]{1,0:T(8,128)S(1)}, u32[]{:S(2)}, u32[]{:S(2)}) collective-permute-start(f32[8,128]{1,0:T(8,128)S(1)} %get-tuple-element.48), channel_id=1, source_target_pairs={{4,8},{8,4},{12,16},{16,12},{20,24},{24,20},{28,32},{32,28},{36,40... | collective-permute-start | bytes 12296 | tf_op jit(solution)/shard_map/ppermute | solution.py:361
  17.9 5.0 %collective-permute-start.3 = (bf16[2,16,1408]{2,1,0:T(8,128)(2,1)S(1)}, bf16[2,16,1408]{2,1,0:T(8,128)(2,1)S(1)}, u32[]{:S(2)}, u32[]{:S(2)}) collective-permute-start(bf16[2,16,1408]{2,1,0:T(8,128)(2,1)S(1)} %get-tuple-element.52), channel_id=1, source_target_pairs={{0,2},{1,3},{2,0},{3,1},{4,6},{5,7},{6,4},{7,5},{8,10},{9,11},{10,... | collective-permute-start | bytes 270344 | tf_op jit(solution)/shard_map/ppermute | solution.py:352
  20.0 4.6 %collective-permute-start.4 = (bf16[2,16,1408]{2,1,0:T(8,128)(2,1)S(1)}, bf16[2,16,1408]{2,1,0:T(8,128)(2,1)S(1)}, u32[]{:S(2)}, u32[]{:S(2)}) collective-permute-start(bf16[2,16,1408]{2,1,0:T(8,128)(2,1)S(1)} %get-tuple-element.53), channel_id=1, source_target_pairs={{0,3},{1,2},{2,1},{3,0},{4,7},{5,6},{6,5},{7,4},{8,11},{9,10},{10,... | collective-permute-start | bytes 270344 | tf_op jit(solution)/shard_map/ppermute | solution.py:352
  27.6 9.9 %collective-permute-start.6 = (bf16[8,16,1024]{2,1,0:T(8,128)(2,1)S(1)}, bf16[8,16,1024]{2,1,0:T(8,128)(2,1)S(1)}, u32[]{:S(2)}, u32[]{:S(2)}) collective-permute-start(bf16[8,16,1024]{2,1,0:T(8,128)(2,1)S(1)} %shard_map.79), channel_id=1, source_target_pairs={{4,8},{8,4},{12,16},{16,12},{20,24},{24,20},{28,32},{32,28},{36,40... | collective-permute-start | bytes 786440 | tf_op jit(solution)/shard_map/ppermute | solution.py:361
  40.3 5.1 %collective-permute-start.9 = (bf16[2,16,1024]{2,1,0:T(8,128)(2,1)S(1)}, bf16[2,16,1024]{2,1,0:T(8,128)(2,1)S(1)}, u32[]{:S(2)}, u32[]{:S(2)}) collective-permute-start(bf16[2,16,1024]{2,1,0:T(8,128)(2,1)S(1)} %get-tuple-element.60), channel_id=1, source_target_pairs={{0,2},{1,3},{2,0},{3,1},{4,6},{5,7},{6,4},{7,5},{8,10},{9,11},{10,... | collective-permute-start | bytes 196616 | tf_op jit(solution)/shard_map/ppermute | solution.py:352
  41.8 4.6 %collective-permute-start.10 = (bf16[2,16,1024]{2,1,0:T(8,128)(2,1)S(1)}, bf16[2,16,1024]{2,1,0:T(8,128)(2,1)S(1)}, u32[]{:S(2)}, u32[]{:S(2)}) collective-permute-start(bf16[2,16,1024]{2,1,0:T(8,128)(2,1)S(1)} %get-tuple-element.61), channel_id=1, source_target_pairs={{0,3},{1,2},{2,1},{3,0},{4,7},{5,6},{6,5},{7,4},{8,11},{9,10},{10,... | collective-permute-start | bytes 196616 | tf_op jit(solution)/shard_map/ppermute | solution.py:352
  50.7 5.7 %collective-permute-start.12 = (bf16[2,16,1024]{2,1,0:T(8,128)(2,1)S(1)}, bf16[2,16,1024]{2,1,0:T(8,128)(2,1)S(1)}, u32[]{:S(2)}, u32[]{:S(2)}) collective-permute-start(bf16[2,16,1024]{2,1,0:T(8,128)(2,1)S(1)} %get-tuple-element.65), channel_id=1, source_target_pairs={{0,2},{1,3},{2,0},{3,1},{4,6},{5,7},{6,4},{7,5},{8,10},{9,11},{10,... | collective-permute-start | bytes 196616 | tf_op jit(solution)/shard_map/ppermute | solution.py:352
  54.0 5.0 %collective-permute-start.13 = (bf16[2,16,1024]{2,1,0:T(8,128)(2,1)S(1)}, bf16[2,16,1024]{2,1,0:T(8,128)(2,1)S(1)}, u32[]{:S(2)}, u32[]{:S(2)}) collective-permute-start(bf16[2,16,1024]{2,1,0:T(8,128)(2,1)S(1)} %get-tuple-element.66), channel_id=1, source_target_pairs={{0,3},{1,2},{2,1},{3,0},{4,7},{5,6},{6,5},{7,4},{8,11},{9,10},{10,... | collective-permute-start | bytes 196616 | tf_op jit(solution)/shard_map/ppermute | solution.py:352
  59.5 4.2 %collective-permute-start.14 = (bf16[12,16,1024]{2,1,0:T(8,128)(2,1)S(1)}, bf16[12,16,1024]{2,1,0:T(8,128)(2,1)S(1)}, u32[]{:S(2)}, u32[]{:S(2)}) collective-permute-start(bf16[12,16,1024]{2,1,0:T(8,128)(2,1)S(1)} %get-tuple-element.68), channel_id=1, source_target_pairs={{0,4},{4,0},{8,12},{12,8},{16,20},{20,16},{24,28},{28,24},{32,36},... | collective-permute-start | bytes 1179656 | tf_op jit(solution)/shard_map/ppermute | solution.py:356
  64.2 8.0 %collective-permute-start.15 = (bf16[8,16,1024]{2,1,0:T(8,128)(2,1)S(1)}, bf16[8,16,1024]{2,1,0:T(8,128)(2,1)S(1)}, u32[]{:S(2)}, u32[]{:S(2)}) collective-permute-start(bf16[8,16,1024]{2,1,0:T(8,128)(2,1)S(1)} %shard_map.83), channel_id=1, source_target_pairs={{4,8},{8,4},{12,16},{16,12},{20,24},{24,20},{28,32},{32,28},{36,40... | collective-permute-start | bytes 786440 | tf_op jit(solution)/shard_map/ppermute | solution.py:361
  75.1 5.1 %collective-permute-start.18 = (bf16[2,16,1024]{2,1,0:T(8,128)(2,1)S(1)}, bf16[2,16,1024]{2,1,0:T(8,128)(2,1)S(1)}, u32[]{:S(2)}, u32[]{:S(2)}) collective-permute-start(bf16[2,16,1024]{2,1,0:T(8,128)(2,1)S(1)} %get-tuple-element.71), channel_id=1, source_target_pairs={{0,2},{1,3},{2,0},{3,1},{4,6},{5,7},{6,4},{7,5},{8,10},{9,11},{10,... | collective-permute-start | bytes 196616 | tf_op jit(solution)/shard_map/ppermute | solution.py:352
  76.6 4.6 %collective-permute-start.19 = (bf16[2,16,1024]{2,1,0:T(8,128)(2,1)S(1)}, bf16[2,16,1024]{2,1,0:T(8,128)(2,1)S(1)}, u32[]{:S(2)}, u32[]{:S(2)}) collective-permute-start(bf16[2,16,1024]{2,1,0:T(8,128)(2,1)S(1)} %get-tuple-element.72), channel_id=1, source_target_pairs={{0,3},{1,2},{2,1},{3,0},{4,7},{5,6},{6,5},{7,4},{8,11},{9,10},{10,... | collective-permute-start | bytes 196616 | tf_op jit(solution)/shard_map/ppermute | solution.py:352
  85.4 4.1 %collective-permute-start.20 = (f32[2,16,1152]{2,1,0:T(8,128)S(1)}, f32[2,16,1152]{2,1,0:T(8,128)S(1)}, u32[]{:S(2)}, u32[]{:S(2)}) collective-permute-start(f32[2,16,1152]{2,1,0:T(8,128)S(1)} %get-tuple-element.78), channel_id=1, source_target_pairs={{0,1},{1,0},{2,3},{3,2},{4,5},{5,4},{6,7},{7,6},{8,9},{9,8},{10,11... | collective-permute-start | bytes 442376 | tf_op jit(solution)/shard_map/ppermute | solution.py:352
  85.6 8.3 %collective-permute-start.21 = (f32[2,16,1152]{2,1,0:T(8,128)S(1)}, f32[2,16,1152]{2,1,0:T(8,128)S(1)}, u32[]{:S(2)}, u32[]{:S(2)}) collective-permute-start(f32[2,16,1152]{2,1,0:T(8,128)S(1)} %get-tuple-element.79), channel_id=1, source_target_pairs={{0,2},{1,3},{2,0},{3,1},{4,6},{5,7},{6,4},{7,5},{8,10},{9,11},{10,... | collective-permute-start | bytes 442376 | tf_op jit(solution)/shard_map/ppermute | solution.py:352
  88.9 7.8 %collective-permute-start.22 = (f32[2,16,1152]{2,1,0:T(8,128)S(1)}, f32[2,16,1152]{2,1,0:T(8,128)S(1)}, u32[]{:S(2)}, u32[]{:S(2)}) collective-permute-start(f32[2,16,1152]{2,1,0:T(8,128)S(1)} %get-tuple-element.80), channel_id=1, source_target_pairs={{0,3},{1,2},{2,1},{3,0},{4,7},{5,6},{6,5},{7,4},{8,11},{9,10},{10,... | collective-permute-start | bytes 442376 | tf_op jit(solution)/shard_map/ppermute | solution.py:352
  97.7 37.2 %collective-permute-start.26 = (f32[4,16,1024]{2,1,0:T(8,128)S(1)}, f32[4,16,1024]{2,1,0:T(8,128)S(1)}, u32[]{:S(2)}, u32[]{:S(2)}) collective-permute-start(f32[4,16,1024]{2,1,0:T(8,128)S(1)} %get-tuple-element.85), channel_id=1, source_target_pairs={{0,4},{4,0},{8,12},{12,8},{16,20},{20,16},{24,28},{28,24},{32,36},... | collective-permute-start | bytes 786440 | tf_op jit(solution)/shard_map/ppermute | solution.py:356
  99.7 35.2 %collective-permute-start.27 = (f32[4,16,1024]{2,1,0:T(8,128)S(1)}, f32[4,16,1024]{2,1,0:T(8,128)S(1)}, u32[]{:S(2)}, u32[]{:S(2)}) collective-permute-start(f32[4,16,1024]{2,1,0:T(8,128)S(1)} %get-tuple-element.86), channel_id=1, source_target_pairs={{4,8},{8,4},{12,16},{16,12},{20,24},{24,20},{28,32},{32,28},{36,40... | collective-permute-start | bytes 786440 | tf_op jit(solution)/shard_map/ppermute | solution.py:361
  131.5 7.6 %collective-permute-start.25 = (bf16[4,16,1024]{2,1,0:T(8,128)(2,1)S(1)}, bf16[4,16,1024]{2,1,0:T(8,128)(2,1)S(1)}, u32[]{:S(2)}, u32[]{:S(2)}) collective-permute-start(bf16[4,16,1024]{2,1,0:T(8,128)(2,1)S(1)} %shard_map.87.s0), channel_id=1, source_target_pairs={{0,3},{1,2},{2,1},{3,0},{4,7},{5,6},{6,5},{7,4},{8,11},{9,10},{10,... | collective-permute-start | bytes 393224 | tf_op jit(solution)/shard_map/ppermute | solution.py:352
  132.4 7.9 %collective-permute-start.24 = (bf16[4,16,1024]{2,1,0:T(8,128)(2,1)S(1)}, bf16[4,16,1024]{2,1,0:T(8,128)(2,1)S(1)}, u32[]{:S(2)}, u32[]{:S(2)}) collective-permute-start(bf16[4,16,1024]{2,1,0:T(8,128)(2,1)S(1)} %shard_map.87.s0), channel_id=1, source_target_pairs={{0,2},{1,3},{2,0},{3,1},{4,6},{5,7},{6,4},{7,5},{8,10},{9,11},{10,... | collective-permute-start | bytes 393224 | tf_op jit(solution)/shard_map/ppermute | solution.py:352
  132.7 7.7 %collective-permute-start.23 = (bf16[4,16,1024]{2,1,0:T(8,128)(2,1)S(1)}, bf16[4,16,1024]{2,1,0:T(8,128)(2,1)S(1)}, u32[]{:S(2)}, u32[]{:S(2)}) collective-permute-start(bf16[4,16,1024]{2,1,0:T(8,128)(2,1)S(1)} %shard_map.87.s0), channel_id=1, source_target_pairs={{0,1},{1,0},{2,3},{3,2},{4,5},{5,4},{6,7},{7,6},{8,9},{9,8},{10,11... | collective-permute-start | bytes 393224 | tf_op jit(solution)/shard_map/ppermute | solution.py:352
  135.2 9.6 %collective-permute-start.30 = (bf16[4,16,1024]{2,1,0:T(8,128)(2,1)S(1)}, bf16[4,16,1024]{2,1,0:T(8,128)(2,1)S(1)}, u32[]{:S(2)}, u32[]{:S(2)}) collective-permute-start(bf16[4,16,1024]{2,1,0:T(8,128)(2,1)S(1)} %shard_map.90.s0), channel_id=1, source_target_pairs={{0,3},{1,2},{2,1},{3,0},{4,7},{5,6},{6,5},{7,4},{8,11},{9,10},{10,... | collective-permute-start | bytes 393224 | tf_op jit(solution)/shard_map/ppermute | solution.py:352
  136.1 8.7 %collective-permute-start.29 = (bf16[4,16,1024]{2,1,0:T(8,128)(2,1)S(1)}, bf16[4,16,1024]{2,1,0:T(8,128)(2,1)S(1)}, u32[]{:S(2)}, u32[]{:S(2)}) collective-permute-start(bf16[4,16,1024]{2,1,0:T(8,128)(2,1)S(1)} %shard_map.90.s0), channel_id=1, source_target_pairs={{0,2},{1,3},{2,0},{3,1},{4,6},{5,7},{6,4},{7,5},{8,10},{9,11},{10,... | collective-permute-start | bytes 393224 | tf_op jit(solution)/shard_map/ppermute | solution.py:352
  139.1 6.9 %collective-permute-start.28 = (bf16[4,16,1024]{2,1,0:T(8,128)(2,1)S(1)}, bf16[4,16,1024]{2,1,0:T(8,128)(2,1)S(1)}, u32[]{:S(2)}, u32[]{:S(2)}) collective-permute-start(bf16[4,16,1024]{2,1,0:T(8,128)(2,1)S(1)} %shard_map.90.s0), channel_id=1, source_target_pairs={{0,1},{1,0},{2,3},{3,2},{4,5},{5,4},{6,7},{7,6},{8,9},{9,8},{10,11... | collective-permute-start | bytes 393224 | tf_op jit(solution)/shard_map/ppermute | solution.py:352
  (11 other events, 97.6 us)

commit v4 on v3

--- a/solution.py
+++ b/solution.py
@@ -10,15 +10,16 @@
 F32 = jnp.float32
 BF16 = jnp.bfloat16
 ANG = 4
+ORDER = (0, 2, 3, 1)
 PAIR = 2
 L = 16
 X = 4096
 Q = X // ANG
 UB = 32
 ZD = 4
-AHEAD = 3
 CH = 128
 COEF = 3 * 128
+CHUNK = 16
 GROUP = 8
 VMEM = pl.BlockSpec(memory_space=pltpu.VMEM)
 SMEM = pl.BlockSpec(memory_space=pltpu.SMEM)
@@ -71,12 +72,12 @@
 
 def send_shares(me, acc, outs):
     for r in range(ANG):
-        quarter = me ^ r
+        quarter = me ^ ORDER[r]
         share = acc[:, :, pl.ds(pl.multiple_of(quarter * Q, Q), Q)]
         outs[r][:, :, :Q] = share.astype(outs[r].dtype)
 
 
-def open_inputs(me, rows_hbm, reach_hbm, cols_hbm, p_hbm, inner, own, outer, cols, p, rows, reach, sem):
+def open_inputs(parity, rows_hbm, reach_hbm, cols_hbm, p_hbm, inner, own, outer, flag, cols, p, rows, reach, sem):
     copies = [
         pltpu.make_async_copy(src, dst, sem.at[at])
         for at, (src, dst) in enumerate(((rows_hbm, rows), (reach_hbm, reach), (cols_hbm, cols), (p_hbm, p)))
@@ -85,7 +86,8 @@
         copy.start()
     copies[0].wait()
     copies[1].wait()
-    even = me[1] == 0
+    flag[...] = jnp.full((L, 128), parity[0], jnp.int32)
+    even = parity[0] == 0
     for i in range(PAIR):
         for z in range(ZD):
             top = jnp.where(reach[i, 0, 1] == 1, rows[i, 0, 2, 0, z], 0.0)
@@ -98,26 +100,22 @@
     copies[3].wait()
 
 
-def back_kernel(me_ref, cols, own, inner, outer, p_ref, w_hbm, o0, o1, o2, o3, w, acc, sem):
+def back_kernel(me_ref, cols, flag, own, inner, outer, p_ref, w_hbm, o0, o1, o2, o3, w, acc, sem):
     copies = []
     for a in range(PAIR):
-        for g in range(UB // GROUP):
-            span = pl.ds(GROUP * g, GROUP)
+        for g in range(UB // CHUNK):
+            span = pl.ds(CHUNK * g, CHUNK)
             copies.append(pltpu.make_async_copy(w_hbm.at[a, span], w.at[a, span], sem.at[a, g]))
-    for copy in copies[:AHEAD]:
-        copy.start()
+            copies[-1].start()
     acc[...] = jnp.zeros_like(acc)
     for a in range(PAIR):
         for block in range(UB):
-            at = (a * UB + block) // GROUP
-            if block % GROUP == 0:
-                copies[at].wait()
-                if at + AHEAD < len(copies):
-                    copies[at + AHEAD].start()
+            if block % CHUNK == 0:
+                copies[(a * UB + block) // CHUNK].wait()
             back_block(a, block, p_ref[a, 0, :, 128 * block:128 * (block + 1)], cols, w, acc)
     outs = (o0, o1, o2, o3)
     send_shares(me_ref[0], acc, outs)
-    even = me_ref[1] == 0
+    even = flag[:8] == 0
     from_low = jnp.where(even, outer[...], inner[...])
     from_high = jnp.where(even, inner[...], outer[...])
     for i in range(PAIR):
@@ -148,7 +146,7 @@
 
 def gather_shares(me, shares, place):
     for r in range(ANG):
-        quarter = me ^ r
+        quarter = me ^ ORDER[r]
         place(pl.ds(pl.multiple_of(quarter * Q, Q), Q), shares[r])
 
 
@@ -167,7 +165,7 @@
 
 
 def second_kernel(me_ref, cols, h0, h1, h2, h3, q0_ref, gamma_ref, curve_ref, inner_ref, w,
-                  o0, o1, o2, o3, w_out, hb, acc):
+                  o0, o1, o2, o3, w_out, sums, hb, acc):
 
     def place(at, share):
         hb[:, :, at] = share[...]
@@ -184,8 +182,7 @@
     row = jnp.zeros((1, 128), F32)
     for at, value in enumerate((gamma_ref[...], curve_ref[...], inner_ref[:8], inner_ref[8:], cross, own)):
         row = jnp.where(lane == at, jnp.sum(value), row)
-    for out in (o0, o1, o2, o3):
-        out[:, :, Q:] = jnp.broadcast_to(row[None], (PAIR, L, 128))
+    sums[...] = jnp.broadcast_to(row[None], sums.shape)
 
 
 def spread_slices(coefs, parts, cut):
@@ -199,111 +196,97 @@
     return totals
 
 
+def is_even(flag, columns=CH):
+    return jnp.concatenate([flag[...]] * (columns // 128), axis=1) == 0
+
+
 def cuts():
     return [pl.ds(at * CH, CH) for at in range(Q // CH)]
 
 
-def combine_parts(coefs, parts, mine, sent):
+def combine_parts(flag, coefs, parts, mine, sent):
+    even = is_even(flag)
     for cut in cuts():
-        for e, total in enumerate(spread_slices(coefs, parts, cut)):
+        totals = spread_slices(coefs, parts, cut)
+        for e, total in enumerate(totals):
             mine[e, :, cut] = total
-            sent[e, :, cut] = total.astype(BF16)
-
-
-def open_kernel(c0, c1, c2, c3, mine, sent, coefs):
+        for z in range(ZD):
+            sent[z, :, cut] = totals[4 + z].astype(BF16)
+            sent[ZD + z, :, cut] = jnp.where(even, totals[8 + z], totals[z]).astype(BF16)
+
+
+def open_kernel(flag, c0, c1, c2, c3, mine, sent, coefs):
     parts = (c0, c1, c2, c3)
     for r in range(ANG):
         for i in range(PAIR):
             value = parts[r][i, :, Q:Q + 128].astype(F32)
             value = value + parts[r][i, :, Q + 128:Q + 256].astype(F32)
             coefs[r, i] = value + parts[r][i, :, Q + 256:].astype(F32)
-    combine_parts(coefs, parts, mine, sent)
-
-
-def combine_kernel(coefs, c0, c1, c2, c3, mine, sent):
-    combine_parts(coefs, (c0, c1, c2, c3), mine, sent)
-
-
-def edge_kernel(me, mine, other, sent):
-    for parity, outer, facing in ((0, 0, 0), (1, 8, 8)):
-        @pl.when(me[1] == parity)
-        def _(outer=outer, facing=facing):
-            for z in range(ZD):
-                sent[z] = (mine[4 + z] + other[facing + z].astype(F32)).astype(BF16)
-                sent[ZD + z] = mine[outer + z].astype(BF16)
-
-
-def pieces_body(me, coefs, mine, other, outer, inner, g_out, outs, begin, note, end):
-    def get(ref, z, cut):
-        return ref[z, :, cut].astype(F32)
-
-    def even_cells(cut):
-        below = [mine[z, :, cut] + get(outer, z, cut) for z in range(ZD)]
-        own = [mine[4 + z, :, cut] + get(other, z, cut) + get(outer, 4 + z, cut) for z in range(ZD)]
-        above = [mine[8 + z, :, cut] + get(other, 4 + z, cut) + get(inner, 4 + z, cut) for z in range(ZD)]
-        return below, own, above
-
-    def odd_cells(cut):
-        below = [mine[z, :, cut] + get(other, 4 + z, cut) + get(inner, 4 + z, cut) for z in range(ZD)]
-        own = [mine[4 + z, :, cut] + get(other, 8 + z, cut) + get(outer, 4 + z, cut) for z in range(ZD)]
-        above = [mine[8 + z, :, cut] + get(outer, z, cut) for z in range(ZD)]
-        return below, own, above
-
-    for parity, cells_of in ((0, even_cells), (1, odd_cells)):
-        @pl.when(me[1] == parity)
-        def _(cells_of=cells_of):
-            kept = begin()
-            for cut in cuts():
-                below, own, above = cells_of(cut)
-                for z in range(ZD):
-                    g_out[z, :, cut] = own[z]
-                    kept = note(kept, z, cut, own[z])
-                cells = below + own + above
-                for r in range(ANG):
-                    for i in range(PAIR):
-                        total = None
-                        for e in range(12):
-                            term = coefs[r, i, e:e + 1, :] * cells[e]
-                            total = term if total is None else total + term
-                        outs[r][i, :, cut] = total.astype(outs[r].dtype)
-            end(kept)
-
-
-def pieces_first(me, coefs, mine, other, outer, inner, g_out, h0, h1, h2, h3, dots):
+    combine_parts(flag, coefs, parts, mine, sent)
+
+
+def combine_kernel(flag, coefs, c0, c1, c2, c3, mine, sent):
+    combine_parts(flag, coefs, (c0, c1, c2, c3), mine, sent)
+
+
+def edge_kernel(flag, mine, other, sent):
+    even = is_even(flag, Q)
+    for z in range(ZD):
+        sent[z] = (mine[4 + z] + other[ZD + z].astype(F32)).astype(BF16)
+        sent[ZD + z] = jnp.where(even, mine[z], mine[8 + z]).astype(BF16)
+
+
+def pieces_body(flag, coefs, mine, other, outer, inner, g_out, outs, kept, note):
+    even = is_even(flag)
+    for cut in cuts():
+        def get(ref, z):
+            return ref[z, :, cut].astype(F32)
+
+        cells = [None] * 12
+        for z in range(ZD):
+            beyond = get(outer, z)
+            beside = get(other, z) + get(inner, 4 + z)
+            cells[z] = mine[z, :, cut] + jnp.where(even, beyond, beside)
+            cells[4 + z] = mine[4 + z, :, cut] + get(other, 4 + z) + get(outer, 4 + z)
+            cells[8 + z] = mine[8 + z, :, cut] + jnp.where(even, beside, beyond)
+            g_out[z, :, cut] = cells[4 + z]
+            kept = note(kept, z, cut, cells[4 + z])
+        for r in range(ANG):
+            for i in range(PAIR):
+                total = None
+                for e in range(12):
+                    term = coefs[r, i, e:e + 1, :] * cells[e]
+                    total = term if total is None else total + term
+                outs[r][i, :, cut] = total.astype(outs[r].dtype)
+    return kept
+
+
+def pieces_first(flag, coefs, mine, other, outer, inner, g_out, h0, h1, h2, h3, dots):
     def note(kept, z, cut, value):
         return kept + fold(value * value)
 
-    def end(kept):
-        dots[...] = kept
-
-    pieces_body(me, coefs, mine, other, outer, inner, g_out, (h0, h1, h2, h3),
-                lambda: jnp.zeros((8, 128), F32), note, end)
-
-
-def pieces_second(me, coefs, g0, mine, other, outer, inner, g_out, h0, h1, h2, h3, dots):
+    dots[...] = pieces_body(
+        flag, coefs, mine, other, outer, inner, g_out, (h0, h1, h2, h3), jnp.zeros((8, 128), F32), note
+    )
+
+
+def pieces_second(flag, coefs, g0, mine, other, outer, inner, g_out, h0, h1, h2, h3, dots):
     def note(kept, z, cut, value):
         return kept[0] + fold(value * g0[z, :, cut]), kept[1] + fold(value * value)
 
-    def end(kept):
-        dots[:8] = kept[0]
-        dots[8:] = kept[1]
-
-    pieces_body(me, coefs, mine, other, outer, inner, g_out, (h0, h1, h2, h3),
-                lambda: (jnp.zeros((8, 128), F32),) * 2, note, end)
-
-
-def last_kernel(me, coefs, c0, c1, c2, c3, own, inner, outer, sums):
-    row = (c0[0, :1, Q:] + c1[0, :1, Q:]) + (c2[0, :1, Q:] + c3[0, :1, Q:])
-    sums[...] = jnp.broadcast_to(row[None], sums.shape)
-    for parity, far, near in ((0, 0, 8), (1, 8, 0)):
-        @pl.when(me[1] == parity)
-        def _(far=far, near=near):
-            for cut in cuts():
-                totals = spread_slices(coefs, (c0, c1, c2, c3), cut)
-                for z in range(ZD):
-                    outer[z, :, cut] = totals[far + z]
-                    own[z, :, cut] = totals[4 + z]
-                    inner[z, :, cut] = totals[near + z]
+    dots[:8], dots[8:] = pieces_body(
+        flag, coefs, mine, other, outer, inner, g_out, (h0, h1, h2, h3), (jnp.zeros((8, 128), F32),) * 2, note
+    )
+
+
+def last_kernel(flag, coefs, c0, c1, c2, c3, own, inner, outer):
+    even = is_even(flag)
+    for cut in cuts():
+        totals = spread_slices(coefs, (c0, c1, c2, c3), cut)
+        for z in range(ZD):
+            own[z, :, cut] = totals[4 + z]
+            inner[z, :, cut] = jnp.where(even, totals[8 + z], totals[z])
+            outer[z, :, cut] = jnp.where(even, totals[z], totals[8 + z])
 
 
 def steps(sums_ref):
@@ -364,22 +347,20 @@
 
 
 def exchange(shares):
-    far = along_ang(shares[2], 2)
-    near = along_ang(shares[1], 1)
-    back = along_ang(shares[3], 3)
-    return (shares[0], near, far, back)
+    return (shares[0],) + tuple(along_ang(shares[i], ORDER[i]) for i in range(1, ANG))
 
 
 def per_device(projections, weights, columns, row_weights, reach):
-    me = jnp.stack([lax.axis_index("ang"), lax.axis_index("slab") % 2]).astype(jnp.int32)
+    me = lax.axis_index("ang").astype(jnp.int32).reshape(1)
+    parity = (lax.axis_index("slab").astype(jnp.int32) & 1).reshape(1)
     row = sds((PAIR * ZD, 128), F32)
-    inner, own, outer, cols, p = call(
-        open_inputs, [row] * 3 + [sds((3, PAIR, UB), jnp.int32), sds(projections.shape, F32)], [SMEM] + [HBM] * 4,
+    inner, own, outer, flag, cols, p = call(
+        open_inputs, [row] * 3 + [sds((L, 128), jnp.int32), sds((3, PAIR, UB), jnp.int32), sds(projections.shape, F32)], [SMEM] + [HBM] * 4,
         [pltpu.SMEM(row_weights.shape, F32), pltpu.SMEM(reach.shape, jnp.int32), pltpu.SemaphoreType.DMA((4,))],
         limit=53,
-    )(me, row_weights, reach, columns.transpose(2, 0, 1), projections)
+    )(parity, row_weights, reach, columns.transpose(2, 0, 1), projections)
     outer = across(outer)
-    edges = (own, on_chip(inner), outer)
+    edges = (flag, own, on_chip(inner), outer)
 
     def share(dtype, more=0):
         return sds((PAIR, L, Q + more), dtype)
@@ -389,47 +370,46 @@
     part_b = sds((ZD, L, Q), BF16)
     acc = pltpu.VMEM((PAIR, L, X), F32)
     macs = 2 * PAIR * L * UB * 384 * 128
-    sent = [sds((3 * ZD, L, Q), F32), sds((3 * ZD, L, Q), BF16)]
+    sent = [sds((3 * ZD, L, Q), F32), sds((2 * ZD, L, Q), BF16)]
 
     def halo(mine, sent):
         other = on_chip(sent)
-        (edge,) = call(edge_kernel, [sds((2 * ZD, L, Q), BF16)], [SMEM] + [VMEM] * 2)(me, mine, other)
+        (edge,) = call(edge_kernel, [sds((2 * ZD, L, Q), BF16)], [VMEM] * 3)(flag, mine, other)
         outer = across(edge)
         return mine, other, outer, on_chip(outer)
 
     *shares, w = call(
         back_kernel, [share(BF16, COEF)] * 4 + [sds((PAIR, UB, 384, 128), BF16)],
-        [SMEM] * 2 + [VMEM] * 4 + [HBM], [acc, pltpu.SemaphoreType.DMA((PAIR, UB // GROUP))],
+        [SMEM] * 2 + [VMEM] * 5 + [HBM], [acc, pltpu.SemaphoreType.DMA((PAIR, UB // CHUNK))],
         flops=2 * macs, nbytes=7_000_000, limit=46,
     )(me, cols, *edges, p, weights.reshape(PAIR, UB, 384, 128))
     *spread, coefs = call(
-        open_kernel, sent + [sds((ANG, PAIR, L, 128), F32)], [VMEM] * 4, flops=10_000_000
-    )(*exchange(shares))
+        open_kernel, sent + [sds((ANG, PAIR, L, 128), F32)], [VMEM] * 5, flops=10_000_000
+    )(flag, *exchange(shares))
     g0, *shares, gamma = call(
-        pieces_first, [part] + [share(BF16)] * 4 + [sds((8, 128), F32)], [SMEM] + [VMEM] * 5, flops=10_000_000
-    )(me, coefs, *halo(*spread))
+        pieces_first, [part] + [share(BF16)] * 4 + [sds((8, 128), F32)], [VMEM] * 6, flops=10_000_000
+    )(flag, coefs, *halo(*spread))
 
     *shares, q0, curve = call(
         first_kernel, [share(MID)] * 4 + [full, sds((8, 128), F32)],
         [SMEM] * 2 + [VMEM] * 5, [pltpu.VMEM((PAIR, L, X), BF16), acc],
         flops=3 * macs, nbytes=7_000_000,
     )(me, cols, *exchange(shares), w)
-    spread = call(combine_kernel, sent, [VMEM] * 5, flops=10_000_000)(coefs, *exchange(shares))
+    spread = call(combine_kernel, sent, [VMEM] * 6, flops=10_000_000)(flag, coefs, *exchange(shares))
     z0, *shares, inner = call(
-        pieces_second, [part] + [share(BF16)] * 4 + [sds((16, 128), F32)], [SMEM] + [VMEM] * 6, flops=10_000_000
-    )(me, coefs, g0, *halo(*spread))
-
-    *shares, w0 = call(
-        second_kernel, [share(F32, 128)] * 4 + [full],
+        pieces_second, [part] + [share(BF16)] * 4 + [sds((16, 128), F32)], [VMEM] * 7, flops=10_000_000
+    )(flag, coefs, g0, *halo(*spread))
+
+    *shares, w0, sums = call(
+        second_kernel, [share(F32)] * 4 + [full, sds((lax.axis_size("slab") * ANG, 1, 128), F32)],
         [SMEM] * 2 + [VMEM] * 9, [pltpu.VMEM((PAIR, L, X), BF16), acc],
         flops=4 * macs, nbytes=9_000_000,
     )(me, cols, *exchange(shares), q0, gamma, curve, inner, w)
-    own, inner, outer, sums = call(
-        last_kernel, [part] * 3 + [sds((lax.axis_size("slab"), 1, 128), F32)], [SMEM] + [VMEM] * 5, flops=10_000_000
-    )(me, coefs, *exchange(shares))
+    shares = exchange(shares)
+    sums = lax.all_to_all(sums, ("slab", "ang"), 0, 0, tiled=True)
+    own, inner, outer = call(last_kernel, [part] * 3, [VMEM] * 6, flops=10_000_000)(flag, coefs, *shares)
     outer = across(outer)
     inner = on_chip(inner)
-    sums = lax.all_to_all(sums, "slab", 0, 0, tiled=True)
     (volume,) = call(volume_kernel, [part_b], [VMEM] * 3)(sums, g0, z0)
     (residual,) = call(residual_kernel, [sds(projections.shape, F32)], [VMEM] * 4)(sums, projections, q0, w0)
     volume = exchange((volume,) * 4)

time: 149 us -> 134 us (0.90)
  blocking collectives: 28.4 us -> 0 us
  starting transfers between devices: 48.1 us -> 64.5 us
  Pallas kernels: 25.6 us -> 22.6 us
    all_to_all x1 -> x0, blocking collectives: 28.4 us -> none  [per_device(): sums = lax.all_to_all(sums, 'slab', 0, 0, tiled=True)]
    all_to_all x0 -> x1, starting transfers between devices: none -> 22.7 us  [per_device(): sums = lax.all_to_all(sums, ('slab', 'ang'), 0, 0, tiled=True)]
    all_to_all x0 -> x1, waiting for transfers between devices: none -> 7.55 us  [per_device(): sums = lax.all_to_all(sums, ('slab', 'ang'), 0, 0, tiled=True)]
    ppermute x21, waiting for transfers between devices: 25.4 us -> 19.3 us  [along_ang(): return lax.ppermute(value, 'ang', [(i, i ^ other) for i in range(ANG)])]
    ppermute x4, starting transfers between devices: 14.9 us -> 11.9 us  [across(): lax.ppermute(value, 'slab', [pair for i in range(1, count - 1, 2) for pai...]
    ppermute x21, starting transfers between devices: 24.9 us -> 22.5 us  [along_ang(): return lax.ppermute(value, 'ang', [(i, i ^ other) for i in range(ANG)])]
    pallas_call x8, Pallas kernels: 10.1 us -> 8.46 us  [the longest x1 4.68 us: per_device(): call(second_kernel, [share(F32)] * 4 + [full, sds((lax.axis_size('slab')...]
  transfers between devices with their start and end apart: 31 -> 32, of which waited for: 21 -> 19; matrix products, arithmetic and copies ran while one was open for 0% -> 0% of each run, Pallas kernels for 2% -> 3%
where the time goes in v4:
time: 134 us
  starting transfers between devices  64.5 us (48%)
  waiting for transfers between devices  43.6 us (33%)
  Pallas kernels  22.6 us (17%)
  local copies, waits for them, and re-layouts  2.05 us (2%)
    all_to_all x1, starting transfers between devices, per_device(): sums = lax.all_to_all(sums, ('slab', 'ang'), 0, 0, tiled=True)  22.7 us
    ppermute x21, starting transfers between devices, along_ang(): return lax.ppermute(value, 'ang', [(i, i ^ other) for i in range(ANG)])  22.5 us
    ppermute x21, waiting for transfers between devices, along_ang(): return lax.ppermute(value, 'ang', [(i, i ^ other) for i in range(ANG)])  19.3 us
    ppermute x4, starting transfers between devices, across(): lax.ppermute(value, 'slab', [pair for i in range(1, count - 1, 2) for pai...  11.9 us
    ppermute x4, waiting for transfers between devices, across(): lax.ppermute(value, 'slab', [pair for i in range(1, count - 1, 2) for pai...  11.1 us
    all_to_all x1, waiting for transfers between devices, per_device(): sums = lax.all_to_all(sums, ('slab', 'ang'), 0, 0, tiled=True)  7.55 us
    ppermute x6, starting transfers between devices, on_chip(): lax.ppermute(value, 'slab', [(i, i ^ 1) for i in range(lax.axis_size('sla...  7.49 us
    ppermute x6, waiting for transfers between devices, on_chip(): lax.ppermute(value, 'slab', [(i, i ^ 1) for i in range(lax.axis_size('sla...  5.75 us
  transfers between devices with their start and end apart: 32, of which 19 were waited for; matrix products, arithmetic and copies ran while one was open for 0% of the time, Pallas kernels for 3%

profile of v4, /device:TPU:1, one launch (start us, length us, event | category | flops | bytes accessed | tf_op | source)
XLA Modules:
  0.0 133.6 jit_solution(8765466771618323079)
XLA Ops:
  3.8 3.3 %collective-permute-start = (f32[8,128]{1,0:T(8,128)S(1)}, f32[8,128]{1,0:T(8,128)S(1)}, u32[]{:S(2)}, u32[]{:S(2)}) collective-permute-start(f32[8,128]{1,0:T(8,128)S(1)} %get-tuple-element.49), channel_id=1, source_target_pairs={{0,4},{4,0},{8,12},{12,8},{16,20},{20,16},{24,28},{28,24},{32,36},... | collective-permute-start | bytes 12296 | tf_op jit(solution)/shard_map/ppermute | solution.py:339
  7.1 1.9 %collective-permute-start.1 = (f32[8,128]{1,0:T(8,128)S(1)}, f32[8,128]{1,0:T(8,128)S(1)}, u32[]{:S(2)}, u32[]{:S(2)}) collective-permute-start(f32[8,128]{1,0:T(8,128)S(1)} %get-tuple-element.50), channel_id=1, source_target_pairs={{4,8},{8,4},{12,16},{16,12},{20,24},{24,20},{28,32},{32,28},{36,40... | collective-permute-start | bytes 12296 | tf_op jit(solution)/shard_map/ppermute | solution.py:344
  9.0 3.0 %collective-permute-done.1.outer = f32[8,128]{1,0:T(8,128)S(1)} collective-permute-done((f32[8,128]{1,0:T(8,128)S(1)}, f32[8,128]{1,0:T(8,128)S(1)}, u32[]{:S(2)}, u32[]{:S(2)}) %collective-permute-start.1) | collective-permute-done | bytes 4128 | tf_op jit(solution)/shard_map/ppermute | solution.py:344
  12.0 4.8 %shard_map.77 = (bf16[2,16,1408]{2,1,0:T(8,128)(2,1)S(1)}, bf16[2,16,1408]{2,1,0:T(8,128)(2,1)S(1)}, bf16[2,16,1408]{2,1,0:T(8,128)(2,1)S(1)}, bf16[2,16,1408]{2...) custom-call(s32[1]{0:T(128)} %bitcast.me_ref, s32[3,2,32]{2,1,0:T(2,128)S(1)} %get-tuple-element.46.cols, ...), custom_call_target="tpu_custom_call" | custom-call | flops 201326592 | bytes 7000000 | tf_op jit(solution)/shard_map/pallas_call | solution.py:381
  19.6 2.6 %collective-permute-done.2.c1 = bf16[2,16,1408]{2,1,0:T(8,128)(2,1)S(1)} collective-permute-done((bf16[2,16,1408]{2,1,0:T(8,128)(2,1)S(1)}, bf16[2,16,1408]{2,1,0:T(8,128)(2,1)S(1)}, u32[]{:S(2)}, u32[]{:S(2)}) %collective-permute-start.2) | collective-permute-done | bytes 90144 | tf_op jit(solution)/shard_map/ppermute | solution.py:335
  25.3 4.3 %collective-permute-start.6 = (bf16[8,16,1024]{2,1,0:T(8,128)(2,1)S(1)}, bf16[8,16,1024]{2,1,0:T(8,128)(2,1)S(1)}, u32[]{:S(2)}, u32[]{:S(2)}) collective-permute-start(bf16[8,16,1024]{2,1,0:T(8,128)(2,1)S(1)} %shard_map.79), channel_id=1, source_target_pairs={{4,8},{8,4},{12,16},{16,12},{20,24},{24,20},{28,32},{32,28},{36,40... | collective-permute-start | bytes 786440 | tf_op jit(solution)/shard_map/ppermute | solution.py:344
  29.6 4.0 %collective-permute-done.6.outer = bf16[8,16,1024]{2,1,0:T(8,128)(2,1)S(1)} collective-permute-done((bf16[8,16,1024]{2,1,0:T(8,128)(2,1)S(1)}, bf16[8,16,1024]{2,1,0:T(8,128)(2,1)S(1)}, u32[]{:S(2)}, u32[]{:S(2)}) %collective-permute-start.6) | collective-permute-done | bytes 262176 | tf_op jit(solution)/shard_map/ppermute | solution.py:344
  39.0 1.9 %collective-permute-done.8.h1 = bf16[2,16,1024]{2,1,0:T(8,128)(2,1)S(1)} collective-permute-done((bf16[2,16,1024]{2,1,0:T(8,128)(2,1)S(1)}, bf16[2,16,1024]{2,1,0:T(8,128)(2,1)S(1)}, u32[]{:S(2)}, u32[]{:S(2)}) %collective-permute-start.8) | collective-permute-done | bytes 65568 | tf_op jit(solution)/shard_map/ppermute | solution.py:335
  42.4 4.1 %shard_map.81 = (bf16[2,16,1024]{2,1,0:T(8,128)(2,1)S(1)}, bf16[2,16,1024]{2,1,0:T(8,128)(2,1)S(1)}, bf16[2,16,1024]{2,1,0:T(8,128)(2,1)S(1)}, bf16[2,16,1024]{2...) custom-call(s32[1]{0:T(128)} %bitcast.me_ref, s32[3,2,32]{2,1,0:T(2,128)S(1)} %get-tuple-element.46.cols, ...), custom_call_target="tpu_custom_call" | custom-call | flops 301989888 | bytes 7000000 | tf_op jit(solution)/shard_map/pallas_call | solution.py:393
  46.5 1.9 %collective-permute-start.11 = (bf16[2,16,1024]{2,1,0:T(8,128)(2,1)S(1)}, bf16[2,16,1024]{2,1,0:T(8,128)(2,1)S(1)}, u32[]{:S(2)}, u32[]{:S(2)}) collective-permute-start(bf16[2,16,1024]{2,1,0:T(8,128)(2,1)S(1)} %get-tuple-element.66), channel_id=1, source_target_pairs={{0,2},{1,3},{2,0},{3,1},{4,6},{5,7},{6,4},{7,5},{8,10},{9,11},{10,... | collective-permute-start | bytes 196616 | tf_op jit(solution)/shard_map/ppermute | solution.py:335
  51.3 2.4 %collective-permute-done.12.c2 = bf16[2,16,1024]{2,1,0:T(8,128)(2,1)S(1)} collective-permute-done((bf16[2,16,1024]{2,1,0:T(8,128)(2,1)S(1)}, bf16[2,16,1024]{2,1,0:T(8,128)(2,1)S(1)}, u32[]{:S(2)}, u32[]{:S(2)}) %collective-permute-start.12) | collective-permute-done | bytes 65568 | tf_op jit(solution)/shard_map/ppermute | solution.py:335
  54.1 1.9 %collective-permute-start.14 = (bf16[8,16,1024]{2,1,0:T(8,128)(2,1)S(1)}, bf16[8,16,1024]{2,1,0:T(8,128)(2,1)S(1)}, u32[]{:S(2)}, u32[]{:S(2)}) collective-permute-start(bf16[8,16,1024]{2,1,0:T(8,128)(2,1)S(1)} %get-tuple-element.70), channel_id=1, source_target_pairs={{0,4},{4,0},{8,12},{12,8},{16,20},{20,16},{24,28},{28,24},{32,36},... | collective-permute-start | bytes 786440 | tf_op jit(solution)/shard_map/ppermute | solution.py:339
  57.3 3.8 %collective-permute-start.15 = (bf16[8,16,1024]{2,1,0:T(8,128)(2,1)S(1)}, bf16[8,16,1024]{2,1,0:T(8,128)(2,1)S(1)}, u32[]{:S(2)}, u32[]{:S(2)}) collective-permute-start(bf16[8,16,1024]{2,1,0:T(8,128)(2,1)S(1)} %shard_map.83), channel_id=1, source_target_pairs={{4,8},{8,4},{12,16},{16,12},{20,24},{24,20},{28,32},{32,28},{36,40... | collective-permute-start | bytes 786440 | tf_op jit(solution)/shard_map/ppermute | solution.py:344
  61.0 4.0 %collective-permute-done.15.outer = bf16[8,16,1024]{2,1,0:T(8,128)(2,1)S(1)} collective-permute-done((bf16[8,16,1024]{2,1,0:T(8,128)(2,1)S(1)}, bf16[8,16,1024]{2,1,0:T(8,128)(2,1)S(1)}, u32[]{:S(2)}, u32[]{:S(2)}) %collective-permute-start.15) | collective-permute-done | bytes 262176 | tf_op jit(solution)/shard_map/ppermute | solution.py:344
  70.2 2.2 %collective-permute-done.17.h1 = bf16[2,16,1024]{2,1,0:T(8,128)(2,1)S(1)} collective-permute-done((bf16[2,16,1024]{2,1,0:T(8,128)(2,1)S(1)}, bf16[2,16,1024]{2,1,0:T(8,128)(2,1)S(1)}, u32[]{:S(2)}, u32[]{:S(2)}) %collective-permute-start.17) | collective-permute-done | bytes 65568 | tf_op jit(solution)/shard_map/ppermute | solution.py:335
  73.8 4.7 %shard_map.85 = (f32[2,16,1024]{2,1,0:T(8,128)S(1)}, f32[2,16,1024]{2,1,0:T(8,128)S(1)}, f32[2,16,1024]{2,1,0:T(8,128)S(1)}, f32[2,16,1024]{2,1,0:T(8,128)S(1)},...) custom-call(s32[1]{0:T(128)} %bitcast.me_ref, s32[3,2,32]{2,1,0:T(2,128)S(1)} %get-tuple-element.46.cols, ...), custom_call_target="tpu_custom_call" | custom-call | flops 402653184 | bytes 9000000 | tf_op jit(solution)/shard_map/pallas_call | solution.py:403
  78.5 1.8 %collective-permute-start.23 = (f32[2,16,1024]{2,1,0:T(8,128)S(1)}, f32[2,16,1024]{2,1,0:T(8,128)S(1)}, u32[]{:S(2)}, u32[]{:S(2)}) collective-permute-start(f32[2,16,1024]{2,1,0:T(8,128)S(1)} %get-tuple-element.83), channel_id=1, source_target_pairs={{0,2},{1,3},{2,0},{3,1},{4,6},{5,7},{6,4},{7,5},{8,10},{9,11},{10,... | collective-permute-start | bytes 393224 | tf_op jit(solution)/shard_map/ppermute | solution.py:335
  81.8 22.7 %all-to-all-start = ((f32[256,1,128]{2,1,0:T(1,128)}), f32[256,1,128]{2,1,0:T(1,128)S(1)}, u32[]{:S(2)}, u32[]{:S(2)}) async-start(f32[256,1,128]{2,1,0:T(1,128)} %get-tuple-element.79), calls=%async_computation | async-start | bytes 262144 | tf_op jit(solution)/shard_map/all_to_all | solution.py:409
  105.5 2.1 %collective-permute-start.26 = (f32[4,16,1024]{2,1,0:T(8,128)}, f32[4,16,1024]{2,1,0:T(8,128)S(1)}, u32[]{:S(2)}, u32[]{:S(2)}) collective-permute-start(f32[4,16,1024]{2,1,0:T(8,128)} %get-tuple-element.87), channel_id=1, source_target_pairs={{0,4},{4,0},{8,12},{12,8},{16,20},{20,16},{24,28},{28,24},{32,36},... | collective-permute-start | bytes 786440 | tf_op jit(solution)/shard_map/ppermute | solution.py:339
  107.7 1.9 %collective-permute-start.27 = (f32[4,16,1024]{2,1,0:T(8,128)S(1)}, f32[4,16,1024]{2,1,0:T(8,128)S(1)}, u32[]{:S(2)}, u32[]{:S(2)}) collective-permute-start(f32[4,16,1024]{2,1,0:T(8,128)S(1)} %get-tuple-element.88), channel_id=1, source_target_pairs={{4,8},{8,4},{12,16},{16,12},{20,24},{24,20},{28,32},{32,28},{36,40... | collective-permute-start | bytes 786440 | tf_op jit(solution)/shard_map/ppermute | solution.py:344
  109.6 7.6 %all-to-all-done.sums = f32[256,1,128]{2,1,0:T(1,128)S(1)} async-done(((f32[256,1,128]{2,1,0:T(1,128)}), f32[256,1,128]{2,1,0:T(1,128)S(1)}, u32[]{:S(2)}, u32[]{:S(2)}) %all-to-all-start) | async-done | bytes 131104 | tf_op jit(solution)/shard_map/all_to_all | solution.py:409
  119.2 1.8 %collective-permute-start.20 = (bf16[4,16,1024]{2,1,0:T(8,128)(2,1)S(1)}, bf16[4,16,1024]{2,1,0:T(8,128)(2,1)S(1)}, u32[]{:S(2)}, u32[]{:S(2)}) collective-permute-start(bf16[4,16,1024]{2,1,0:T(8,128)(2,1)S(1)} %shard_map.86.s0), channel_id=1, source_target_pairs={{0,2},{1,3},{2,0},{3,1},{4,6},{5,7},{6,4},{7,5},{8,10},{9,11},{10,... | collective-permute-start | bytes 393224 | tf_op jit(solution)/shard_map/ppermute | solution.py:335
  123.1 1.8 %collective-permute-start.28 = (bf16[4,16,1024]{2,1,0:T(8,128)(2,1)S(1)}, bf16[4,16,1024]{2,1,0:T(8,128)(2,1)S(1)}, u32[]{:S(2)}, u32[]{:S(2)}) collective-permute-start(bf16[4,16,1024]{2,1,0:T(8,128)(2,1)S(1)} %shard_map.90.s0), channel_id=1, source_target_pairs={{0,2},{1,3},{2,0},{3,1},{4,6},{5,7},{6,4},{7,5},{8,10},{9,11},{10,... | collective-permute-start | bytes 393224 | tf_op jit(solution)/shard_map/ppermute | solution.py:335
  128.2 4.4 %collective-permute-done.29.s2 = bf16[4,16,1024]{2,1,0:T(8,128)(2,1)S(1)} collective-permute-done((bf16[4,16,1024]{2,1,0:T(8,128)(2,1)S(1)}, bf16[4,16,1024]{2,1,0:T(8,128)(2,1)S(1)}, u32[]{:S(2)}, u32[]{:S(2)}) %collective-permute-start.29) | collective-permute-done | bytes 131104 | tf_op jit(solution)/shard_map/ppermute | solution.py:335
  (64 shorter events, 37.8 us)
Async XLA Ops:
  3.8 5.3 %collective-permute-start = (f32[8,128]{1,0:T(8,128)S(1)}, f32[8,128]{1,0:T(8,128)S(1)}, u32[]{:S(2)}, u32[]{:S(2)}) collective-permute-start(f32[8,128]{1,0:T(8,128)S(1)} %get-tuple-element.49), channel_id=1, source_target_pairs={{0,4},{4,0},{8,12},{12,8},{16,20},{20,16},{24,28},{28,24},{32,36},... | collective-permute-start | bytes 12296 | tf_op jit(solution)/shard_map/ppermute | solution.py:339
  7.1 4.9 %collective-permute-start.1 = (f32[8,128]{1,0:T(8,128)S(1)}, f32[8,128]{1,0:T(8,128)S(1)}, u32[]{:S(2)}, u32[]{:S(2)}) collective-permute-start(f32[8,128]{1,0:T(8,128)S(1)} %get-tuple-element.50), channel_id=1, source_target_pairs={{4,8},{8,4},{12,16},{16,12},{20,24},{24,20},{28,32},{32,28},{36,40... | collective-permute-start | bytes 12296 | tf_op jit(solution)/shard_map/ppermute | solution.py:344
  16.9 5.3 %collective-permute-start.2 = (bf16[2,16,1408]{2,1,0:T(8,128)(2,1)S(1)}, bf16[2,16,1408]{2,1,0:T(8,128)(2,1)S(1)}, u32[]{:S(2)}, u32[]{:S(2)}) collective-permute-start(bf16[2,16,1408]{2,1,0:T(8,128)(2,1)S(1)} %get-tuple-element.53), channel_id=1, source_target_pairs={{0,2},{1,3},{2,0},{3,1},{4,6},{5,7},{6,4},{7,5},{8,10},{9,11},{10,... | collective-permute-start | bytes 270344 | tf_op jit(solution)/shard_map/ppermute | solution.py:335
  18.1 5.0 %collective-permute-start.3 = (bf16[2,16,1408]{2,1,0:T(8,128)(2,1)S(1)}, bf16[2,16,1408]{2,1,0:T(8,128)(2,1)S(1)}, u32[]{:S(2)}, u32[]{:S(2)}) collective-permute-start(bf16[2,16,1408]{2,1,0:T(8,128)(2,1)S(1)} %get-tuple-element.54), channel_id=1, source_target_pairs={{0,3},{1,2},{2,1},{3,0},{4,7},{5,6},{6,5},{7,4},{8,11},{9,10},{10,... | collective-permute-start | bytes 270344 | tf_op jit(solution)/shard_map/ppermute | solution.py:335
  25.3 8.3 %collective-permute-start.6 = (bf16[8,16,1024]{2,1,0:T(8,128)(2,1)S(1)}, bf16[8,16,1024]{2,1,0:T(8,128)(2,1)S(1)}, u32[]{:S(2)}, u32[]{:S(2)}) collective-permute-start(bf16[8,16,1024]{2,1,0:T(8,128)(2,1)S(1)} %shard_map.79), channel_id=1, source_target_pairs={{4,8},{8,4},{12,16},{16,12},{20,24},{24,20},{28,32},{32,28},{36,40... | collective-permute-start | bytes 786440 | tf_op jit(solution)/shard_map/ppermute | solution.py:344
  35.8 5.1 %collective-permute-start.8 = (bf16[2,16,1024]{2,1,0:T(8,128)(2,1)S(1)}, bf16[2,16,1024]{2,1,0:T(8,128)(2,1)S(1)}, u32[]{:S(2)}, u32[]{:S(2)}) collective-permute-start(bf16[2,16,1024]{2,1,0:T(8,128)(2,1)S(1)} %get-tuple-element.61), channel_id=1, source_target_pairs={{0,2},{1,3},{2,0},{3,1},{4,6},{5,7},{6,4},{7,5},{8,10},{9,11},{10,... | collective-permute-start | bytes 196616 | tf_op jit(solution)/shard_map/ppermute | solution.py:335
  37.3 5.0 %collective-permute-start.9 = (bf16[2,16,1024]{2,1,0:T(8,128)(2,1)S(1)}, bf16[2,16,1024]{2,1,0:T(8,128)(2,1)S(1)}, u32[]{:S(2)}, u32[]{:S(2)}) collective-permute-start(bf16[2,16,1024]{2,1,0:T(8,128)(2,1)S(1)} %get-tuple-element.62), channel_id=1, source_target_pairs={{0,3},{1,2},{2,1},{3,0},{4,7},{5,6},{6,5},{7,4},{8,11},{9,10},{10,... | collective-permute-start | bytes 196616 | tf_op jit(solution)/shard_map/ppermute | solution.py:335
  46.5 4.7 %collective-permute-start.11 = (bf16[2,16,1024]{2,1,0:T(8,128)(2,1)S(1)}, bf16[2,16,1024]{2,1,0:T(8,128)(2,1)S(1)}, u32[]{:S(2)}, u32[]{:S(2)}) collective-permute-start(bf16[2,16,1024]{2,1,0:T(8,128)(2,1)S(1)} %get-tuple-element.66), channel_id=1, source_target_pairs={{0,2},{1,3},{2,0},{3,1},{4,6},{5,7},{6,4},{7,5},{8,10},{9,11},{10,... | collective-permute-start | bytes 196616 | tf_op jit(solution)/shard_map/ppermute | solution.py:335
  48.5 5.2 %collective-permute-start.12 = (bf16[2,16,1024]{2,1,0:T(8,128)(2,1)S(1)}, bf16[2,16,1024]{2,1,0:T(8,128)(2,1)S(1)}, u32[]{:S(2)}, u32[]{:S(2)}) collective-permute-start(bf16[2,16,1024]{2,1,0:T(8,128)(2,1)S(1)} %get-tuple-element.67), channel_id=1, source_target_pairs={{0,3},{1,2},{2,1},{3,0},{4,7},{5,6},{6,5},{7,4},{8,11},{9,10},{10,... | collective-permute-start | bytes 196616 | tf_op jit(solution)/shard_map/ppermute | solution.py:335
  57.3 7.8 %collective-permute-start.15 = (bf16[8,16,1024]{2,1,0:T(8,128)(2,1)S(1)}, bf16[8,16,1024]{2,1,0:T(8,128)(2,1)S(1)}, u32[]{:S(2)}, u32[]{:S(2)}) collective-permute-start(bf16[8,16,1024]{2,1,0:T(8,128)(2,1)S(1)} %shard_map.83), channel_id=1, source_target_pairs={{4,8},{8,4},{12,16},{16,12},{20,24},{24,20},{28,32},{32,28},{36,40... | collective-permute-start | bytes 786440 | tf_op jit(solution)/shard_map/ppermute | solution.py:344
  67.2 5.1 %collective-permute-start.17 = (bf16[2,16,1024]{2,1,0:T(8,128)(2,1)S(1)}, bf16[2,16,1024]{2,1,0:T(8,128)(2,1)S(1)}, u32[]{:S(2)}, u32[]{:S(2)}) collective-permute-start(bf16[2,16,1024]{2,1,0:T(8,128)(2,1)S(1)} %get-tuple-element.72), channel_id=1, source_target_pairs={{0,2},{1,3},{2,0},{3,1},{4,6},{5,7},{6,4},{7,5},{8,10},{9,11},{10,... | collective-permute-start | bytes 196616 | tf_op jit(solution)/shard_map/ppermute | solution.py:335
  68.7 5.1 %collective-permute-start.18 = (bf16[2,16,1024]{2,1,0:T(8,128)(2,1)S(1)}, bf16[2,16,1024]{2,1,0:T(8,128)(2,1)S(1)}, u32[]{:S(2)}, u32[]{:S(2)}) collective-permute-start(bf16[2,16,1024]{2,1,0:T(8,128)(2,1)S(1)} %get-tuple-element.73), channel_id=1, source_target_pairs={{0,3},{1,2},{2,1},{3,0},{4,7},{5,6},{6,5},{7,4},{8,11},{9,10},{10,... | collective-permute-start | bytes 196616 | tf_op jit(solution)/shard_map/ppermute | solution.py:335
  78.5 26.0 %collective-permute-start.23 = (f32[2,16,1024]{2,1,0:T(8,128)S(1)}, f32[2,16,1024]{2,1,0:T(8,128)S(1)}, u32[]{:S(2)}, u32[]{:S(2)}) collective-permute-start(f32[2,16,1024]{2,1,0:T(8,128)S(1)} %get-tuple-element.83), channel_id=1, source_target_pairs={{0,2},{1,3},{2,0},{3,1},{4,6},{5,7},{6,4},{7,5},{8,10},{9,11},{10,... | collective-permute-start | bytes 393224 | tf_op jit(solution)/shard_map/ppermute | solution.py:335
  80.3 24.2 %collective-permute-start.24 = (f32[2,16,1024]{2,1,0:T(8,128)S(1)}, f32[2,16,1024]{2,1,0:T(8,128)S(1)}, u32[]{:S(2)}, u32[]{:S(2)}) collective-permute-start(f32[2,16,1024]{2,1,0:T(8,128)S(1)} %get-tuple-element.84), channel_id=1, source_target_pairs={{0,3},{1,2},{2,1},{3,0},{4,7},{5,6},{6,5},{7,4},{8,11},{9,10},{10,... | collective-permute-start | bytes 393224 | tf_op jit(solution)/shard_map/ppermute | solution.py:335
  81.8 22.7 %collective-permute-start.25 = (f32[2,16,1024]{2,1,0:T(8,128)S(1)}, f32[2,16,1024]{2,1,0:T(8,128)S(1)}, u32[]{:S(2)}, u32[]{:S(2)}) collective-permute-start(f32[2,16,1024]{2,1,0:T(8,128)S(1)} %get-tuple-element.85), channel_id=1, source_target_pairs={{0,1},{1,0},{2,3},{3,2},{4,5},{5,4},{6,7},{7,6},{8,9},{9,8},{10,11... | collective-permute-start | bytes 393224 | tf_op jit(solution)/shard_map/ppermute | solution.py:335
  81.8 35.4 %all-to-all-start = ((f32[256,1,128]{2,1,0:T(1,128)}), f32[256,1,128]{2,1,0:T(1,128)S(1)}, u32[]{:S(2)}, u32[]{:S(2)}) async-start(f32[256,1,128]{2,1,0:T(1,128)} %get-tuple-element.79), calls=%async_computation | async-start | bytes 262144 | tf_op jit(solution)/shard_map/all_to_all | solution.py:409
  105.5 15.5 %collective-permute-start.26 = (f32[4,16,1024]{2,1,0:T(8,128)}, f32[4,16,1024]{2,1,0:T(8,128)S(1)}, u32[]{:S(2)}, u32[]{:S(2)}) collective-permute-start(f32[4,16,1024]{2,1,0:T(8,128)} %get-tuple-element.87), channel_id=1, source_target_pairs={{0,4},{4,0},{8,12},{12,8},{16,20},{20,16},{24,28},{28,24},{32,36},... | collective-permute-start | bytes 786440 | tf_op jit(solution)/shard_map/ppermute | solution.py:339
  107.7 13.3 %collective-permute-start.27 = (f32[4,16,1024]{2,1,0:T(8,128)S(1)}, f32[4,16,1024]{2,1,0:T(8,128)S(1)}, u32[]{:S(2)}, u32[]{:S(2)}) collective-permute-start(f32[4,16,1024]{2,1,0:T(8,128)S(1)} %get-tuple-element.88), channel_id=1, source_target_pairs={{4,8},{8,4},{12,16},{16,12},{20,24},{24,20},{28,32},{32,28},{36,40... | collective-permute-start | bytes 786440 | tf_op jit(solution)/shard_map/ppermute | solution.py:344
  117.7 5.4 %collective-permute-start.22 = (bf16[4,16,1024]{2,1,0:T(8,128)(2,1)S(1)}, bf16[4,16,1024]{2,1,0:T(8,128)(2,1)S(1)}, u32[]{:S(2)}, u32[]{:S(2)}) collective-permute-start(bf16[4,16,1024]{2,1,0:T(8,128)(2,1)S(1)} %shard_map.86.s0), channel_id=1, source_target_pairs={{0,1},{1,0},{2,3},{3,2},{4,5},{5,4},{6,7},{7,6},{8,9},{9,8},{10,11... | collective-permute-start | bytes 393224 | tf_op jit(solution)/shard_map/ppermute | solution.py:335
  118.1 8.2 %collective-permute-start.21 = (bf16[4,16,1024]{2,1,0:T(8,128)(2,1)S(1)}, bf16[4,16,1024]{2,1,0:T(8,128)(2,1)S(1)}, u32[]{:S(2)}, u32[]{:S(2)}) collective-permute-start(bf16[4,16,1024]{2,1,0:T(8,128)(2,1)S(1)} %shard_map.86.s0), channel_id=1, source_target_pairs={{0,3},{1,2},{2,1},{3,0},{4,7},{5,6},{6,5},{7,4},{8,11},{9,10},{10,... | collective-permute-start | bytes 393224 | tf_op jit(solution)/shard_map/ppermute | solution.py:335
  119.2 7.1 %collective-permute-start.20 = (bf16[4,16,1024]{2,1,0:T(8,128)(2,1)S(1)}, bf16[4,16,1024]{2,1,0:T(8,128)(2,1)S(1)}, u32[]{:S(2)}, u32[]{:S(2)}) collective-permute-start(bf16[4,16,1024]{2,1,0:T(8,128)(2,1)S(1)} %shard_map.86.s0), channel_id=1, source_target_pairs={{0,2},{1,3},{2,0},{3,1},{4,6},{5,7},{6,4},{7,5},{8,10},{9,11},{10,... | collective-permute-start | bytes 393224 | tf_op jit(solution)/shard_map/ppermute | solution.py:335
  121.6 6.7 %collective-permute-start.30 = (bf16[4,16,1024]{2,1,0:T(8,128)(2,1)S(1)}, bf16[4,16,1024]{2,1,0:T(8,128)(2,1)S(1)}, u32[]{:S(2)}, u32[]{:S(2)}) collective-permute-start(bf16[4,16,1024]{2,1,0:T(8,128)(2,1)S(1)} %shard_map.90.s0), channel_id=1, source_target_pairs={{0,1},{1,0},{2,3},{3,2},{4,5},{5,4},{6,7},{7,6},{8,9},{9,8},{10,11... | collective-permute-start | bytes 393224 | tf_op jit(solution)/shard_map/ppermute | solution.py:335
  122.0 10.6 %collective-permute-start.29 = (bf16[4,16,1024]{2,1,0:T(8,128)(2,1)S(1)}, bf16[4,16,1024]{2,1,0:T(8,128)(2,1)S(1)}, u32[]{:S(2)}, u32[]{:S(2)}) collective-permute-start(bf16[4,16,1024]{2,1,0:T(8,128)(2,1)S(1)} %shard_map.90.s0), channel_id=1, source_target_pairs={{0,3},{1,2},{2,1},{3,0},{4,7},{5,6},{6,5},{7,4},{8,11},{9,10},{10,... | collective-permute-start | bytes 393224 | tf_op jit(solution)/shard_map/ppermute | solution.py:335
  123.1 9.5 %collective-permute-start.28 = (bf16[4,16,1024]{2,1,0:T(8,128)(2,1)S(1)}, bf16[4,16,1024]{2,1,0:T(8,128)(2,1)S(1)}, u32[]{:S(2)}, u32[]{:S(2)}) collective-permute-start(bf16[4,16,1024]{2,1,0:T(8,128)(2,1)S(1)} %shard_map.90.s0), channel_id=1, source_target_pairs={{0,2},{1,3},{2,0},{3,1},{4,6},{5,7},{6,4},{7,5},{8,10},{9,11},{10,... | collective-permute-start | bytes 393224 | tf_op jit(solution)/shard_map/ppermute | solution.py:335
  (12 other events, 92.2 us)

commit v5 on v4

--- a/solution.py
+++ b/solution.py
@@ -100,7 +100,7 @@
     copies[3].wait()
 
 
-def back_kernel(me_ref, cols, flag, own, inner, outer, p_ref, w_hbm, o0, o1, o2, o3, w, acc, sem):
+def back_kernel(me_ref, cols, p_ref, w_hbm, o0, o1, o2, o3, w, acc, sem):
     copies = []
     for a in range(PAIR):
         for g in range(UB // CHUNK):
@@ -113,8 +113,13 @@
             if block % CHUNK == 0:
                 copies[(a * UB + block) // CHUNK].wait()
             back_block(a, block, p_ref[a, 0, :, 128 * block:128 * (block + 1)], cols, w, acc)
+    send_shares(me_ref[0], acc, (o0, o1, o2, o3))
+
+
+def stencil_kernel(flag, own, inner, outer, c0, c1, c2, c3, o0, o1, o2, o3):
     outs = (o0, o1, o2, o3)
-    send_shares(me_ref[0], acc, outs)
+    for share, out in zip((c0, c1, c2, c3), outs):
+        out[:, :, :Q] = share[...]
     even = flag[:8] == 0
     from_low = jnp.where(even, outer[...], inner[...])
     from_high = jnp.where(even, inner[...], outer[...])
@@ -379,10 +384,11 @@
         return mine, other, outer, on_chip(outer)
 
     *shares, w = call(
-        back_kernel, [share(BF16, COEF)] * 4 + [sds((PAIR, UB, 384, 128), BF16)],
-        [SMEM] * 2 + [VMEM] * 5 + [HBM], [acc, pltpu.SemaphoreType.DMA((PAIR, UB // CHUNK))],
+        back_kernel, [share(BF16)] * 4 + [sds((PAIR, UB, 384, 128), BF16)],
+        [SMEM] * 2 + [VMEM, HBM], [acc, pltpu.SemaphoreType.DMA((PAIR, UB // CHUNK))],
         flops=2 * macs, nbytes=7_000_000, limit=46,
-    )(me, cols, *edges, p, weights.reshape(PAIR, UB, 384, 128))
+    )(me, cols, p, weights.reshape(PAIR, UB, 384, 128))
+    shares = call(stencil_kernel, [share(BF16, COEF)] * 4, [VMEM] * 8)(*edges, *shares)
     *spread, coefs = call(
         open_kernel, sent + [sds((ANG, PAIR, L, 128), F32)], [VMEM] * 5, flops=10_000_000
     )(flag, *exchange(shares))

time: 134 us -> 130 us (0.970)
  waiting for transfers between devices: 43.6 us -> 41.1 us
  starting transfers between devices: 64.5 us -> 63.1 us
    ppermute x4, waiting for transfers between devices: 11.1 us -> 8.09 us  [across(): lax.ppermute(value, 'slab', [pair for i in range(1, count - 1, 2) for pai...]
    all_to_all x1, starting transfers between devices: 22.7 us -> 20.7 us  [per_device(): sums = lax.all_to_all(sums, ('slab', 'ang'), 0, 0, tiled=True)]
    pallas_call x1 -> x2, Pallas kernels: 4.83 us -> 4.85 us  [the longest x1 4.82 us: per_device(): call(back_kernel, [share(BF16)] * 4 + [sds((PAIR, UB, 384, 128), BF16)],...]
  transfers between devices with their start and end apart: 32 -> 32, of which waited for: 19 -> 17; matrix products, arithmetic and copies ran while one was open for 0% -> 0% of each run, Pallas kernels for 3% -> 7%
where the time goes in v5:
time: 130 us
  starting transfers between devices  63.1 us (49%)
  waiting for transfers between devices  41.1 us (32%)
  Pallas kernels  22.6 us (17%)
  local copies, waits for them, and re-layouts  2.05 us (2%)
    ppermute x21, starting transfers between devices, along_ang(): return lax.ppermute(value, 'ang', [(i, i ^ other) for i in range(ANG)])  22.8 us
    all_to_all x1, starting transfers between devices, per_device(): sums = lax.all_to_all(sums, ('slab', 'ang'), 0, 0, tiled=True)  20.7 us
    ppermute x21, waiting for transfers between devices, along_ang(): return lax.ppermute(value, 'ang', [(i, i ^ other) for i in range(ANG)])  19.7 us
    ppermute x4, starting transfers between devices, across(): lax.ppermute(value, 'slab', [pair for i in range(1, count - 1, 2) for pai...  12.2 us
    ppermute x4, waiting for transfers between devices, across(): lax.ppermute(value, 'slab', [pair for i in range(1, count - 1, 2) for pai...  8.09 us
    all_to_all x1, waiting for transfers between devices, per_device(): sums = lax.all_to_all(sums, ('slab', 'ang'), 0, 0, tiled=True)  7.55 us
    ppermute x6, starting transfers between devices, on_chip(): lax.ppermute(value, 'slab', [(i, i ^ 1) for i in range(lax.axis_size('sla...  7.49 us
    ppermute x6, waiting for transfers between devices, on_chip(): lax.ppermute(value, 'slab', [(i, i ^ 1) for i in range(lax.axis_size('sla...  5.75 us
  transfers between devices with their start and end apart: 32, of which 17 were waited for; matrix products, arithmetic and copies ran while one was open for 0% of the time, Pallas kernels for 7%

profile of v5, /device:TPU:1, one launch (start us, length us, event | category | flops | bytes accessed | tf_op | source)
XLA Modules:
  0.0 129.7 jit_solution(2045208913780337634)
XLA Ops:
  3.8 3.3 %collective-permute-start = (f32[8,128]{1,0:T(8,128)S(1)}, f32[8,128]{1,0:T(8,128)S(1)}, u32[]{:S(2)}, u32[]{:S(2)}) collective-permute-start(f32[8,128]{1,0:T(8,128)S(1)} %get-tuple-element.53), channel_id=1, source_target_pairs={{0,4},{4,0},{8,12},{12,8},{16,20},{20,16},{24,28},{28,24},{32,36},... | collective-permute-start | bytes 12296 | tf_op jit(solution)/shard_map/ppermute | solution.py:344
  7.1 1.9 %collective-permute-start.1 = (f32[8,128]{1,0:T(8,128)S(1)}, f32[8,128]{1,0:T(8,128)S(1)}, u32[]{:S(2)}, u32[]{:S(2)}) collective-permute-start(f32[8,128]{1,0:T(8,128)S(1)} %get-tuple-element.54), channel_id=1, source_target_pairs={{4,8},{8,4},{12,16},{16,12},{20,24},{24,20},{28,32},{32,28},{36,40... | collective-permute-start | bytes 12296 | tf_op jit(solution)/shard_map/ppermute | solution.py:349
  9.0 4.8 %shard_map.77 = (bf16[2,16,1024]{2,1,0:T(8,128)(2,1)S(1)}, bf16[2,16,1024]{2,1,0:T(8,128)(2,1)S(1)}, bf16[2,16,1024]{2,1,0:T(8,128)(2,1)S(1)}, bf16[2,16,1024]{2...) custom-call(s32[1]{0:T(128)} %bitcast.me_ref, s32[3,2,32]{2,1,0:T(2,128)S(1)} %get-tuple-element.50.cols, ...), custom_call_target="tpu_custom_call" | custom-call | flops 201326592 | bytes 7000000 | tf_op jit(solution)/shard_map/pallas_call | solution.py:386
  13.9 2.4 %collective-permute-start.2 = (bf16[2,16,1408]{2,1,0:T(8,128)(2,1)S(1)}, bf16[2,16,1408]{2,1,0:T(8,128)(2,1)S(1)}, u32[]{:S(2)}, u32[]{:S(2)}) collective-permute-start(bf16[2,16,1408]{2,1,0:T(8,128)(2,1)S(1)} %get-tuple-element.61), channel_id=1, source_target_pairs={{0,2},{1,3},{2,0},{3,1},{4,6},{5,7},{6,4},{7,5},{8,10},{9,11},{10,... | collective-permute-start | bytes 270344 | tf_op jit(solution)/shard_map/ppermute | solution.py:340
  17.1 2.1 %collective-permute-done.2.c1 = bf16[2,16,1408]{2,1,0:T(8,128)(2,1)S(1)} collective-permute-done((bf16[2,16,1408]{2,1,0:T(8,128)(2,1)S(1)}, bf16[2,16,1408]{2,1,0:T(8,128)(2,1)S(1)}, u32[]{:S(2)}, u32[]{:S(2)}) %collective-permute-start.2) | collective-permute-done | bytes 90144 | tf_op jit(solution)/shard_map/ppermute | solution.py:340
  19.2 1.8 %collective-permute-done.3.c2 = bf16[2,16,1408]{2,1,0:T(8,128)(2,1)S(1)} collective-permute-done((bf16[2,16,1408]{2,1,0:T(8,128)(2,1)S(1)}, bf16[2,16,1408]{2,1,0:T(8,128)(2,1)S(1)}, u32[]{:S(2)}, u32[]{:S(2)}) %collective-permute-start.3) | collective-permute-done | bytes 90144 | tf_op jit(solution)/shard_map/ppermute | solution.py:340
  23.2 4.6 %collective-permute-start.6 = (bf16[8,16,1024]{2,1,0:T(8,128)(2,1)S(1)}, bf16[8,16,1024]{2,1,0:T(8,128)(2,1)S(1)}, u32[]{:S(2)}, u32[]{:S(2)}) collective-permute-start(bf16[8,16,1024]{2,1,0:T(8,128)(2,1)S(1)} %shard_map.80), channel_id=1, source_target_pairs={{4,8},{8,4},{12,16},{16,12},{20,24},{24,20},{28,32},{32,28},{36,40... | collective-permute-start | bytes 786440 | tf_op jit(solution)/shard_map/ppermute | solution.py:349
  27.8 4.0 %collective-permute-done.6.outer = bf16[8,16,1024]{2,1,0:T(8,128)(2,1)S(1)} collective-permute-done((bf16[8,16,1024]{2,1,0:T(8,128)(2,1)S(1)}, bf16[8,16,1024]{2,1,0:T(8,128)(2,1)S(1)}, u32[]{:S(2)}, u32[]{:S(2)}) %collective-permute-start.6) | collective-permute-done | bytes 262176 | tf_op jit(solution)/shard_map/ppermute | solution.py:349
  37.2 2.0 %collective-permute-done.8.h1 = bf16[2,16,1024]{2,1,0:T(8,128)(2,1)S(1)} collective-permute-done((bf16[2,16,1024]{2,1,0:T(8,128)(2,1)S(1)}, bf16[2,16,1024]{2,1,0:T(8,128)(2,1)S(1)}, u32[]{:S(2)}, u32[]{:S(2)}) %collective-permute-start.8) | collective-permute-done | bytes 65568 | tf_op jit(solution)/shard_map/ppermute | solution.py:340
  40.6 4.1 %shard_map.82 = (bf16[2,16,1024]{2,1,0:T(8,128)(2,1)S(1)}, bf16[2,16,1024]{2,1,0:T(8,128)(2,1)S(1)}, bf16[2,16,1024]{2,1,0:T(8,128)(2,1)S(1)}, bf16[2,16,1024]{2...) custom-call(s32[1]{0:T(128)} %bitcast.me_ref, s32[3,2,32]{2,1,0:T(2,128)S(1)} %get-tuple-element.50.cols, ...), custom_call_target="tpu_custom_call" | custom-call | flops 301989888 | bytes 7000000 | tf_op jit(solution)/shard_map/pallas_call | solution.py:399
  44.7 1.9 %collective-permute-start.11 = (bf16[2,16,1024]{2,1,0:T(8,128)(2,1)S(1)}, bf16[2,16,1024]{2,1,0:T(8,128)(2,1)S(1)}, u32[]{:S(2)}, u32[]{:S(2)}) collective-permute-start(bf16[2,16,1024]{2,1,0:T(8,128)(2,1)S(1)} %get-tuple-element.74), channel_id=1, source_target_pairs={{0,2},{1,3},{2,0},{3,1},{4,6},{5,7},{6,4},{7,5},{8,10},{9,11},{10,... | collective-permute-start | bytes 196616 | tf_op jit(solution)/shard_map/ppermute | solution.py:340
  49.4 2.4 %collective-permute-done.12.c2 = bf16[2,16,1024]{2,1,0:T(8,128)(2,1)S(1)} collective-permute-done((bf16[2,16,1024]{2,1,0:T(8,128)(2,1)S(1)}, bf16[2,16,1024]{2,1,0:T(8,128)(2,1)S(1)}, u32[]{:S(2)}, u32[]{:S(2)}) %collective-permute-start.12) | collective-permute-done | bytes 65568 | tf_op jit(solution)/shard_map/ppermute | solution.py:340
  52.3 1.9 %collective-permute-start.14 = (bf16[8,16,1024]{2,1,0:T(8,128)(2,1)S(1)}, bf16[8,16,1024]{2,1,0:T(8,128)(2,1)S(1)}, u32[]{:S(2)}, u32[]{:S(2)}) collective-permute-start(bf16[8,16,1024]{2,1,0:T(8,128)(2,1)S(1)} %get-tuple-element.78), channel_id=1, source_target_pairs={{0,4},{4,0},{8,12},{12,8},{16,20},{20,16},{24,28},{28,24},{32,36},... | collective-permute-start | bytes 786440 | tf_op jit(solution)/shard_map/ppermute | solution.py:344
  55.4 3.8 %collective-permute-start.15 = (bf16[8,16,1024]{2,1,0:T(8,128)(2,1)S(1)}, bf16[8,16,1024]{2,1,0:T(8,128)(2,1)S(1)}, u32[]{:S(2)}, u32[]{:S(2)}) collective-permute-start(bf16[8,16,1024]{2,1,0:T(8,128)(2,1)S(1)} %shard_map.84), channel_id=1, source_target_pairs={{4,8},{8,4},{12,16},{16,12},{20,24},{24,20},{28,32},{32,28},{36,40... | collective-permute-start | bytes 786440 | tf_op jit(solution)/shard_map/ppermute | solution.py:349
  59.2 4.0 %collective-permute-done.15.outer = bf16[8,16,1024]{2,1,0:T(8,128)(2,1)S(1)} collective-permute-done((bf16[8,16,1024]{2,1,0:T(8,128)(2,1)S(1)}, bf16[8,16,1024]{2,1,0:T(8,128)(2,1)S(1)}, u32[]{:S(2)}, u32[]{:S(2)}) %collective-permute-start.15) | collective-permute-done | bytes 262176 | tf_op jit(solution)/shard_map/ppermute | solution.py:349
  68.3 2.2 %collective-permute-done.17.h1 = bf16[2,16,1024]{2,1,0:T(8,128)(2,1)S(1)} collective-permute-done((bf16[2,16,1024]{2,1,0:T(8,128)(2,1)S(1)}, bf16[2,16,1024]{2,1,0:T(8,128)(2,1)S(1)}, u32[]{:S(2)}, u32[]{:S(2)}) %collective-permute-start.17) | collective-permute-done | bytes 65568 | tf_op jit(solution)/shard_map/ppermute | solution.py:340
  72.0 4.7 %shard_map.86 = (f32[2,16,1024]{2,1,0:T(8,128)S(1)}, f32[2,16,1024]{2,1,0:T(8,128)S(1)}, f32[2,16,1024]{2,1,0:T(8,128)S(1)}, f32[2,16,1024]{2,1,0:T(8,128)S(1)},...) custom-call(s32[1]{0:T(128)} %bitcast.me_ref, s32[3,2,32]{2,1,0:T(2,128)S(1)} %get-tuple-element.50.cols, ...), custom_call_target="tpu_custom_call" | custom-call | flops 402653184 | bytes 9000000 | tf_op jit(solution)/shard_map/pallas_call | solution.py:409
  76.6 1.8 %collective-permute-start.23 = (f32[2,16,1024]{2,1,0:T(8,128)S(1)}, f32[2,16,1024]{2,1,0:T(8,128)S(1)}, u32[]{:S(2)}, u32[]{:S(2)}) collective-permute-start(f32[2,16,1024]{2,1,0:T(8,128)S(1)} %get-tuple-element.91), channel_id=1, source_target_pairs={{0,2},{1,3},{2,0},{3,1},{4,6},{5,7},{6,4},{7,5},{8,10},{9,11},{10,... | collective-permute-start | bytes 393224 | tf_op jit(solution)/shard_map/ppermute | solution.py:340
  79.9 20.7 %all-to-all-start = ((f32[256,1,128]{2,1,0:T(1,128)}), f32[256,1,128]{2,1,0:T(1,128)S(1)}, u32[]{:S(2)}, u32[]{:S(2)}) async-start(f32[256,1,128]{2,1,0:T(1,128)} %get-tuple-element.87), calls=%async_computation | async-start | bytes 262144 | tf_op jit(solution)/shard_map/all_to_all | solution.py:415
  101.6 2.1 %collective-permute-start.26 = (f32[4,16,1024]{2,1,0:T(8,128)}, f32[4,16,1024]{2,1,0:T(8,128)S(1)}, u32[]{:S(2)}, u32[]{:S(2)}) collective-permute-start(f32[4,16,1024]{2,1,0:T(8,128)} %get-tuple-element.95), channel_id=1, source_target_pairs={{0,4},{4,0},{8,12},{12,8},{16,20},{20,16},{24,28},{28,24},{32,36},... | collective-permute-start | bytes 786440 | tf_op jit(solution)/shard_map/ppermute | solution.py:344
  103.8 1.9 %collective-permute-start.27 = (f32[4,16,1024]{2,1,0:T(8,128)S(1)}, f32[4,16,1024]{2,1,0:T(8,128)S(1)}, u32[]{:S(2)}, u32[]{:S(2)}) collective-permute-start(f32[4,16,1024]{2,1,0:T(8,128)S(1)} %get-tuple-element.96), channel_id=1, source_target_pairs={{4,8},{8,4},{12,16},{16,12},{20,24},{24,20},{28,32},{32,28},{36,40... | collective-permute-start | bytes 786440 | tf_op jit(solution)/shard_map/ppermute | solution.py:349
  105.7 7.6 %all-to-all-done.sums = f32[256,1,128]{2,1,0:T(1,128)S(1)} async-done(((f32[256,1,128]{2,1,0:T(1,128)}), f32[256,1,128]{2,1,0:T(1,128)S(1)}, u32[]{:S(2)}, u32[]{:S(2)}) %all-to-all-start) | async-done | bytes 131104 | tf_op jit(solution)/shard_map/all_to_all | solution.py:415
  115.3 1.8 %collective-permute-start.20 = (bf16[4,16,1024]{2,1,0:T(8,128)(2,1)S(1)}, bf16[4,16,1024]{2,1,0:T(8,128)(2,1)S(1)}, u32[]{:S(2)}, u32[]{:S(2)}) collective-permute-start(bf16[4,16,1024]{2,1,0:T(8,128)(2,1)S(1)} %shard_map.87.s0), channel_id=1, source_target_pairs={{0,2},{1,3},{2,0},{3,1},{4,6},{5,7},{6,4},{7,5},{8,10},{9,11},{10,... | collective-permute-start | bytes 393224 | tf_op jit(solution)/shard_map/ppermute | solution.py:340
  124.3 4.4 %collective-permute-done.29.s2 = bf16[4,16,1024]{2,1,0:T(8,128)(2,1)S(1)} collective-permute-done((bf16[4,16,1024]{2,1,0:T(8,128)(2,1)S(1)}, bf16[4,16,1024]{2,1,0:T(8,128)(2,1)S(1)}, u32[]{:S(2)}, u32[]{:S(2)}) %collective-permute-start.29) | collective-permute-done | bytes 131104 | tf_op jit(solution)/shard_map/ppermute | solution.py:340
  (65 shorter events, 36.6 us)
Async XLA Ops:
  3.8 10.1 %collective-permute-start = (f32[8,128]{1,0:T(8,128)S(1)}, f32[8,128]{1,0:T(8,128)S(1)}, u32[]{:S(2)}, u32[]{:S(2)}) collective-permute-start(f32[8,128]{1,0:T(8,128)S(1)} %get-tuple-element.53), channel_id=1, source_target_pairs={{0,4},{4,0},{8,12},{12,8},{16,20},{20,16},{24,28},{28,24},{32,36},... | collective-permute-start | bytes 12296 | tf_op jit(solution)/shard_map/ppermute | solution.py:344
  7.1 6.8 %collective-permute-start.1 = (f32[8,128]{1,0:T(8,128)S(1)}, f32[8,128]{1,0:T(8,128)S(1)}, u32[]{:S(2)}, u32[]{:S(2)}) collective-permute-start(f32[8,128]{1,0:T(8,128)S(1)} %get-tuple-element.54), channel_id=1, source_target_pairs={{4,8},{8,4},{12,16},{16,12},{20,24},{24,20},{28,32},{32,28},{36,40... | collective-permute-start | bytes 12296 | tf_op jit(solution)/shard_map/ppermute | solution.py:349
  13.9 5.2 %collective-permute-start.2 = (bf16[2,16,1408]{2,1,0:T(8,128)(2,1)S(1)}, bf16[2,16,1408]{2,1,0:T(8,128)(2,1)S(1)}, u32[]{:S(2)}, u32[]{:S(2)}) collective-permute-start(bf16[2,16,1408]{2,1,0:T(8,128)(2,1)S(1)} %get-tuple-element.61), channel_id=1, source_target_pairs={{0,2},{1,3},{2,0},{3,1},{4,6},{5,7},{6,4},{7,5},{8,10},{9,11},{10,... | collective-permute-start | bytes 270344 | tf_op jit(solution)/shard_map/ppermute | solution.py:340
  16.3 4.7 %collective-permute-start.3 = (bf16[2,16,1408]{2,1,0:T(8,128)(2,1)S(1)}, bf16[2,16,1408]{2,1,0:T(8,128)(2,1)S(1)}, u32[]{:S(2)}, u32[]{:S(2)}) collective-permute-start(bf16[2,16,1408]{2,1,0:T(8,128)(2,1)S(1)} %get-tuple-element.62), channel_id=1, source_target_pairs={{0,3},{1,2},{2,1},{3,0},{4,7},{5,6},{6,5},{7,4},{8,11},{9,10},{10,... | collective-permute-start | bytes 270344 | tf_op jit(solution)/shard_map/ppermute | solution.py:340
  23.2 8.6 %collective-permute-start.6 = (bf16[8,16,1024]{2,1,0:T(8,128)(2,1)S(1)}, bf16[8,16,1024]{2,1,0:T(8,128)(2,1)S(1)}, u32[]{:S(2)}, u32[]{:S(2)}) collective-permute-start(bf16[8,16,1024]{2,1,0:T(8,128)(2,1)S(1)} %shard_map.80), channel_id=1, source_target_pairs={{4,8},{8,4},{12,16},{16,12},{20,24},{24,20},{28,32},{32,28},{36,40... | collective-permute-start | bytes 786440 | tf_op jit(solution)/shard_map/ppermute | solution.py:349
  34.0 5.1 %collective-permute-start.8 = (bf16[2,16,1024]{2,1,0:T(8,128)(2,1)S(1)}, bf16[2,16,1024]{2,1,0:T(8,128)(2,1)S(1)}, u32[]{:S(2)}, u32[]{:S(2)}) collective-permute-start(bf16[2,16,1024]{2,1,0:T(8,128)(2,1)S(1)} %get-tuple-element.69), channel_id=1, source_target_pairs={{0,2},{1,3},{2,0},{3,1},{4,6},{5,7},{6,4},{7,5},{8,10},{9,11},{10,... | collective-permute-start | bytes 196616 | tf_op jit(solution)/shard_map/ppermute | solution.py:340
  35.5 5.1 %collective-permute-start.9 = (bf16[2,16,1024]{2,1,0:T(8,128)(2,1)S(1)}, bf16[2,16,1024]{2,1,0:T(8,128)(2,1)S(1)}, u32[]{:S(2)}, u32[]{:S(2)}) collective-permute-start(bf16[2,16,1024]{2,1,0:T(8,128)(2,1)S(1)} %get-tuple-element.70), channel_id=1, source_target_pairs={{0,3},{1,2},{2,1},{3,0},{4,7},{5,6},{6,5},{7,4},{8,11},{9,10},{10,... | collective-permute-start | bytes 196616 | tf_op jit(solution)/shard_map/ppermute | solution.py:340
  44.7 4.7 %collective-permute-start.11 = (bf16[2,16,1024]{2,1,0:T(8,128)(2,1)S(1)}, bf16[2,16,1024]{2,1,0:T(8,128)(2,1)S(1)}, u32[]{:S(2)}, u32[]{:S(2)}) collective-permute-start(bf16[2,16,1024]{2,1,0:T(8,128)(2,1)S(1)} %get-tuple-element.74), channel_id=1, source_target_pairs={{0,2},{1,3},{2,0},{3,1},{4,6},{5,7},{6,4},{7,5},{8,10},{9,11},{10,... | collective-permute-start | bytes 196616 | tf_op jit(solution)/shard_map/ppermute | solution.py:340
  46.6 5.2 %collective-permute-start.12 = (bf16[2,16,1024]{2,1,0:T(8,128)(2,1)S(1)}, bf16[2,16,1024]{2,1,0:T(8,128)(2,1)S(1)}, u32[]{:S(2)}, u32[]{:S(2)}) collective-permute-start(bf16[2,16,1024]{2,1,0:T(8,128)(2,1)S(1)} %get-tuple-element.75), channel_id=1, source_target_pairs={{0,3},{1,2},{2,1},{3,0},{4,7},{5,6},{6,5},{7,4},{8,11},{9,10},{10,... | collective-permute-start | bytes 196616 | tf_op jit(solution)/shard_map/ppermute | solution.py:340
  55.4 7.8 %collective-permute-start.15 = (bf16[8,16,1024]{2,1,0:T(8,128)(2,1)S(1)}, bf16[8,16,1024]{2,1,0:T(8,128)(2,1)S(1)}, u32[]{:S(2)}, u32[]{:S(2)}) collective-permute-start(bf16[8,16,1024]{2,1,0:T(8,128)(2,1)S(1)} %shard_map.84), channel_id=1, source_target_pairs={{4,8},{8,4},{12,16},{16,12},{20,24},{24,20},{28,32},{32,28},{36,40... | collective-permute-start | bytes 786440 | tf_op jit(solution)/shard_map/ppermute | solution.py:349
  65.4 5.1 %collective-permute-start.17 = (bf16[2,16,1024]{2,1,0:T(8,128)(2,1)S(1)}, bf16[2,16,1024]{2,1,0:T(8,128)(2,1)S(1)}, u32[]{:S(2)}, u32[]{:S(2)}) collective-permute-start(bf16[2,16,1024]{2,1,0:T(8,128)(2,1)S(1)} %get-tuple-element.80), channel_id=1, source_target_pairs={{0,2},{1,3},{2,0},{3,1},{4,6},{5,7},{6,4},{7,5},{8,10},{9,11},{10,... | collective-permute-start | bytes 196616 | tf_op jit(solution)/shard_map/ppermute | solution.py:340
  66.9 5.1 %collective-permute-start.18 = (bf16[2,16,1024]{2,1,0:T(8,128)(2,1)S(1)}, bf16[2,16,1024]{2,1,0:T(8,128)(2,1)S(1)}, u32[]{:S(2)}, u32[]{:S(2)}) collective-permute-start(bf16[2,16,1024]{2,1,0:T(8,128)(2,1)S(1)} %get-tuple-element.81), channel_id=1, source_target_pairs={{0,3},{1,2},{2,1},{3,0},{4,7},{5,6},{6,5},{7,4},{8,11},{9,10},{10,... | collective-permute-start | bytes 196616 | tf_op jit(solution)/shard_map/ppermute | solution.py:340
  76.6 24.0 %collective-permute-start.23 = (f32[2,16,1024]{2,1,0:T(8,128)S(1)}, f32[2,16,1024]{2,1,0:T(8,128)S(1)}, u32[]{:S(2)}, u32[]{:S(2)}) collective-permute-start(f32[2,16,1024]{2,1,0:T(8,128)S(1)} %get-tuple-element.91), channel_id=1, source_target_pairs={{0,2},{1,3},{2,0},{3,1},{4,6},{5,7},{6,4},{7,5},{8,10},{9,11},{10,... | collective-permute-start | bytes 393224 | tf_op jit(solution)/shard_map/ppermute | solution.py:340
  78.5 22.1 %collective-permute-start.24 = (f32[2,16,1024]{2,1,0:T(8,128)S(1)}, f32[2,16,1024]{2,1,0:T(8,128)S(1)}, u32[]{:S(2)}, u32[]{:S(2)}) collective-permute-start(f32[2,16,1024]{2,1,0:T(8,128)S(1)} %get-tuple-element.92), channel_id=1, source_target_pairs={{0,3},{1,2},{2,1},{3,0},{4,7},{5,6},{6,5},{7,4},{8,11},{9,10},{10,... | collective-permute-start | bytes 393224 | tf_op jit(solution)/shard_map/ppermute | solution.py:340
  79.9 20.7 %collective-permute-start.25 = (f32[2,16,1024]{2,1,0:T(8,128)S(1)}, f32[2,16,1024]{2,1,0:T(8,128)S(1)}, u32[]{:S(2)}, u32[]{:S(2)}) collective-permute-start(f32[2,16,1024]{2,1,0:T(8,128)S(1)} %get-tuple-element.93), channel_id=1, source_target_pairs={{0,1},{1,0},{2,3},{3,2},{4,5},{5,4},{6,7},{7,6},{8,9},{9,8},{10,11... | collective-permute-start | bytes 393224 | tf_op jit(solution)/shard_map/ppermute | solution.py:340
  79.9 33.3 %all-to-all-start = ((f32[256,1,128]{2,1,0:T(1,128)}), f32[256,1,128]{2,1,0:T(1,128)S(1)}, u32[]{:S(2)}, u32[]{:S(2)}) async-start(f32[256,1,128]{2,1,0:T(1,128)} %get-tuple-element.87), calls=%async_computation | async-start | bytes 262144 | tf_op jit(solution)/shard_map/all_to_all | solution.py:415
  101.6 15.5 %collective-permute-start.26 = (f32[4,16,1024]{2,1,0:T(8,128)}, f32[4,16,1024]{2,1,0:T(8,128)S(1)}, u32[]{:S(2)}, u32[]{:S(2)}) collective-permute-start(f32[4,16,1024]{2,1,0:T(8,128)} %get-tuple-element.95), channel_id=1, source_target_pairs={{0,4},{4,0},{8,12},{12,8},{16,20},{20,16},{24,28},{28,24},{32,36},... | collective-permute-start | bytes 786440 | tf_op jit(solution)/shard_map/ppermute | solution.py:344
  103.8 13.3 %collective-permute-start.27 = (f32[4,16,1024]{2,1,0:T(8,128)S(1)}, f32[4,16,1024]{2,1,0:T(8,128)S(1)}, u32[]{:S(2)}, u32[]{:S(2)}) collective-permute-start(f32[4,16,1024]{2,1,0:T(8,128)S(1)} %get-tuple-element.96), channel_id=1, source_target_pairs={{4,8},{8,4},{12,16},{16,12},{20,24},{24,20},{28,32},{32,28},{36,40... | collective-permute-start | bytes 786440 | tf_op jit(solution)/shard_map/ppermute | solution.py:349
  113.8 5.4 %collective-permute-start.22 = (bf16[4,16,1024]{2,1,0:T(8,128)(2,1)S(1)}, bf16[4,16,1024]{2,1,0:T(8,128)(2,1)S(1)}, u32[]{:S(2)}, u32[]{:S(2)}) collective-permute-start(bf16[4,16,1024]{2,1,0:T(8,128)(2,1)S(1)} %shard_map.87.s0), channel_id=1, source_target_pairs={{0,1},{1,0},{2,3},{3,2},{4,5},{5,4},{6,7},{7,6},{8,9},{9,8},{10,11... | collective-permute-start | bytes 393224 | tf_op jit(solution)/shard_map/ppermute | solution.py:340
  114.2 8.2 %collective-permute-start.21 = (bf16[4,16,1024]{2,1,0:T(8,128)(2,1)S(1)}, bf16[4,16,1024]{2,1,0:T(8,128)(2,1)S(1)}, u32[]{:S(2)}, u32[]{:S(2)}) collective-permute-start(bf16[4,16,1024]{2,1,0:T(8,128)(2,1)S(1)} %shard_map.87.s0), channel_id=1, source_target_pairs={{0,3},{1,2},{2,1},{3,0},{4,7},{5,6},{6,5},{7,4},{8,11},{9,10},{10,... | collective-permute-start | bytes 393224 | tf_op jit(solution)/shard_map/ppermute | solution.py:340
  115.3 7.1 %collective-permute-start.20 = (bf16[4,16,1024]{2,1,0:T(8,128)(2,1)S(1)}, bf16[4,16,1024]{2,1,0:T(8,128)(2,1)S(1)}, u32[]{:S(2)}, u32[]{:S(2)}) collective-permute-start(bf16[4,16,1024]{2,1,0:T(8,128)(2,1)S(1)} %shard_map.87.s0), channel_id=1, source_target_pairs={{0,2},{1,3},{2,0},{3,1},{4,6},{5,7},{6,4},{7,5},{8,10},{9,11},{10,... | collective-permute-start | bytes 393224 | tf_op jit(solution)/shard_map/ppermute | solution.py:340
  117.7 6.7 %collective-permute-start.30 = (bf16[4,16,1024]{2,1,0:T(8,128)(2,1)S(1)}, bf16[4,16,1024]{2,1,0:T(8,128)(2,1)S(1)}, u32[]{:S(2)}, u32[]{:S(2)}) collective-permute-start(bf16[4,16,1024]{2,1,0:T(8,128)(2,1)S(1)} %shard_map.91.s0), channel_id=1, source_target_pairs={{0,1},{1,0},{2,3},{3,2},{4,5},{5,4},{6,7},{7,6},{8,9},{9,8},{10,11... | collective-permute-start | bytes 393224 | tf_op jit(solution)/shard_map/ppermute | solution.py:340
  118.1 10.6 %collective-permute-start.29 = (bf16[4,16,1024]{2,1,0:T(8,128)(2,1)S(1)}, bf16[4,16,1024]{2,1,0:T(8,128)(2,1)S(1)}, u32[]{:S(2)}, u32[]{:S(2)}) collective-permute-start(bf16[4,16,1024]{2,1,0:T(8,128)(2,1)S(1)} %shard_map.91.s0), channel_id=1, source_target_pairs={{0,3},{1,2},{2,1},{3,0},{4,7},{5,6},{6,5},{7,4},{8,11},{9,10},{10,... | collective-permute-start | bytes 393224 | tf_op jit(solution)/shard_map/ppermute | solution.py:340
  119.2 9.5 %collective-permute-start.28 = (bf16[4,16,1024]{2,1,0:T(8,128)(2,1)S(1)}, bf16[4,16,1024]{2,1,0:T(8,128)(2,1)S(1)}, u32[]{:S(2)}, u32[]{:S(2)}) collective-permute-start(bf16[4,16,1024]{2,1,0:T(8,128)(2,1)S(1)} %shard_map.91.s0), channel_id=1, source_target_pairs={{0,2},{1,3},{2,0},{3,1},{4,6},{5,7},{6,4},{7,5},{8,10},{9,11},{10,... | collective-permute-start | bytes 393224 | tf_op jit(solution)/shard_map/ppermute | solution.py:340
  (12 other events, 89.9 us)

commit v6 on v5

--- a/solution.py
+++ b/solution.py
@@ -18,7 +18,7 @@
 UB = 32
 ZD = 4
 CH = 128
-COEF = 3 * 128
+COEF = 128
 CHUNK = 16
 GROUP = 8
 VMEM = pl.BlockSpec(memory_space=pltpu.VMEM)
@@ -126,11 +126,14 @@
     for i in range(PAIR):
         at = slice(ZD * i, ZD * (i + 1))
         rest = jnp.concatenate([from_low[at], own[at], from_high[at], jnp.zeros((4, 128), F32)], axis=0)
+        lane = lax.broadcasted_iota(jnp.int32, (L, 128), 1)
+        packed = jnp.zeros((L, 128), F32)
         for part in range(3):
-            piece = rest.astype(BF16)
-            rest = rest - piece.astype(F32)
-            for out in outs:
-                out[i, :, Q + 128 * part:Q + 128 * (part + 1)] = piece
+            piece = rest.astype(BF16).astype(F32)
+            rest = rest - piece
+            packed = jnp.where(lane == part, piece, packed)
+        for out in outs:
+            out[i, :, Q:] = packed.astype(BF16)
 
 
 def both_body(cols, w, acc, lhs, store):
@@ -224,9 +227,9 @@
     parts = (c0, c1, c2, c3)
     for r in range(ANG):
         for i in range(PAIR):
-            value = parts[r][i, :, Q:Q + 128].astype(F32)
-            value = value + parts[r][i, :, Q + 128:Q + 256].astype(F32)
-            coefs[r, i] = value + parts[r][i, :, Q + 256:].astype(F32)
+            value = parts[r][i, :, Q:].astype(F32)
+            total = value[:, 0:1] + value[:, 1:2] + value[:, 2:3]
+            coefs[r, i] = jnp.broadcast_to(total, (L, 128))
     combine_parts(flag, coefs, parts, mine, sent)
 
 
@@ -295,9 +298,12 @@
 
 
 def steps(sums_ref):
-    total = sums_ref[0]
-    for at in range(1, sums_ref.shape[0]):
-        total = total + sums_ref[at]
+    parts = [sums_ref[at] for at in range(16)]
+    for at in range(16, sums_ref.shape[0]):
+        parts[at % 16] = parts[at % 16] + sums_ref[at]
+    while len(parts) > 1:
+        parts = [low + high for low, high in zip(parts[::2], parts[1::2])]
+    total = parts[0]
     lane = lax.broadcasted_iota(jnp.int32, (1, 128), 1)
     gamma0, curve0, inner, norm, cross, own = [
         jnp.sum(jnp.where(lane == at, total, 0.0)) for at in range(6)

time: 130 us -> 130 us (level)
  no operation moved by 1% of the time
where the time goes in v6:
time: 130 us; the launch traced here: 129 us
  starting transfers between devices  62.7 us (48%)
  waiting for transfers between devices  41.9 us (32%)
  Pallas kernels  22.1 us (17%)
  local copies, waits for them, and re-layouts  2.05 us (2%)
    ppermute x21, starting transfers between devices, along_ang(): return lax.ppermute(value, 'ang', [(i, i ^ other) for i in range(ANG)])  21.8 us
    all_to_all x1, starting transfers between devices, per_device(): sums = lax.all_to_all(sums, ('slab', 'ang'), 0, 0, tiled=True)  21.3 us
    ppermute x21, waiting for transfers between devices, along_ang(): return lax.ppermute(value, 'ang', [(i, i ^ other) for i in range(ANG)])  20.5 us
    ppermute x4, starting transfers between devices, across(): lax.ppermute(value, 'slab', [pair for i in range(1, count - 1, 2) for pai...  12.2 us
    ppermute x4, waiting for transfers between devices, across(): lax.ppermute(value, 'slab', [pair for i in range(1, count - 1, 2) for pai...  8.09 us
    all_to_all x1, waiting for transfers between devices, per_device(): sums = lax.all_to_all(sums, ('slab', 'ang'), 0, 0, tiled=True)  7.55 us
    ppermute x6, starting transfers between devices, on_chip(): lax.ppermute(value, 'slab', [(i, i ^ 1) for i in range(lax.axis_size('sla...  7.5 us
    ppermute x6, waiting for transfers between devices, on_chip(): lax.ppermute(value, 'slab', [(i, i ^ 1) for i in range(lax.axis_size('sla...  5.75 us
  transfers between devices with their start and end apart: 32, of which 17 were waited for; matrix products, arithmetic and copies ran while one was open for 0% of the time, Pallas kernels for 7%

profile of v6, /device:TPU:1, one launch (start us, length us, event | category | flops | bytes accessed | tf_op | source)
XLA Modules:
  0.0 129.5 jit_solution(3358504066888459497)
XLA Ops:
  3.8 3.3 %collective-permute-start = (f32[8,128]{1,0:T(8,128)S(1)}, f32[8,128]{1,0:T(8,128)S(1)}, u32[]{:S(2)}, u32[]{:S(2)}) collective-permute-start(f32[8,128]{1,0:T(8,128)S(1)} %get-tuple-element.53), channel_id=1, source_target_pairs={{0,4},{4,0},{8,12},{12,8},{16,20},{20,16},{24,28},{28,24},{32,36},... | collective-permute-start | bytes 12296 | tf_op jit(solution)/shard_map/ppermute | solution.py:350
  7.1 1.9 %collective-permute-start.1 = (f32[8,128]{1,0:T(8,128)S(1)}, f32[8,128]{1,0:T(8,128)S(1)}, u32[]{:S(2)}, u32[]{:S(2)}) collective-permute-start(f32[8,128]{1,0:T(8,128)S(1)} %get-tuple-element.54), channel_id=1, source_target_pairs={{4,8},{8,4},{12,16},{16,12},{20,24},{24,20},{28,32},{32,28},{36,40... | collective-permute-start | bytes 12296 | tf_op jit(solution)/shard_map/ppermute | solution.py:355
  9.0 4.8 %shard_map.77 = (bf16[2,16,1024]{2,1,0:T(8,128)(2,1)S(1)}, bf16[2,16,1024]{2,1,0:T(8,128)(2,1)S(1)}, bf16[2,16,1024]{2,1,0:T(8,128)(2,1)S(1)}, bf16[2,16,1024]{2...) custom-call(s32[1]{0:T(128)} %bitcast.me_ref, s32[3,2,32]{2,1,0:T(2,128)S(1)} %get-tuple-element.50.cols, ...), custom_call_target="tpu_custom_call" | custom-call | flops 201326592 | bytes 7000000 | tf_op jit(solution)/shard_map/pallas_call | solution.py:392
  13.9 2.4 %collective-permute-start.2 = (bf16[2,16,1152]{2,1,0:T(8,128)(2,1)S(1)}, bf16[2,16,1152]{2,1,0:T(8,128)(2,1)S(1)}, u32[]{:S(2)}, u32[]{:S(2)}) collective-permute-start(bf16[2,16,1152]{2,1,0:T(8,128)(2,1)S(1)} %get-tuple-element.61), channel_id=1, source_target_pairs={{0,2},{1,3},{2,0},{3,1},{4,6},{5,7},{6,4},{7,5},{8,10},{9,11},{10,... | collective-permute-start | bytes 221192 | tf_op jit(solution)/shard_map/ppermute | solution.py:346
  17.1 1.7 %collective-permute-done.2.c1 = bf16[2,16,1152]{2,1,0:T(8,128)(2,1)S(1)} collective-permute-done((bf16[2,16,1152]{2,1,0:T(8,128)(2,1)S(1)}, bf16[2,16,1152]{2,1,0:T(8,128)(2,1)S(1)}, u32[]{:S(2)}, u32[]{:S(2)}) %collective-permute-start.2) | collective-permute-done | bytes 73760 | tf_op jit(solution)/shard_map/ppermute | solution.py:346
  18.8 1.9 %collective-permute-done.3.c2 = bf16[2,16,1152]{2,1,0:T(8,128)(2,1)S(1)} collective-permute-done((bf16[2,16,1152]{2,1,0:T(8,128)(2,1)S(1)}, bf16[2,16,1152]{2,1,0:T(8,128)(2,1)S(1)}, u32[]{:S(2)}, u32[]{:S(2)}) %collective-permute-start.3) | collective-permute-done | bytes 73760 | tf_op jit(solution)/shard_map/ppermute | solution.py:346
  23.0 4.5 %collective-permute-start.6 = (bf16[8,16,1024]{2,1,0:T(8,128)(2,1)S(1)}, bf16[8,16,1024]{2,1,0:T(8,128)(2,1)S(1)}, u32[]{:S(2)}, u32[]{:S(2)}) collective-permute-start(bf16[8,16,1024]{2,1,0:T(8,128)(2,1)S(1)} %shard_map.80), channel_id=1, source_target_pairs={{4,8},{8,4},{12,16},{16,12},{20,24},{24,20},{28,32},{32,28},{36,40... | collective-permute-start | bytes 786440 | tf_op jit(solution)/shard_map/ppermute | solution.py:355
  27.5 4.0 %collective-permute-done.6.outer = bf16[8,16,1024]{2,1,0:T(8,128)(2,1)S(1)} collective-permute-done((bf16[8,16,1024]{2,1,0:T(8,128)(2,1)S(1)}, bf16[8,16,1024]{2,1,0:T(8,128)(2,1)S(1)}, u32[]{:S(2)}, u32[]{:S(2)}) %collective-permute-start.6) | collective-permute-done | bytes 262176 | tf_op jit(solution)/shard_map/ppermute | solution.py:355
  36.6 2.3 %collective-permute-done.8.h1 = bf16[2,16,1024]{2,1,0:T(8,128)(2,1)S(1)} collective-permute-done((bf16[2,16,1024]{2,1,0:T(8,128)(2,1)S(1)}, bf16[2,16,1024]{2,1,0:T(8,128)(2,1)S(1)}, u32[]{:S(2)}, u32[]{:S(2)}) %collective-permute-start.8) | collective-permute-done | bytes 65568 | tf_op jit(solution)/shard_map/ppermute | solution.py:346
  40.5 4.1 %shard_map.82 = (bf16[2,16,1024]{2,1,0:T(8,128)(2,1)S(1)}, bf16[2,16,1024]{2,1,0:T(8,128)(2,1)S(1)}, bf16[2,16,1024]{2,1,0:T(8,128)(2,1)S(1)}, bf16[2,16,1024]{2...) custom-call(s32[1]{0:T(128)} %bitcast.me_ref, s32[3,2,32]{2,1,0:T(2,128)S(1)} %get-tuple-element.50.cols, ...), custom_call_target="tpu_custom_call" | custom-call | flops 301989888 | bytes 7000000 | tf_op jit(solution)/shard_map/pallas_call | solution.py:405
  49.3 1.9 %collective-permute-done.12.c2 = bf16[2,16,1024]{2,1,0:T(8,128)(2,1)S(1)} collective-permute-done((bf16[2,16,1024]{2,1,0:T(8,128)(2,1)S(1)}, bf16[2,16,1024]{2,1,0:T(8,128)(2,1)S(1)}, u32[]{:S(2)}, u32[]{:S(2)}) %collective-permute-start.12) | collective-permute-done | bytes 65568 | tf_op jit(solution)/shard_map/ppermute | solution.py:346
  51.6 1.9 %collective-permute-start.14 = (bf16[8,16,1024]{2,1,0:T(8,128)(2,1)S(1)}, bf16[8,16,1024]{2,1,0:T(8,128)(2,1)S(1)}, u32[]{:S(2)}, u32[]{:S(2)}) collective-permute-start(bf16[8,16,1024]{2,1,0:T(8,128)(2,1)S(1)} %get-tuple-element.78), channel_id=1, source_target_pairs={{0,4},{4,0},{8,12},{12,8},{16,20},{20,16},{24,28},{28,24},{32,36},... | collective-permute-start | bytes 786440 | tf_op jit(solution)/shard_map/ppermute | solution.py:350
  54.8 3.8 %collective-permute-start.15 = (bf16[8,16,1024]{2,1,0:T(8,128)(2,1)S(1)}, bf16[8,16,1024]{2,1,0:T(8,128)(2,1)S(1)}, u32[]{:S(2)}, u32[]{:S(2)}) collective-permute-start(bf16[8,16,1024]{2,1,0:T(8,128)(2,1)S(1)} %shard_map.84), channel_id=1, source_target_pairs={{4,8},{8,4},{12,16},{16,12},{20,24},{24,20},{28,32},{32,28},{36,40... | collective-permute-start | bytes 786440 | tf_op jit(solution)/shard_map/ppermute | solution.py:355
  58.6 4.0 %collective-permute-done.15.outer = bf16[8,16,1024]{2,1,0:T(8,128)(2,1)S(1)} collective-permute-done((bf16[8,16,1024]{2,1,0:T(8,128)(2,1)S(1)}, bf16[8,16,1024]{2,1,0:T(8,128)(2,1)S(1)}, u32[]{:S(2)}, u32[]{:S(2)}) %collective-permute-start.15) | collective-permute-done | bytes 262176 | tf_op jit(solution)/shard_map/ppermute | solution.py:355
  67.7 2.3 %collective-permute-done.17.h1 = bf16[2,16,1024]{2,1,0:T(8,128)(2,1)S(1)} collective-permute-done((bf16[2,16,1024]{2,1,0:T(8,128)(2,1)S(1)}, bf16[2,16,1024]{2,1,0:T(8,128)(2,1)S(1)}, u32[]{:S(2)}, u32[]{:S(2)}) %collective-permute-start.17) | collective-permute-done | bytes 65568 | tf_op jit(solution)/shard_map/ppermute | solution.py:346
  71.5 4.7 %shard_map.86 = (f32[2,16,1024]{2,1,0:T(8,128)S(1)}, f32[2,16,1024]{2,1,0:T(8,128)S(1)}, f32[2,16,1024]{2,1,0:T(8,128)S(1)}, f32[2,16,1024]{2,1,0:T(8,128)S(1)},...) custom-call(s32[1]{0:T(128)} %bitcast.me_ref, s32[3,2,32]{2,1,0:T(2,128)S(1)} %get-tuple-element.50.cols, ...), custom_call_target="tpu_custom_call" | custom-call | flops 402653184 | bytes 9000000 | tf_op jit(solution)/shard_map/pallas_call | solution.py:415
  76.2 1.7 %collective-permute-start.23 = (f32[2,16,1024]{2,1,0:T(8,128)S(1)}, f32[2,16,1024]{2,1,0:T(8,128)S(1)}, u32[]{:S(2)}, u32[]{:S(2)}) collective-permute-start(f32[2,16,1024]{2,1,0:T(8,128)S(1)} %get-tuple-element.91), channel_id=1, source_target_pairs={{0,2},{1,3},{2,0},{3,1},{4,6},{5,7},{6,4},{7,5},{8,10},{9,11},{10,... | collective-permute-start | bytes 393224 | tf_op jit(solution)/shard_map/ppermute | solution.py:346
  79.3 21.3 %all-to-all-start = ((f32[256,1,128]{2,1,0:T(1,128)}), f32[256,1,128]{2,1,0:T(1,128)S(1)}, u32[]{:S(2)}, u32[]{:S(2)}) async-start(f32[256,1,128]{2,1,0:T(1,128)} %get-tuple-element.87), calls=%async_computation | async-start | bytes 262144 | tf_op jit(solution)/shard_map/all_to_all | solution.py:421
  101.6 2.1 %collective-permute-start.26 = (f32[4,16,1024]{2,1,0:T(8,128)}, f32[4,16,1024]{2,1,0:T(8,128)S(1)}, u32[]{:S(2)}, u32[]{:S(2)}) collective-permute-start(f32[4,16,1024]{2,1,0:T(8,128)} %get-tuple-element.95), channel_id=1, source_target_pairs={{0,4},{4,0},{8,12},{12,8},{16,20},{20,16},{24,28},{28,24},{32,36},... | collective-permute-start | bytes 786440 | tf_op jit(solution)/shard_map/ppermute | solution.py:350
  103.8 1.9 %collective-permute-start.27 = (f32[4,16,1024]{2,1,0:T(8,128)S(1)}, f32[4,16,1024]{2,1,0:T(8,128)S(1)}, u32[]{:S(2)}, u32[]{:S(2)}) collective-permute-start(f32[4,16,1024]{2,1,0:T(8,128)S(1)} %get-tuple-element.96), channel_id=1, source_target_pairs={{4,8},{8,4},{12,16},{16,12},{20,24},{24,20},{28,32},{32,28},{36,40... | collective-permute-start | bytes 786440 | tf_op jit(solution)/shard_map/ppermute | solution.py:355
  105.7 7.6 %all-to-all-done.sums = f32[256,1,128]{2,1,0:T(1,128)S(1)} async-done(((f32[256,1,128]{2,1,0:T(1,128)}), f32[256,1,128]{2,1,0:T(1,128)S(1)}, u32[]{:S(2)}, u32[]{:S(2)}) %all-to-all-start) | async-done | bytes 131104 | tf_op jit(solution)/shard_map/all_to_all | solution.py:421
  115.1 1.8 %collective-permute-start.20 = (bf16[4,16,1024]{2,1,0:T(8,128)(2,1)S(1)}, bf16[4,16,1024]{2,1,0:T(8,128)(2,1)S(1)}, u32[]{:S(2)}, u32[]{:S(2)}) collective-permute-start(bf16[4,16,1024]{2,1,0:T(8,128)(2,1)S(1)} %shard_map.87.s0), channel_id=1, source_target_pairs={{0,2},{1,3},{2,0},{3,1},{4,6},{5,7},{6,4},{7,5},{8,10},{9,11},{10,... | collective-permute-start | bytes 393224 | tf_op jit(solution)/shard_map/ppermute | solution.py:346
  118.7 1.8 %collective-permute-start.28 = (bf16[4,16,1024]{2,1,0:T(8,128)(2,1)S(1)}, bf16[4,16,1024]{2,1,0:T(8,128)(2,1)S(1)}, u32[]{:S(2)}, u32[]{:S(2)}) collective-permute-start(bf16[4,16,1024]{2,1,0:T(8,128)(2,1)S(1)} %shard_map.91.s0), channel_id=1, source_target_pairs={{0,2},{1,3},{2,0},{3,1},{4,6},{5,7},{6,4},{7,5},{8,10},{9,11},{10,... | collective-permute-start | bytes 393224 | tf_op jit(solution)/shard_map/ppermute | solution.py:346
  124.1 4.4 %collective-permute-done.29.s2 = bf16[4,16,1024]{2,1,0:T(8,128)(2,1)S(1)} collective-permute-done((bf16[4,16,1024]{2,1,0:T(8,128)(2,1)S(1)}, bf16[4,16,1024]{2,1,0:T(8,128)(2,1)S(1)}, u32[]{:S(2)}, u32[]{:S(2)}) %collective-permute-start.29) | collective-permute-done | bytes 131104 | tf_op jit(solution)/shard_map/ppermute | solution.py:346
  (65 shorter events, 36.4 us)
Async XLA Ops:
  3.8 10.1 %collective-permute-start = (f32[8,128]{1,0:T(8,128)S(1)}, f32[8,128]{1,0:T(8,128)S(1)}, u32[]{:S(2)}, u32[]{:S(2)}) collective-permute-start(f32[8,128]{1,0:T(8,128)S(1)} %get-tuple-element.53), channel_id=1, source_target_pairs={{0,4},{4,0},{8,12},{12,8},{16,20},{20,16},{24,28},{28,24},{32,36},... | collective-permute-start | bytes 12296 | tf_op jit(solution)/shard_map/ppermute | solution.py:350
  7.1 6.8 %collective-permute-start.1 = (f32[8,128]{1,0:T(8,128)S(1)}, f32[8,128]{1,0:T(8,128)S(1)}, u32[]{:S(2)}, u32[]{:S(2)}) collective-permute-start(f32[8,128]{1,0:T(8,128)S(1)} %get-tuple-element.54), channel_id=1, source_target_pairs={{4,8},{8,4},{12,16},{16,12},{20,24},{24,20},{28,32},{32,28},{36,40... | collective-permute-start | bytes 12296 | tf_op jit(solution)/shard_map/ppermute | solution.py:355
  13.9 4.9 %collective-permute-start.2 = (bf16[2,16,1152]{2,1,0:T(8,128)(2,1)S(1)}, bf16[2,16,1152]{2,1,0:T(8,128)(2,1)S(1)}, u32[]{:S(2)}, u32[]{:S(2)}) collective-permute-start(bf16[2,16,1152]{2,1,0:T(8,128)(2,1)S(1)} %get-tuple-element.61), channel_id=1, source_target_pairs={{0,2},{1,3},{2,0},{3,1},{4,6},{5,7},{6,4},{7,5},{8,10},{9,11},{10,... | collective-permute-start | bytes 221192 | tf_op jit(solution)/shard_map/ppermute | solution.py:346
  16.3 4.4 %collective-permute-start.3 = (bf16[2,16,1152]{2,1,0:T(8,128)(2,1)S(1)}, bf16[2,16,1152]{2,1,0:T(8,128)(2,1)S(1)}, u32[]{:S(2)}, u32[]{:S(2)}) collective-permute-start(bf16[2,16,1152]{2,1,0:T(8,128)(2,1)S(1)} %get-tuple-element.62), channel_id=1, source_target_pairs={{0,3},{1,2},{2,1},{3,0},{4,7},{5,6},{6,5},{7,4},{8,11},{9,10},{10,... | collective-permute-start | bytes 221192 | tf_op jit(solution)/shard_map/ppermute | solution.py:346
  23.0 8.5 %collective-permute-start.6 = (bf16[8,16,1024]{2,1,0:T(8,128)(2,1)S(1)}, bf16[8,16,1024]{2,1,0:T(8,128)(2,1)S(1)}, u32[]{:S(2)}, u32[]{:S(2)}) collective-permute-start(bf16[8,16,1024]{2,1,0:T(8,128)(2,1)S(1)} %shard_map.80), channel_id=1, source_target_pairs={{4,8},{8,4},{12,16},{16,12},{20,24},{24,20},{28,32},{32,28},{36,40... | collective-permute-start | bytes 786440 | tf_op jit(solution)/shard_map/ppermute | solution.py:355
  33.7 5.1 %collective-permute-start.8 = (bf16[2,16,1024]{2,1,0:T(8,128)(2,1)S(1)}, bf16[2,16,1024]{2,1,0:T(8,128)(2,1)S(1)}, u32[]{:S(2)}, u32[]{:S(2)}) collective-permute-start(bf16[2,16,1024]{2,1,0:T(8,128)(2,1)S(1)} %get-tuple-element.69), channel_id=1, source_target_pairs={{0,2},{1,3},{2,0},{3,1},{4,6},{5,7},{6,4},{7,5},{8,10},{9,11},{10,... | collective-permute-start | bytes 196616 | tf_op jit(solution)/shard_map/ppermute | solution.py:346
  35.0 5.5 %collective-permute-start.9 = (bf16[2,16,1024]{2,1,0:T(8,128)(2,1)S(1)}, bf16[2,16,1024]{2,1,0:T(8,128)(2,1)S(1)}, u32[]{:S(2)}, u32[]{:S(2)}) collective-permute-start(bf16[2,16,1024]{2,1,0:T(8,128)(2,1)S(1)} %get-tuple-element.70), channel_id=1, source_target_pairs={{0,3},{1,2},{2,1},{3,0},{4,7},{5,6},{6,5},{7,4},{8,11},{9,10},{10,... | collective-permute-start | bytes 196616 | tf_op jit(solution)/shard_map/ppermute | solution.py:346
  44.6 4.7 %collective-permute-start.11 = (bf16[2,16,1024]{2,1,0:T(8,128)(2,1)S(1)}, bf16[2,16,1024]{2,1,0:T(8,128)(2,1)S(1)}, u32[]{:S(2)}, u32[]{:S(2)}) collective-permute-start(bf16[2,16,1024]{2,1,0:T(8,128)(2,1)S(1)} %get-tuple-element.74), channel_id=1, source_target_pairs={{0,2},{1,3},{2,0},{3,1},{4,6},{5,7},{6,4},{7,5},{8,10},{9,11},{10,... | collective-permute-start | bytes 196616 | tf_op jit(solution)/shard_map/ppermute | solution.py:346
  46.1 5.0 %collective-permute-start.12 = (bf16[2,16,1024]{2,1,0:T(8,128)(2,1)S(1)}, bf16[2,16,1024]{2,1,0:T(8,128)(2,1)S(1)}, u32[]{:S(2)}, u32[]{:S(2)}) collective-permute-start(bf16[2,16,1024]{2,1,0:T(8,128)(2,1)S(1)} %get-tuple-element.75), channel_id=1, source_target_pairs={{0,3},{1,2},{2,1},{3,0},{4,7},{5,6},{6,5},{7,4},{8,11},{9,10},{10,... | collective-permute-start | bytes 196616 | tf_op jit(solution)/shard_map/ppermute | solution.py:346
  54.8 7.9 %collective-permute-start.15 = (bf16[8,16,1024]{2,1,0:T(8,128)(2,1)S(1)}, bf16[8,16,1024]{2,1,0:T(8,128)(2,1)S(1)}, u32[]{:S(2)}, u32[]{:S(2)}) collective-permute-start(bf16[8,16,1024]{2,1,0:T(8,128)(2,1)S(1)} %shard_map.84), channel_id=1, source_target_pairs={{4,8},{8,4},{12,16},{16,12},{20,24},{24,20},{28,32},{32,28},{36,40... | collective-permute-start | bytes 786440 | tf_op jit(solution)/shard_map/ppermute | solution.py:355
  64.9 5.1 %collective-permute-start.17 = (bf16[2,16,1024]{2,1,0:T(8,128)(2,1)S(1)}, bf16[2,16,1024]{2,1,0:T(8,128)(2,1)S(1)}, u32[]{:S(2)}, u32[]{:S(2)}) collective-permute-start(bf16[2,16,1024]{2,1,0:T(8,128)(2,1)S(1)} %get-tuple-element.80), channel_id=1, source_target_pairs={{0,2},{1,3},{2,0},{3,1},{4,6},{5,7},{6,4},{7,5},{8,10},{9,11},{10,... | collective-permute-start | bytes 196616 | tf_op jit(solution)/shard_map/ppermute | solution.py:346
  66.2 5.2 %collective-permute-start.18 = (bf16[2,16,1024]{2,1,0:T(8,128)(2,1)S(1)}, bf16[2,16,1024]{2,1,0:T(8,128)(2,1)S(1)}, u32[]{:S(2)}, u32[]{:S(2)}) collective-permute-start(bf16[2,16,1024]{2,1,0:T(8,128)(2,1)S(1)} %get-tuple-element.81), channel_id=1, source_target_pairs={{0,3},{1,2},{2,1},{3,0},{4,7},{5,6},{6,5},{7,4},{8,11},{9,10},{10,... | collective-permute-start | bytes 196616 | tf_op jit(solution)/shard_map/ppermute | solution.py:346
  76.2 24.4 %collective-permute-start.23 = (f32[2,16,1024]{2,1,0:T(8,128)S(1)}, f32[2,16,1024]{2,1,0:T(8,128)S(1)}, u32[]{:S(2)}, u32[]{:S(2)}) collective-permute-start(f32[2,16,1024]{2,1,0:T(8,128)S(1)} %get-tuple-element.91), channel_id=1, source_target_pairs={{0,2},{1,3},{2,0},{3,1},{4,6},{5,7},{6,4},{7,5},{8,10},{9,11},{10,... | collective-permute-start | bytes 393224 | tf_op jit(solution)/shard_map/ppermute | solution.py:346
  77.9 22.7 %collective-permute-start.24 = (f32[2,16,1024]{2,1,0:T(8,128)S(1)}, f32[2,16,1024]{2,1,0:T(8,128)S(1)}, u32[]{:S(2)}, u32[]{:S(2)}) collective-permute-start(f32[2,16,1024]{2,1,0:T(8,128)S(1)} %get-tuple-element.92), channel_id=1, source_target_pairs={{0,3},{1,2},{2,1},{3,0},{4,7},{5,6},{6,5},{7,4},{8,11},{9,10},{10,... | collective-permute-start | bytes 393224 | tf_op jit(solution)/shard_map/ppermute | solution.py:346
  79.3 21.3 %collective-permute-start.25 = (f32[2,16,1024]{2,1,0:T(8,128)S(1)}, f32[2,16,1024]{2,1,0:T(8,128)S(1)}, u32[]{:S(2)}, u32[]{:S(2)}) collective-permute-start(f32[2,16,1024]{2,1,0:T(8,128)S(1)} %get-tuple-element.93), channel_id=1, source_target_pairs={{0,1},{1,0},{2,3},{3,2},{4,5},{5,4},{6,7},{7,6},{8,9},{9,8},{10,11... | collective-permute-start | bytes 393224 | tf_op jit(solution)/shard_map/ppermute | solution.py:346
  79.3 33.9 %all-to-all-start = ((f32[256,1,128]{2,1,0:T(1,128)}), f32[256,1,128]{2,1,0:T(1,128)S(1)}, u32[]{:S(2)}, u32[]{:S(2)}) async-start(f32[256,1,128]{2,1,0:T(1,128)} %get-tuple-element.87), calls=%async_computation | async-start | bytes 262144 | tf_op jit(solution)/shard_map/all_to_all | solution.py:421
  101.6 15.3 %collective-permute-start.26 = (f32[4,16,1024]{2,1,0:T(8,128)}, f32[4,16,1024]{2,1,0:T(8,128)S(1)}, u32[]{:S(2)}, u32[]{:S(2)}) collective-permute-start(f32[4,16,1024]{2,1,0:T(8,128)} %get-tuple-element.95), channel_id=1, source_target_pairs={{0,4},{4,0},{8,12},{12,8},{16,20},{20,16},{24,28},{28,24},{32,36},... | collective-permute-start | bytes 786440 | tf_op jit(solution)/shard_map/ppermute | solution.py:350
  103.8 13.1 %collective-permute-start.27 = (f32[4,16,1024]{2,1,0:T(8,128)S(1)}, f32[4,16,1024]{2,1,0:T(8,128)S(1)}, u32[]{:S(2)}, u32[]{:S(2)}) collective-permute-start(f32[4,16,1024]{2,1,0:T(8,128)S(1)} %get-tuple-element.96), channel_id=1, source_target_pairs={{4,8},{8,4},{12,16},{16,12},{20,24},{24,20},{28,32},{32,28},{36,40... | collective-permute-start | bytes 786440 | tf_op jit(solution)/shard_map/ppermute | solution.py:355
  113.5 5.2 %collective-permute-start.22 = (bf16[4,16,1024]{2,1,0:T(8,128)(2,1)S(1)}, bf16[4,16,1024]{2,1,0:T(8,128)(2,1)S(1)}, u32[]{:S(2)}, u32[]{:S(2)}) collective-permute-start(bf16[4,16,1024]{2,1,0:T(8,128)(2,1)S(1)} %shard_map.87.s0), channel_id=1, source_target_pairs={{0,1},{1,0},{2,3},{3,2},{4,5},{5,4},{6,7},{7,6},{8,9},{9,8},{10,11... | collective-permute-start | bytes 393224 | tf_op jit(solution)/shard_map/ppermute | solution.py:346
  114.0 7.8 %collective-permute-start.21 = (bf16[4,16,1024]{2,1,0:T(8,128)(2,1)S(1)}, bf16[4,16,1024]{2,1,0:T(8,128)(2,1)S(1)}, u32[]{:S(2)}, u32[]{:S(2)}) collective-permute-start(bf16[4,16,1024]{2,1,0:T(8,128)(2,1)S(1)} %shard_map.87.s0), channel_id=1, source_target_pairs={{0,3},{1,2},{2,1},{3,0},{4,7},{5,6},{6,5},{7,4},{8,11},{9,10},{10,... | collective-permute-start | bytes 393224 | tf_op jit(solution)/shard_map/ppermute | solution.py:346
  115.1 6.7 %collective-permute-start.20 = (bf16[4,16,1024]{2,1,0:T(8,128)(2,1)S(1)}, bf16[4,16,1024]{2,1,0:T(8,128)(2,1)S(1)}, u32[]{:S(2)}, u32[]{:S(2)}) collective-permute-start(bf16[4,16,1024]{2,1,0:T(8,128)(2,1)S(1)} %shard_map.87.s0), channel_id=1, source_target_pairs={{0,2},{1,3},{2,0},{3,1},{4,6},{5,7},{6,4},{7,5},{8,10},{9,11},{10,... | collective-permute-start | bytes 393224 | tf_op jit(solution)/shard_map/ppermute | solution.py:346
  117.2 6.9 %collective-permute-start.30 = (bf16[4,16,1024]{2,1,0:T(8,128)(2,1)S(1)}, bf16[4,16,1024]{2,1,0:T(8,128)(2,1)S(1)}, u32[]{:S(2)}, u32[]{:S(2)}) collective-permute-start(bf16[4,16,1024]{2,1,0:T(8,128)(2,1)S(1)} %shard_map.91.s0), channel_id=1, source_target_pairs={{0,1},{1,0},{2,3},{3,2},{4,5},{5,4},{6,7},{7,6},{8,9},{9,8},{10,11... | collective-permute-start | bytes 393224 | tf_op jit(solution)/shard_map/ppermute | solution.py:346
  117.6 10.8 %collective-permute-start.29 = (bf16[4,16,1024]{2,1,0:T(8,128)(2,1)S(1)}, bf16[4,16,1024]{2,1,0:T(8,128)(2,1)S(1)}, u32[]{:S(2)}, u32[]{:S(2)}) collective-permute-start(bf16[4,16,1024]{2,1,0:T(8,128)(2,1)S(1)} %shard_map.91.s0), channel_id=1, source_target_pairs={{0,3},{1,2},{2,1},{3,0},{4,7},{5,6},{6,5},{7,4},{8,11},{9,10},{10,... | collective-permute-start | bytes 393224 | tf_op jit(solution)/shard_map/ppermute | solution.py:346
  118.7 9.7 %collective-permute-start.28 = (bf16[4,16,1024]{2,1,0:T(8,128)(2,1)S(1)}, bf16[4,16,1024]{2,1,0:T(8,128)(2,1)S(1)}, u32[]{:S(2)}, u32[]{:S(2)}) collective-permute-start(bf16[4,16,1024]{2,1,0:T(8,128)(2,1)S(1)} %shard_map.91.s0), channel_id=1, source_target_pairs={{0,2},{1,3},{2,0},{3,1},{4,6},{5,7},{6,4},{7,5},{8,10},{9,11},{10,... | collective-permute-start | bytes 393224 | tf_op jit(solution)/shard_map/ppermute | solution.py:346
  (12 other events, 90.4 us)

commit v7 on v6

--- a/solution.py
+++ b/solution.py
@@ -293,7 +293,7 @@
         totals = spread_slices(coefs, (c0, c1, c2, c3), cut)
         for z in range(ZD):
             own[z, :, cut] = totals[4 + z]
-            inner[z, :, cut] = jnp.where(even, totals[8 + z], totals[z])
+            inner[z, :, cut] = jnp.where(even, totals[8 + z], totals[z]).astype(BF16)
             outer[z, :, cut] = jnp.where(even, totals[z], totals[8 + z])
 
 
@@ -325,7 +325,7 @@
 def gradient_kernel(sums, t1, inner, outer, g0, z0, out):
     one, two = steps(sums)
     for z in range(ZD):
-        last = t1[z] + inner[z] + outer[z]
+        last = t1[z] + inner[z].astype(F32) + outer[z]
         out[z] = (g0[z] - one * z0[z] + two * last).astype(BF16)
 
 
@@ -419,7 +419,7 @@
     )(me, cols, *exchange(shares), q0, gamma, curve, inner, w)
     shares = exchange(shares)
     sums = lax.all_to_all(sums, ("slab", "ang"), 0, 0, tiled=True)
-    own, inner, outer = call(last_kernel, [part] * 3, [VMEM] * 6, flops=10_000_000)(flag, coefs, *shares)
+    own, inner, outer = call(last_kernel, [part, part_b, part], [VMEM] * 6, flops=10_000_000)(flag, coefs, *shares)
     outer = across(outer)
     inner = on_chip(inner)
     (volume,) = call(volume_kernel, [part_b], [VMEM] * 3)(sums, g0, z0)

time: 130 us -> 130 us (level)
    ppermute x6, starting transfers between devices: 7.5 us -> 5.45 us  [on_chip(): lax.ppermute(value, 'slab', [(i, i ^ 1) for i in range(lax.axis_size('sla...]
    ppermute x4, starting transfers between devices: 12.2 us -> 13.8 us  [across(): lax.ppermute(value, 'slab', [pair for i in range(1, count - 1, 2) for pai...]
  transfers between devices with their start and end apart: 32 -> 32, of which waited for: 17 -> 17; matrix products, arithmetic and copies ran while one was open for 0% -> 0% of each run, Pallas kernels for 7% -> 6%
where the time goes in v7:
time: 130 us; the launch traced here: 129 us
  starting transfers between devices  62.2 us (48%)
  waiting for transfers between devices  42.9 us (33%)
  Pallas kernels  21.5 us (17%)
  local copies, waits for them, and re-layouts  2.05 us (2%)
    ppermute x21, starting transfers between devices, along_ang(): return lax.ppermute(value, 'ang', [(i, i ^ other) for i in range(ANG)])  21.7 us
    all_to_all x1, starting transfers between devices, per_device(): sums = lax.all_to_all(sums, ('slab', 'ang'), 0, 0, tiled=True)  21.2 us
    ppermute x21, waiting for transfers between devices, along_ang(): return lax.ppermute(value, 'ang', [(i, i ^ other) for i in range(ANG)])  20.5 us
    ppermute x4, starting transfers between devices, across(): lax.ppermute(value, 'slab', [pair for i in range(1, count - 1, 2) for pai...  13.8 us
    all_to_all x1, waiting for transfers between devices, per_device(): sums = lax.all_to_all(sums, ('slab', 'ang'), 0, 0, tiled=True)  8.53 us
    ppermute x4, waiting for transfers between devices, across(): lax.ppermute(value, 'slab', [pair for i in range(1, count - 1, 2) for pai...  8.09 us
    ppermute x6, waiting for transfers between devices, on_chip(): lax.ppermute(value, 'slab', [(i, i ^ 1) for i in range(lax.axis_size('sla...  5.75 us
    ppermute x6, starting transfers between devices, on_chip(): lax.ppermute(value, 'slab', [(i, i ^ 1) for i in range(lax.axis_size('sla...  5.45 us
  transfers between devices with their start and end apart: 32, of which 17 were waited for; matrix products, arithmetic and copies ran while one was open for 0% of the time, Pallas kernels for 6%

profile of v7, /device:TPU:1, one launch (start us, length us, event | category | flops | bytes accessed | tf_op | source)
XLA Modules:
  0.0 129.5 jit_solution(8355122537945199028)
XLA Ops:
  3.8 3.3 %collective-permute-start = (f32[8,128]{1,0:T(8,128)S(1)}, f32[8,128]{1,0:T(8,128)S(1)}, u32[]{:S(2)}, u32[]{:S(2)}) collective-permute-start(f32[8,128]{1,0:T(8,128)S(1)} %get-tuple-element.53), channel_id=1, source_target_pairs={{0,4},{4,0},{8,12},{12,8},{16,20},{20,16},{24,28},{28,24},{32,36},... | collective-permute-start | bytes 12296 | tf_op jit(solution)/shard_map/ppermute | solution.py:350
  7.1 1.9 %collective-permute-start.1 = (f32[8,128]{1,0:T(8,128)S(1)}, f32[8,128]{1,0:T(8,128)S(1)}, u32[]{:S(2)}, u32[]{:S(2)}) collective-permute-start(f32[8,128]{1,0:T(8,128)S(1)} %get-tuple-element.54), channel_id=1, source_target_pairs={{4,8},{8,4},{12,16},{16,12},{20,24},{24,20},{28,32},{32,28},{36,40... | collective-permute-start | bytes 12296 | tf_op jit(solution)/shard_map/ppermute | solution.py:355
  9.0 4.8 %shard_map.77 = (bf16[2,16,1024]{2,1,0:T(8,128)(2,1)S(1)}, bf16[2,16,1024]{2,1,0:T(8,128)(2,1)S(1)}, bf16[2,16,1024]{2,1,0:T(8,128)(2,1)S(1)}, bf16[2,16,1024]{2...) custom-call(s32[1]{0:T(128)} %bitcast.me_ref, s32[3,2,32]{2,1,0:T(2,128)S(1)} %get-tuple-element.50.cols, ...), custom_call_target="tpu_custom_call" | custom-call | flops 201326592 | bytes 7000000 | tf_op jit(solution)/shard_map/pallas_call | solution.py:392
  13.9 2.4 %collective-permute-start.2 = (bf16[2,16,1152]{2,1,0:T(8,128)(2,1)S(1)}, bf16[2,16,1152]{2,1,0:T(8,128)(2,1)S(1)}, u32[]{:S(2)}, u32[]{:S(2)}) collective-permute-start(bf16[2,16,1152]{2,1,0:T(8,128)(2,1)S(1)} %get-tuple-element.61), channel_id=1, source_target_pairs={{0,2},{1,3},{2,0},{3,1},{4,6},{5,7},{6,4},{7,5},{8,10},{9,11},{10,... | collective-permute-start | bytes 221192 | tf_op jit(solution)/shard_map/ppermute | solution.py:346
  17.1 1.7 %collective-permute-done.2.c1 = bf16[2,16,1152]{2,1,0:T(8,128)(2,1)S(1)} collective-permute-done((bf16[2,16,1152]{2,1,0:T(8,128)(2,1)S(1)}, bf16[2,16,1152]{2,1,0:T(8,128)(2,1)S(1)}, u32[]{:S(2)}, u32[]{:S(2)}) %collective-permute-start.2) | collective-permute-done | bytes 73760 | tf_op jit(solution)/shard_map/ppermute | solution.py:346
  18.8 1.9 %collective-permute-done.3.c2 = bf16[2,16,1152]{2,1,0:T(8,128)(2,1)S(1)} collective-permute-done((bf16[2,16,1152]{2,1,0:T(8,128)(2,1)S(1)}, bf16[2,16,1152]{2,1,0:T(8,128)(2,1)S(1)}, u32[]{:S(2)}, u32[]{:S(2)}) %collective-permute-start.3) | collective-permute-done | bytes 73760 | tf_op jit(solution)/shard_map/ppermute | solution.py:346
  23.0 4.5 %collective-permute-start.6 = (bf16[8,16,1024]{2,1,0:T(8,128)(2,1)S(1)}, bf16[8,16,1024]{2,1,0:T(8,128)(2,1)S(1)}, u32[]{:S(2)}, u32[]{:S(2)}) collective-permute-start(bf16[8,16,1024]{2,1,0:T(8,128)(2,1)S(1)} %shard_map.80), channel_id=1, source_target_pairs={{4,8},{8,4},{12,16},{16,12},{20,24},{24,20},{28,32},{32,28},{36,40... | collective-permute-start | bytes 786440 | tf_op jit(solution)/shard_map/ppermute | solution.py:355
  27.5 4.0 %collective-permute-done.6.outer = bf16[8,16,1024]{2,1,0:T(8,128)(2,1)S(1)} collective-permute-done((bf16[8,16,1024]{2,1,0:T(8,128)(2,1)S(1)}, bf16[8,16,1024]{2,1,0:T(8,128)(2,1)S(1)}, u32[]{:S(2)}, u32[]{:S(2)}) %collective-permute-start.6) | collective-permute-done | bytes 262176 | tf_op jit(solution)/shard_map/ppermute | solution.py:355
  36.6 2.3 %collective-permute-done.8.h1 = bf16[2,16,1024]{2,1,0:T(8,128)(2,1)S(1)} collective-permute-done((bf16[2,16,1024]{2,1,0:T(8,128)(2,1)S(1)}, bf16[2,16,1024]{2,1,0:T(8,128)(2,1)S(1)}, u32[]{:S(2)}, u32[]{:S(2)}) %collective-permute-start.8) | collective-permute-done | bytes 65568 | tf_op jit(solution)/shard_map/ppermute | solution.py:346
  38.9 1.6 %collective-permute-done.9.h2 = bf16[2,16,1024]{2,1,0:T(8,128)(2,1)S(1)} collective-permute-done((bf16[2,16,1024]{2,1,0:T(8,128)(2,1)S(1)}, bf16[2,16,1024]{2,1,0:T(8,128)(2,1)S(1)}, u32[]{:S(2)}, u32[]{:S(2)}) %collective-permute-start.9) | collective-permute-done | bytes 65568 | tf_op jit(solution)/shard_map/ppermute | solution.py:346
  40.5 4.1 %shard_map.82 = (bf16[2,16,1024]{2,1,0:T(8,128)(2,1)S(1)}, bf16[2,16,1024]{2,1,0:T(8,128)(2,1)S(1)}, bf16[2,16,1024]{2,1,0:T(8,128)(2,1)S(1)}, bf16[2,16,1024]{2...) custom-call(s32[1]{0:T(128)} %bitcast.me_ref, s32[3,2,32]{2,1,0:T(2,128)S(1)} %get-tuple-element.50.cols, ...), custom_call_target="tpu_custom_call" | custom-call | flops 301989888 | bytes 7000000 | tf_op jit(solution)/shard_map/pallas_call | solution.py:405
  49.3 1.9 %collective-permute-done.12.c2 = bf16[2,16,1024]{2,1,0:T(8,128)(2,1)S(1)} collective-permute-done((bf16[2,16,1024]{2,1,0:T(8,128)(2,1)S(1)}, bf16[2,16,1024]{2,1,0:T(8,128)(2,1)S(1)}, u32[]{:S(2)}, u32[]{:S(2)}) %collective-permute-start.12) | collective-permute-done | bytes 65568 | tf_op jit(solution)/shard_map/ppermute | solution.py:346
  51.6 1.9 %collective-permute-start.14 = (bf16[8,16,1024]{2,1,0:T(8,128)(2,1)S(1)}, bf16[8,16,1024]{2,1,0:T(8,128)(2,1)S(1)}, u32[]{:S(2)}, u32[]{:S(2)}) collective-permute-start(bf16[8,16,1024]{2,1,0:T(8,128)(2,1)S(1)} %get-tuple-element.78), channel_id=1, source_target_pairs={{0,4},{4,0},{8,12},{12,8},{16,20},{20,16},{24,28},{28,24},{32,36},... | collective-permute-start | bytes 786440 | tf_op jit(solution)/shard_map/ppermute | solution.py:350
  54.8 3.8 %collective-permute-start.15 = (bf16[8,16,1024]{2,1,0:T(8,128)(2,1)S(1)}, bf16[8,16,1024]{2,1,0:T(8,128)(2,1)S(1)}, u32[]{:S(2)}, u32[]{:S(2)}) collective-permute-start(bf16[8,16,1024]{2,1,0:T(8,128)(2,1)S(1)} %shard_map.84), channel_id=1, source_target_pairs={{4,8},{8,4},{12,16},{16,12},{20,24},{24,20},{28,32},{32,28},{36,40... | collective-permute-start | bytes 786440 | tf_op jit(solution)/shard_map/ppermute | solution.py:355
  58.7 4.0 %collective-permute-done.15.outer = bf16[8,16,1024]{2,1,0:T(8,128)(2,1)S(1)} collective-permute-done((bf16[8,16,1024]{2,1,0:T(8,128)(2,1)S(1)}, bf16[8,16,1024]{2,1,0:T(8,128)(2,1)S(1)}, u32[]{:S(2)}, u32[]{:S(2)}) %collective-permute-start.15) | collective-permute-done | bytes 262176 | tf_op jit(solution)/shard_map/ppermute | solution.py:355
  67.7 2.3 %collective-permute-done.17.h1 = bf16[2,16,1024]{2,1,0:T(8,128)(2,1)S(1)} collective-permute-done((bf16[2,16,1024]{2,1,0:T(8,128)(2,1)S(1)}, bf16[2,16,1024]{2,1,0:T(8,128)(2,1)S(1)}, u32[]{:S(2)}, u32[]{:S(2)}) %collective-permute-start.17) | collective-permute-done | bytes 65568 | tf_op jit(solution)/shard_map/ppermute | solution.py:346
  71.5 4.7 %shard_map.86 = (f32[2,16,1024]{2,1,0:T(8,128)S(1)}, f32[2,16,1024]{2,1,0:T(8,128)S(1)}, f32[2,16,1024]{2,1,0:T(8,128)S(1)}, f32[2,16,1024]{2,1,0:T(8,128)S(1)},...) custom-call(s32[1]{0:T(128)} %bitcast.me_ref, s32[3,2,32]{2,1,0:T(2,128)S(1)} %get-tuple-element.50.cols, ...), custom_call_target="tpu_custom_call" | custom-call | flops 402653184 | bytes 9000000 | tf_op jit(solution)/shard_map/pallas_call | solution.py:415
  76.2 1.7 %collective-permute-start.23 = (f32[2,16,1024]{2,1,0:T(8,128)S(1)}, f32[2,16,1024]{2,1,0:T(8,128)S(1)}, u32[]{:S(2)}, u32[]{:S(2)}) collective-permute-start(f32[2,16,1024]{2,1,0:T(8,128)S(1)} %get-tuple-element.91), channel_id=1, source_target_pairs={{0,2},{1,3},{2,0},{3,1},{4,6},{5,7},{6,4},{7,5},{8,10},{9,11},{10,... | collective-permute-start | bytes 393224 | tf_op jit(solution)/shard_map/ppermute | solution.py:346
  79.3 21.2 %all-to-all-start = ((f32[256,1,128]{2,1,0:T(1,128)}), f32[256,1,128]{2,1,0:T(1,128)S(1)}, u32[]{:S(2)}, u32[]{:S(2)}) async-start(f32[256,1,128]{2,1,0:T(1,128)} %get-tuple-element.87), calls=%async_computation | async-start | bytes 262144 | tf_op jit(solution)/shard_map/all_to_all | solution.py:421
  101.0 3.5 %collective-permute-start.27 = (f32[4,16,1024]{2,1,0:T(8,128)S(1)}, f32[4,16,1024]{2,1,0:T(8,128)S(1)}, u32[]{:S(2)}, u32[]{:S(2)}) collective-permute-start(f32[4,16,1024]{2,1,0:T(8,128)S(1)} %get-tuple-element.96), channel_id=1, source_target_pairs={{4,8},{8,4},{12,16},{16,12},{20,24},{24,20},{28,32},{32,28},{36,40... | collective-permute-start | bytes 786440 | tf_op jit(solution)/shard_map/ppermute | solution.py:355
  104.7 8.5 %all-to-all-done.sums = f32[256,1,128]{2,1,0:T(1,128)S(1)} async-done(((f32[256,1,128]{2,1,0:T(1,128)}), f32[256,1,128]{2,1,0:T(1,128)S(1)}, u32[]{:S(2)}, u32[]{:S(2)}) %all-to-all-start) | async-done | bytes 131104 | tf_op jit(solution)/shard_map/all_to_all | solution.py:421
  115.1 1.8 %collective-permute-start.20 = (bf16[4,16,1024]{2,1,0:T(8,128)(2,1)S(1)}, bf16[4,16,1024]{2,1,0:T(8,128)(2,1)S(1)}, u32[]{:S(2)}, u32[]{:S(2)}) collective-permute-start(bf16[4,16,1024]{2,1,0:T(8,128)(2,1)S(1)} %shard_map.87.s0), channel_id=1, source_target_pairs={{0,2},{1,3},{2,0},{3,1},{4,6},{5,7},{6,4},{7,5},{8,10},{9,11},{10,... | collective-permute-start | bytes 393224 | tf_op jit(solution)/shard_map/ppermute | solution.py:346
  118.7 1.8 %collective-permute-start.28 = (bf16[4,16,1024]{2,1,0:T(8,128)(2,1)S(1)}, bf16[4,16,1024]{2,1,0:T(8,128)(2,1)S(1)}, u32[]{:S(2)}, u32[]{:S(2)}) collective-permute-start(bf16[4,16,1024]{2,1,0:T(8,128)(2,1)S(1)} %shard_map.91.s0), channel_id=1, source_target_pairs={{0,2},{1,3},{2,0},{3,1},{4,6},{5,7},{6,4},{7,5},{8,10},{9,11},{10,... | collective-permute-start | bytes 393224 | tf_op jit(solution)/shard_map/ppermute | solution.py:346
  124.1 4.4 %collective-permute-done.29.s2 = bf16[4,16,1024]{2,1,0:T(8,128)(2,1)S(1)} collective-permute-done((bf16[4,16,1024]{2,1,0:T(8,128)(2,1)S(1)}, bf16[4,16,1024]{2,1,0:T(8,128)(2,1)S(1)}, u32[]{:S(2)}, u32[]{:S(2)}) %collective-permute-start.29) | collective-permute-done | bytes 131104 | tf_op jit(solution)/shard_map/ppermute | solution.py:346
  (65 shorter events, 34.4 us)
Async XLA Ops:
  3.8 10.1 %collective-permute-start = (f32[8,128]{1,0:T(8,128)S(1)}, f32[8,128]{1,0:T(8,128)S(1)}, u32[]{:S(2)}, u32[]{:S(2)}) collective-permute-start(f32[8,128]{1,0:T(8,128)S(1)} %get-tuple-element.53), channel_id=1, source_target_pairs={{0,4},{4,0},{8,12},{12,8},{16,20},{20,16},{24,28},{28,24},{32,36},... | collective-permute-start | bytes 12296 | tf_op jit(solution)/shard_map/ppermute | solution.py:350
  7.1 6.8 %collective-permute-start.1 = (f32[8,128]{1,0:T(8,128)S(1)}, f32[8,128]{1,0:T(8,128)S(1)}, u32[]{:S(2)}, u32[]{:S(2)}) collective-permute-start(f32[8,128]{1,0:T(8,128)S(1)} %get-tuple-element.54), channel_id=1, source_target_pairs={{4,8},{8,4},{12,16},{16,12},{20,24},{24,20},{28,32},{32,28},{36,40... | collective-permute-start | bytes 12296 | tf_op jit(solution)/shard_map/ppermute | solution.py:355
  13.9 4.9 %collective-permute-start.2 = (bf16[2,16,1152]{2,1,0:T(8,128)(2,1)S(1)}, bf16[2,16,1152]{2,1,0:T(8,128)(2,1)S(1)}, u32[]{:S(2)}, u32[]{:S(2)}) collective-permute-start(bf16[2,16,1152]{2,1,0:T(8,128)(2,1)S(1)} %get-tuple-element.61), channel_id=1, source_target_pairs={{0,2},{1,3},{2,0},{3,1},{4,6},{5,7},{6,4},{7,5},{8,10},{9,11},{10,... | collective-permute-start | bytes 221192 | tf_op jit(solution)/shard_map/ppermute | solution.py:346
  16.3 4.4 %collective-permute-start.3 = (bf16[2,16,1152]{2,1,0:T(8,128)(2,1)S(1)}, bf16[2,16,1152]{2,1,0:T(8,128)(2,1)S(1)}, u32[]{:S(2)}, u32[]{:S(2)}) collective-permute-start(bf16[2,16,1152]{2,1,0:T(8,128)(2,1)S(1)} %get-tuple-element.62), channel_id=1, source_target_pairs={{0,3},{1,2},{2,1},{3,0},{4,7},{5,6},{6,5},{7,4},{8,11},{9,10},{10,... | collective-permute-start | bytes 221192 | tf_op jit(solution)/shard_map/ppermute | solution.py:346
  23.0 8.5 %collective-permute-start.6 = (bf16[8,16,1024]{2,1,0:T(8,128)(2,1)S(1)}, bf16[8,16,1024]{2,1,0:T(8,128)(2,1)S(1)}, u32[]{:S(2)}, u32[]{:S(2)}) collective-permute-start(bf16[8,16,1024]{2,1,0:T(8,128)(2,1)S(1)} %shard_map.80), channel_id=1, source_target_pairs={{4,8},{8,4},{12,16},{16,12},{20,24},{24,20},{28,32},{32,28},{36,40... | collective-permute-start | bytes 786440 | tf_op jit(solution)/shard_map/ppermute | solution.py:355
  33.7 5.1 %collective-permute-start.8 = (bf16[2,16,1024]{2,1,0:T(8,128)(2,1)S(1)}, bf16[2,16,1024]{2,1,0:T(8,128)(2,1)S(1)}, u32[]{:S(2)}, u32[]{:S(2)}) collective-permute-start(bf16[2,16,1024]{2,1,0:T(8,128)(2,1)S(1)} %get-tuple-element.69), channel_id=1, source_target_pairs={{0,2},{1,3},{2,0},{3,1},{4,6},{5,7},{6,4},{7,5},{8,10},{9,11},{10,... | collective-permute-start | bytes 196616 | tf_op jit(solution)/shard_map/ppermute | solution.py:346
  35.0 5.5 %collective-permute-start.9 = (bf16[2,16,1024]{2,1,0:T(8,128)(2,1)S(1)}, bf16[2,16,1024]{2,1,0:T(8,128)(2,1)S(1)}, u32[]{:S(2)}, u32[]{:S(2)}) collective-permute-start(bf16[2,16,1024]{2,1,0:T(8,128)(2,1)S(1)} %get-tuple-element.70), channel_id=1, source_target_pairs={{0,3},{1,2},{2,1},{3,0},{4,7},{5,6},{6,5},{7,4},{8,11},{9,10},{10,... | collective-permute-start | bytes 196616 | tf_op jit(solution)/shard_map/ppermute | solution.py:346
  44.6 4.7 %collective-permute-start.11 = (bf16[2,16,1024]{2,1,0:T(8,128)(2,1)S(1)}, bf16[2,16,1024]{2,1,0:T(8,128)(2,1)S(1)}, u32[]{:S(2)}, u32[]{:S(2)}) collective-permute-start(bf16[2,16,1024]{2,1,0:T(8,128)(2,1)S(1)} %get-tuple-element.74), channel_id=1, source_target_pairs={{0,2},{1,3},{2,0},{3,1},{4,6},{5,7},{6,4},{7,5},{8,10},{9,11},{10,... | collective-permute-start | bytes 196616 | tf_op jit(solution)/shard_map/ppermute | solution.py:346
  46.1 5.0 %collective-permute-start.12 = (bf16[2,16,1024]{2,1,0:T(8,128)(2,1)S(1)}, bf16[2,16,1024]{2,1,0:T(8,128)(2,1)S(1)}, u32[]{:S(2)}, u32[]{:S(2)}) collective-permute-start(bf16[2,16,1024]{2,1,0:T(8,128)(2,1)S(1)} %get-tuple-element.75), channel_id=1, source_target_pairs={{0,3},{1,2},{2,1},{3,0},{4,7},{5,6},{6,5},{7,4},{8,11},{9,10},{10,... | collective-permute-start | bytes 196616 | tf_op jit(solution)/shard_map/ppermute | solution.py:346
  54.8 7.9 %collective-permute-start.15 = (bf16[8,16,1024]{2,1,0:T(8,128)(2,1)S(1)}, bf16[8,16,1024]{2,1,0:T(8,128)(2,1)S(1)}, u32[]{:S(2)}, u32[]{:S(2)}) collective-permute-start(bf16[8,16,1024]{2,1,0:T(8,128)(2,1)S(1)} %shard_map.84), channel_id=1, source_target_pairs={{4,8},{8,4},{12,16},{16,12},{20,24},{24,20},{28,32},{32,28},{36,40... | collective-permute-start | bytes 786440 | tf_op jit(solution)/shard_map/ppermute | solution.py:355
  64.9 5.1 %collective-permute-start.17 = (bf16[2,16,1024]{2,1,0:T(8,128)(2,1)S(1)}, bf16[2,16,1024]{2,1,0:T(8,128)(2,1)S(1)}, u32[]{:S(2)}, u32[]{:S(2)}) collective-permute-start(bf16[2,16,1024]{2,1,0:T(8,128)(2,1)S(1)} %get-tuple-element.80), channel_id=1, source_target_pairs={{0,2},{1,3},{2,0},{3,1},{4,6},{5,7},{6,4},{7,5},{8,10},{9,11},{10,... | collective-permute-start | bytes 196616 | tf_op jit(solution)/shard_map/ppermute | solution.py:346
  66.2 5.3 %collective-permute-start.18 = (bf16[2,16,1024]{2,1,0:T(8,128)(2,1)S(1)}, bf16[2,16,1024]{2,1,0:T(8,128)(2,1)S(1)}, u32[]{:S(2)}, u32[]{:S(2)}) collective-permute-start(bf16[2,16,1024]{2,1,0:T(8,128)(2,1)S(1)} %get-tuple-element.81), channel_id=1, source_target_pairs={{0,3},{1,2},{2,1},{3,0},{4,7},{5,6},{6,5},{7,4},{8,11},{9,10},{10,... | collective-permute-start | bytes 196616 | tf_op jit(solution)/shard_map/ppermute | solution.py:346
  76.2 24.4 %collective-permute-start.23 = (f32[2,16,1024]{2,1,0:T(8,128)S(1)}, f32[2,16,1024]{2,1,0:T(8,128)S(1)}, u32[]{:S(2)}, u32[]{:S(2)}) collective-permute-start(f32[2,16,1024]{2,1,0:T(8,128)S(1)} %get-tuple-element.91), channel_id=1, source_target_pairs={{0,2},{1,3},{2,0},{3,1},{4,6},{5,7},{6,4},{7,5},{8,10},{9,11},{10,... | collective-permute-start | bytes 393224 | tf_op jit(solution)/shard_map/ppermute | solution.py:346
  77.8 22.7 %collective-permute-start.24 = (f32[2,16,1024]{2,1,0:T(8,128)S(1)}, f32[2,16,1024]{2,1,0:T(8,128)S(1)}, u32[]{:S(2)}, u32[]{:S(2)}) collective-permute-start(f32[2,16,1024]{2,1,0:T(8,128)S(1)} %get-tuple-element.92), channel_id=1, source_target_pairs={{0,3},{1,2},{2,1},{3,0},{4,7},{5,6},{6,5},{7,4},{8,11},{9,10},{10,... | collective-permute-start | bytes 393224 | tf_op jit(solution)/shard_map/ppermute | solution.py:346
  79.3 21.3 %collective-permute-start.25 = (f32[2,16,1024]{2,1,0:T(8,128)S(1)}, f32[2,16,1024]{2,1,0:T(8,128)S(1)}, u32[]{:S(2)}, u32[]{:S(2)}) collective-permute-start(f32[2,16,1024]{2,1,0:T(8,128)S(1)} %get-tuple-element.93), channel_id=1, source_target_pairs={{0,1},{1,0},{2,3},{3,2},{4,5},{5,4},{6,7},{7,6},{8,9},{9,8},{10,11... | collective-permute-start | bytes 393224 | tf_op jit(solution)/shard_map/ppermute | solution.py:346
  79.3 33.9 %all-to-all-start = ((f32[256,1,128]{2,1,0:T(1,128)}), f32[256,1,128]{2,1,0:T(1,128)S(1)}, u32[]{:S(2)}, u32[]{:S(2)}) async-start(f32[256,1,128]{2,1,0:T(1,128)} %get-tuple-element.87), calls=%async_computation | async-start | bytes 262144 | tf_op jit(solution)/shard_map/all_to_all | solution.py:421
  101.0 15.8 %collective-permute-start.27 = (f32[4,16,1024]{2,1,0:T(8,128)S(1)}, f32[4,16,1024]{2,1,0:T(8,128)S(1)}, u32[]{:S(2)}, u32[]{:S(2)}) collective-permute-start(f32[4,16,1024]{2,1,0:T(8,128)S(1)} %get-tuple-element.96), channel_id=1, source_target_pairs={{4,8},{8,4},{12,16},{16,12},{20,24},{24,20},{28,32},{32,28},{36,40... | collective-permute-start | bytes 786440 | tf_op jit(solution)/shard_map/ppermute | solution.py:355
  104.6 12.3 %collective-permute-start.26 = (bf16[4,16,1024]{2,1,0:T(8,128)(2,1)S(1)}, bf16[4,16,1024]{2,1,0:T(8,128)(2,1)S(1)}, u32[]{:S(2)}, u32[]{:S(2)}) collective-permute-start(bf16[4,16,1024]{2,1,0:T(8,128)(2,1)S(1)} %get-tuple-element.95), channel_id=1, source_target_pairs={{0,4},{4,0},{8,12},{12,8},{16,20},{20,16},{24,28},{28,24},{32,36},... | collective-permute-start | bytes 393224 | tf_op jit(solution)/shard_map/ppermute | solution.py:350
  113.5 5.2 %collective-permute-start.22 = (bf16[4,16,1024]{2,1,0:T(8,128)(2,1)S(1)}, bf16[4,16,1024]{2,1,0:T(8,128)(2,1)S(1)}, u32[]{:S(2)}, u32[]{:S(2)}) collective-permute-start(bf16[4,16,1024]{2,1,0:T(8,128)(2,1)S(1)} %shard_map.87.s0), channel_id=1, source_target_pairs={{0,1},{1,0},{2,3},{3,2},{4,5},{5,4},{6,7},{7,6},{8,9},{9,8},{10,11... | collective-permute-start | bytes 393224 | tf_op jit(solution)/shard_map/ppermute | solution.py:346
  114.0 7.8 %collective-permute-start.21 = (bf16[4,16,1024]{2,1,0:T(8,128)(2,1)S(1)}, bf16[4,16,1024]{2,1,0:T(8,128)(2,1)S(1)}, u32[]{:S(2)}, u32[]{:S(2)}) collective-permute-start(bf16[4,16,1024]{2,1,0:T(8,128)(2,1)S(1)} %shard_map.87.s0), channel_id=1, source_target_pairs={{0,3},{1,2},{2,1},{3,0},{4,7},{5,6},{6,5},{7,4},{8,11},{9,10},{10,... | collective-permute-start | bytes 393224 | tf_op jit(solution)/shard_map/ppermute | solution.py:346
  115.1 6.7 %collective-permute-start.20 = (bf16[4,16,1024]{2,1,0:T(8,128)(2,1)S(1)}, bf16[4,16,1024]{2,1,0:T(8,128)(2,1)S(1)}, u32[]{:S(2)}, u32[]{:S(2)}) collective-permute-start(bf16[4,16,1024]{2,1,0:T(8,128)(2,1)S(1)} %shard_map.87.s0), channel_id=1, source_target_pairs={{0,2},{1,3},{2,0},{3,1},{4,6},{5,7},{6,4},{7,5},{8,10},{9,11},{10,... | collective-permute-start | bytes 393224 | tf_op jit(solution)/shard_map/ppermute | solution.py:346
  117.2 6.9 %collective-permute-start.30 = (bf16[4,16,1024]{2,1,0:T(8,128)(2,1)S(1)}, bf16[4,16,1024]{2,1,0:T(8,128)(2,1)S(1)}, u32[]{:S(2)}, u32[]{:S(2)}) collective-permute-start(bf16[4,16,1024]{2,1,0:T(8,128)(2,1)S(1)} %shard_map.91.s0), channel_id=1, source_target_pairs={{0,1},{1,0},{2,3},{3,2},{4,5},{5,4},{6,7},{7,6},{8,9},{9,8},{10,11... | collective-permute-start | bytes 393224 | tf_op jit(solution)/shard_map/ppermute | solution.py:346
  117.6 10.8 %collective-permute-start.29 = (bf16[4,16,1024]{2,1,0:T(8,128)(2,1)S(1)}, bf16[4,16,1024]{2,1,0:T(8,128)(2,1)S(1)}, u32[]{:S(2)}, u32[]{:S(2)}) collective-permute-start(bf16[4,16,1024]{2,1,0:T(8,128)(2,1)S(1)} %shard_map.91.s0), channel_id=1, source_target_pairs={{0,3},{1,2},{2,1},{3,0},{4,7},{5,6},{6,5},{7,4},{8,11},{9,10},{10,... | collective-permute-start | bytes 393224 | tf_op jit(solution)/shard_map/ppermute | solution.py:346
  118.7 9.7 %collective-permute-start.28 = (bf16[4,16,1024]{2,1,0:T(8,128)(2,1)S(1)}, bf16[4,16,1024]{2,1,0:T(8,128)(2,1)S(1)}, u32[]{:S(2)}, u32[]{:S(2)}) collective-permute-start(bf16[4,16,1024]{2,1,0:T(8,128)(2,1)S(1)} %shard_map.91.s0), channel_id=1, source_target_pairs={{0,2},{1,3},{2,0},{3,1},{4,6},{5,7},{6,4},{7,5},{8,10},{9,11},{10,... | collective-permute-start | bytes 393224 | tf_op jit(solution)/shard_map/ppermute | solution.py:346
  (12 other events, 90.4 us)
